TPU v7x, 128 devices: a whole 4x4x4 slice. The times are simulated.
128 devices in a mesh: dom: 32 (over y, x, core), band: 4 (over z).
Axes of the slice: x: 4, y: 4, z: 4, core: 2. Of those that a mesh axis runs over, the one named last changes fastest.
Arguments:
- block: float32 [64, 442368], P('band', 'dom')
- stiffness: float32 [343, 343], replicated
- cell_scale: float32 [2048], P('dom'), may hold values from 0.3 to 3
- potential: float32 [343, 2048], P(None, 'dom'), may hold values from 0.1 to 2
- cell_dofs: int32 [343, 2048], P(None, 'dom'), may hold values from 0 to 17919, as said below
- cell_count: int32 [32], P('dom'), may hold values from 32 to 64, as said below
- hang_rows: int32 [27648], P('dom'), may hold values from 0 to 13823, as said below
- hang_masters: int32 [4, 27648], P(None, 'dom'), may hold values from 0 to 13823, as said below
- hang_weights: float32 [4, 27648], P(None, 'dom'), may hold values from 0.1 to 0.6
Outputs:
- basis: float32 [64, 442368], P('band', 'dom')
Inputs may be any that keep to these rules, and one draw needn't show every extreme that they name: `cell_dofs`: each cell's 343 rows are distinct and lie within a window of 686 rows of the extended vector of 17920 rows. `cell_count`: every shard has at least 32 live cells; some shard has exactly 64. `hang_rows`: within a shard the hanging rows are distinct and none of them is a master. `hang_masters`: masters are owned rows of the same shard.
All inputs are finite; a program needn't handle non-finite values.
Results may differ from a plain program's by a relative error of at most 0.00026.
Values sent between devices are 32-bit elements; how exact they have to be, the bound alone decides.
No kernel may reach another device: no remote copies, remote signals or barrier semaphores. Data moves between devices by JAX's collectives and lax.ppermute only.
A program may use at most 192 MiB of HBM per device.

v0:
```python
import jax
import jax.numpy as jnp
from jax import lax
from jax.sharding import PartitionSpec as P

RIM = 2048


def padded(x, sides, width):
    for axis, dim in sides:
        size, length = (lax.axis_size(axis), x.shape[dim])
        up = [(i, (i + 1) % size) for i in range(size - 1)]
        down = [(j, i) for i, j in up]
        last = lax.slice_in_dim(x, length - width, length, axis=dim)
        initial = lax.slice_in_dim(x, 0, width, axis=dim)
        before = lax.ppermute(last, axis, up)
        after = lax.ppermute(initial, axis, down)
        x = jnp.concatenate([before, x, after], axis=dim)
    return x


def body(
    block,
    stiffness,
    cell_scale,
    potential,
    cell_dofs,
    cell_count,
    hang_rows,
    hang_masters,
    hang_weights,
):
    states, local = block.shape
    cells = cell_dofs.shape[1]
    count = cell_count[0]

    def distribute(v):
        vals = jnp.sum(hang_weights[None] * v[:, hang_masters], axis=1)
        return v.at[:, hang_rows].set(vals)

    def condense(y):
        contrib = hang_weights[None] * y[:, hang_rows][:, None, :]
        y = y.at[:, hang_masters.reshape(-1)].add(contrib.reshape(states, -1))
        return y.at[:, hang_rows].set(jnp.zeros((states, hang_rows.shape[0]), jnp.float32))

    def products(extended, dofs, scales, pots):
        gathered = extended[:, dofs]
        prod = jnp.einsum("ij,sjc->sic", stiffness, gathered, precision=lax.Precision.HIGHEST)
        return scales[None, None, :] * prod + pots[None] * gathered

    def apply(v):
        u = distribute(v)
        extended = padded(u, (("dom", 1),), RIM)
        empty = jnp.zeros_like(extended)
        alive = (jnp.arange(cells) < count).astype(jnp.float32)
        out = products(extended, cell_dofs, cell_scale, potential) * alive[None, None, :]
        accum = empty.at[:, cell_dofs].add(out)
        edges = jnp.concatenate([accum[:, :RIM], accum[:, RIM + local :]], axis=1)
        beside_all = padded(edges, (("dom", 1),), RIM)
        owned = accum[:, RIM : RIM + local]
        owned = owned.at[:, :RIM].add(beside_all[:, :RIM])
        owned = owned.at[:, local - RIM :].add(beside_all[:, 3 * RIM :])
        return condense(owned)

    centre = 4.5
    half = 3.5
    first = (apply(block) - centre * block) / half
    second = 2.0 * (apply(first) - centre * first) / half - block
    third = 2.0 * (apply(second) - centre * second) / half - first
    filtered = distribute(third)
    scaling = jnp.sqrt(jnp.float32(local * lax.axis_size("dom")))
    quarter = lax.all_to_all(filtered, "band", split_axis=1, concat_axis=0, tiled=True)
    intersection = jnp.dot(quarter, quarter.T, precision=lax.Precision.HIGHEST)
    intersection = lax.psum(intersection, ("dom", "band"))
    factor = jnp.linalg.cholesky(intersection)
    inverse = lax.linalg.triangular_solve(
        factor, jnp.eye(intersection.shape[0], dtype=jnp.float32), left_side=True, lower=True
    )
    result = jnp.dot(inverse, quarter, precision=lax.Precision.HIGHEST) * scaling
    return lax.all_to_all(result, "band", split_axis=0, concat_axis=1, tiled=True)


def solution(mesh):
    return jax.shard_map(
        body,
        mesh=mesh,
        in_specs=(
            P("band", "dom"),
            P(),
            P("dom"),
            P(None, "dom"),
            P(None, "dom"),
            P("dom"),
            P("dom"),
            P(None, "dom"),
            P(None, "dom"),
        ),
        out_specs=P("band", "dom"),
        check_vma=False,
    )
```

profile of v0, /device:TPU:0, one launch (start us, length us, event | category | flops | bytes accessed | tf_op | source)
XLA Modules:
  0.0 1106.8 jit_solution(18004184117599378335)
XLA Ops:
  44.9 44.6 %gather_fusion.1 = f32[21952,16]{1,0:T(8,128)} fusion(f32[16,17920]{0,1:T(8,128)} %pad_maximum_fusion, s32[22528]{0:T(1024)S(1)} %pad_clamp_fusion), kind=kCustom, calls=%fused_computation.1 | custom fusion | bytes 2897664 | tf_op jit(solution)/shard_map/gather | solution.py:47
  103.2 11.2 %copy.187 = f32[343,64,16]{2,1,0:T(8,128)} copy(f32[343,64,16]{0,1,2:T(8,128)} %fusion.21) | data formatting | bytes 2809856 | tf_op jit(solution)/shard_map/mul | solution.py:56
  114.5 121.9 %scatter_custom_fusion.1 = f32[16,17920]{0,1:T(8,128)} fusion(s32[21952]{0:T(1024)S(1)} %reshape.364, f32[21952,16]{1,0:T(8,128)} %bitcast.120, f32[]{:T(128)} %constant.191.clone.1), kind=kCustom, calls=%fused_computation.31 | custom fusion | flops 351232 | bytes 1147392 | tf_op jit(solution)/shard_map/scatter-add | solution.py:57
  261.7 25.6 %scatter_custom_fusion.2 = f32[16,13824]{0,1:T(8,128)} fusion(f32[16,13824]{0,1:T(8,128)} %fusion.35, s32[3456]{0:T(1024)S(1)} %fusion.50, f32[16,3456]{0,1:T(8,128)S(1)} %bitcast_multiply_fusion.2), kind=kCustom, calls=%fused_computation.39 | custom fusion | flops 55296 | bytes 2654208 | tf_op jit(solution)/shard_map/scatter-add | solution.py:43
  287.4 10.1 scatter_custom_fusion.3
  306.6 10.3 gather_fusion.3
  319.7 10.4 scatter_fusion.1
  346.5 10.1 pad_maximum_fusion.1
  356.6 44.6 %gather_fusion.4 = f32[21952,16]{1,0:T(8,128)} fusion(f32[16,17920]{0,1:T(8,128)} %pad_maximum_fusion.1, s32[22528]{0:T(1024)S(1)} %pad_clamp_fusion), kind=kCustom, calls=%fused_computation.4 | custom fusion | bytes 2897664 | tf_op jit(solution)/shard_map/gather | solution.py:47
  401.1 10.3 copy.155
  417.6 11.2 %copy.190 = f32[343,64,16]{2,1,0:T(8,128)} copy(f32[343,64,16]{0,1,2:T(8,128)} %fusion.17) | data formatting | bytes 2809856 | tf_op jit(solution)/shard_map/mul | solution.py:56
  428.8 121.8 %scatter_custom_fusion.5 = f32[16,17920]{0,1:T(8,128)} fusion(s32[21952]{0:T(1024)S(1)} %reshape.364, f32[21952,16]{1,0:T(8,128)} %bitcast.121, f32[]{:T(128)} %constant.191.clone.1), kind=kCustom, calls=%fused_computation.29 | custom fusion | flops 351232 | bytes 1147392 | tf_op jit(solution)/shard_map/scatter-add | solution.py:57
  584.3 26.0 %scatter_custom_fusion.6 = f32[16,13824]{0,1:T(8,128)} fusion(f32[16,13824]{0,1:T(8,128)} %fusion.34, s32[3456]{0:T(1024)S(1)} %fusion.50, f32[16,3456]{0,1:T(8,128)} %bitcast_multiply_fusion.1), kind=kCustom, calls=%fused_computation.36 | custom fusion | flops 55296 | bytes 2654208 | tf_op jit(solution)/shard_map/scatter-add | solution.py:43
  610.3 10.1 scatter_custom_fusion.7
  631.8 10.3 gather_fusion.6
  678.7 44.6 %gather_fusion.7 = f32[21952,16]{1,0:T(8,128)} fusion(f32[16,17920]{0,1:T(8,128)} %pad_maximum_fusion.2, s32[22528]{0:T(1024)S(1)} %pad_clamp_fusion), kind=kCustom, calls=%fused_computation.7 | custom fusion | bytes 2897664 | tf_op jit(solution)/shard_map/gather | solution.py:47
  723.2 10.3 copy.170
  739.7 11.2 %copy.193 = f32[343,64,16]{2,1,0:T(8,128)} copy(f32[343,64,16]{0,1,2:T(8,128)} %fusion.13) | data formatting | bytes 2809856 | tf_op jit(solution)/shard_map/mul | solution.py:56
  750.9 121.8 %scatter_custom_fusion.9 = f32[16,17920]{0,1:T(8,128)} fusion(s32[21952]{0:T(1024)S(1)} %reshape.364, f32[21952,16]{1,0:T(8,128)} %bitcast.119, f32[]{:T(128)} %constant.191.clone.1), kind=kCustom, calls=%fused_computation.27 | custom fusion | flops 351232 | bytes 1147392 | tf_op jit(solution)/shard_map/scatter-add | solution.py:57
  908.7 26.0 %scatter_custom_fusion.10 = f32[16,13824]{0,1:T(8,128)} fusion(f32[16,13824]{0,1:T(8,128)} %fusion.33, s32[3456]{0:T(1024)S(1)} %fusion.50, f32[16,3456]{0,1:T(8,128)} %bitcast_multiply_fusion), kind=kCustom, calls=%fused_computation.33 | custom fusion | flops 55296 | bytes 2654208 | tf_op jit(solution)/shard_map/scatter-add | solution.py:43
  934.7 10.1 scatter_custom_fusion.11
  979.6 18.0 %all_to_all.38 = f32[16,4,3456]{2,0,1:T(8,128)S(1)} all-to-all(f32[16,4,3456]{2,0,1:T(8,128)S(1)} %copy.180), channel_id=1, replica_groups=mesh['dom'=32,'band'=4] {'band'}, dimensions={1} | all-to-all | bytes 1769472 | tf_op jit(solution)/shard_map/all_to_all | solution.py:72
  998.5 77.9 %psum.7 = f32[64,64]{0,1:T(8,128)S(1)} all-reduce(f32[64,64]{0,1:T(8,128)S(1)} %fusion.57), channel_id=1, replica_groups=mesh['dom'=32,'band'=4] {'dom','band'}, use_global_device_ids=true, to_apply=%region_18.0 | all-reduce | flops 4096 | bytes 32768 | tf_op jit(solution)/shard_map/psum | solution.py:74
  1089.7 15.8 %all_to_all.39 = f32[4,16,3456]{2,1,0:T(8,128)S(1)} all-to-all(f32[4,16,3456]{2,1,0:T(8,128)S(1)} %bitcast.122), channel_id=1, replica_groups=mesh['dom'=32,'band'=4] {'band'}, dimensions={0} | all-to-all | bytes 1769472 | tf_op jit(solution)/shard_map/all_to_all | solution.py:80
  (136 shorter events, 291.2 us)
Async XLA Ops:
  0.0 98.9 %copy-start = (f32[343,343]{1,0:T(8,128)S(1)}, f32[343,343]{1,0:T(8,128)}, u32[]{:S(2)}) copy-start(f32[343,343]{1,0:T(8,128)} %param.22) | copy-start | bytes 1411792
  0.0 15.6 %copy-start.4 = (f32[4,864]{1,0:T(4,128)S(1)}, f32[4,864]{1,0:T(4,128)}, u32[]{:S(2)}) copy-start(f32[4,864]{1,0:T(4,128)} %param.29) | copy-start | bytes 41476
  6.8 26.6 %copy-start.5 = (s32[343,64]{0,1:T(8,128)S(1)}, s32[343,64]{0,1:T(8,128)}, u32[]{:S(2)}) copy-start(s32[343,64]{0,1:T(8,128)} %param.25) | copy-start | bytes 263428
  28.2 6.5 collective-permute-start.1
  29.8 4.5 collective-permute-start
  89.5 9.4 copy-start.3
  89.5 9.4 copy-start.7
  114.5 127.5 %copy-start.6 = (s32[4,864]{1,0:T(4,128)S(1)}, s32[4,864]{1,0:T(4,128)}, u32[]{:S(2)}) copy-start(s32[4,864]{1,0:T(4,128)} %param.28) | copy-start | bytes 41476
  238.4 11.3 %collective-permute-start.2 = (f32[16,2048]{1,0:T(8,128)S(1)}, f32[16,2048]{1,0:T(8,128)S(1)}, u32[]{:S(2)}, u32[]{:S(2)}) collective-permute-start(f32[16,2048]{1,0:T(8,128)S(1)} %copy.143), channel_id=1, source_target_pairs={{0,4},{4,8},{8,12},{12,16},{16,20},{20,24},{24,28},{28,32},{32,36}... | collective-permute-start | bytes 393224 | tf_op jit(solution)/shard_map/ppermute | solution.py:16
  248.4 5.2 collective-permute-start.3
  287.4 14.8 %copy-start.1 = (f32[16,13824]{1,0:T(8,128)S(1)}, f32[16,13824]{1,0:T(8,128)}, u32[]{:S(2)}) copy-start(f32[16,13824]{1,0:T(8,128)} %param.21) | copy-start | bytes 2654212
  302.2 17.5 %copy-start.2 = (f32[16,13824]{1,0:T(8,128)}, f32[16,13824]{1,0:T(8,128)S(1)}, u32[]{:S(2)}) copy-start(f32[16,13824]{1,0:T(8,128)S(1)} %copy.147) | copy-start | bytes 2654212
  334.7 8.5 collective-permute-start.4
  341.7 3.5 collective-permute-start.5
  555.2 13.8 %collective-permute-start.6 = (f32[16,2048]{1,0:T(8,128)S(1)}, f32[16,2048]{1,0:T(8,128)S(1)}, u32[]{:S(2)}, u32[]{:S(2)}) collective-permute-start(f32[16,2048]{1,0:T(8,128)S(1)} %copy.158), channel_id=1, source_target_pairs={{0,4},{4,8},{8,12},{12,16},{16,20},{20,24},{24,28},{28,32},{32,36}... | collective-permute-start | bytes 393224 | tf_op jit(solution)/shard_map/ppermute | solution.py:16
  567.3 6.3 collective-permute-start.7
  658.8 6.0 collective-permute-start.8
  663.3 4.0 collective-permute-start.9
  877.3 16.1 %collective-permute-start.10 = (f32[16,2048]{1,0:T(8,128)S(1)}, f32[16,2048]{1,0:T(8,128)S(1)}, u32[]{:S(2)}, u32[]{:S(2)}) collective-permute-start(f32[16,2048]{1,0:T(8,128)S(1)} %copy.173), channel_id=1, source_target_pairs={{0,4},{4,8},{8,12},{12,16},{16,20},{20,24},{24,28},{28,32},{32,36}... | collective-permute-start | bytes 393224 | tf_op jit(solution)/shard_map/ppermute | solution.py:16
  891.9 6.1 collective-permute-start.11
where the time goes:
time: 1110 us
  other arithmetic  518 us (47%)
  local copies, waits for them, and re-layouts  417 us (38%)
  blocking collectives  112 us (10%)
  starting transfers between devices  37.7 us (3%)
  matrix products  18.6 us (2%)
    scatter-add x3, other arithmetic, apply(): accum = empty.at[:, cell_dofs].add(out)  366 us
    gather x6, local copies, waits for them, and re-layouts, products(): gathered = extended[:, dofs]  164 us
    psum x1, blocking collectives, body(): intersection = lax.psum(intersection, ('dom', 'band'))  77.9 us
    scatter-add x3, other arithmetic, condense(): y = y.at[:, hang_masters.reshape(-1)].add(contrib.reshape(states, -1))  77.7 us
    scatter x6, local copies, waits for them, and re-layouts, condense(): y.at[:, hang_rows].set(jnp.zeros((states, hang_rows.shape[0]), jnp.float32))  45.1 us
    scatter x4, local copies, waits for them, and re-layouts, distribute(): return v.at[:, hang_rows].set(vals)  40.5 us
    gather x4, local copies, waits for them, and re-layouts, distribute(): vals = jnp.sum(hang_weights[None] * v[:, hang_masters], axis=1)  38.3 us
    mul x3, local copies, waits for them, and re-layouts, apply(): products(extended, cell_dofs, cell_scale, potential) * alive[None, None, :]  33.7 us
  transfers between devices with their start and end apart: 12, of which 3 were waited for; matrix products, arithmetic and copies ran while one was open for 4% of the time, Pallas kernels for 0%

commit v1 on v0

v1 whole, which is shorter than its diff:
```python
import functools
import jax
import jax.numpy as jnp
from jax import lax
from jax.experimental import pallas as pl
from jax.experimental.pallas import tpu as pltpu
from jax.sharding import PartitionSpec as P

RIM = 2048
NODES = 343
HANG = 864
MASTERS = 4
LOC = 13824
CELLS = 64
S = 16
L = 128
EXT = LOC + 2 * RIM
NB = LOC // L
RB = RIM // L
NPAD = 384
NJ = NPAD // L
WB = 7
TOPB = EXT // L - WB
SLOTS = 3 * CELLS
GROUP = 16
HPAD = 896
HB = HPAD // L
ME = MASTERS * HPAD
HE = 1024
E = ME + HE
QLO = 256
QHI = 18
BIG = 1 << 20
CENTRE = 4.5
HALF = 3.5
F32 = jnp.float32
BF16 = jnp.bfloat16
I32 = jnp.int32
VLIM = 40 * 1024 * 1024

VM = pl.BlockSpec(memory_space=pltpu.VMEM)
SM = pl.BlockSpec(memory_space=pltpu.SMEM)
NT = (((1,), (1,)), ((), ()))


def iota(shape, dim):
    return lax.broadcasted_iota(I32, shape, dim)


def lanes(x, idx):
    return jnp.take_along_axis(x, idx, axis=1, mode="promise_in_bounds")


def nn(a, b):
    return jnp.dot(a, b, preferred_element_type=F32)


def nt(a, b):
    return lax.dot_general(a, b, NT, preferred_element_type=F32)


def split(x):
    hi = x.astype(BF16)
    return hi, (x - hi.astype(F32)).astype(BF16)


def at(b):
    return pl.ds(pl.multiple_of(b * L, L), L)


def hang_tables(ent_ref, a_ref, b_ref, lhs_ref, oh_ref, pe_ref, src_ref, posr_ref, hq_ref, start_ref):
    for i in range(E // L):
        col = slice(i * L, (i + 1) * L)
        row = jnp.broadcast_to(ent_ref[0:1, col], (L, L))
        it = iota((L, L), 0)
        a_ref[:, col] = (it == (row >> 7)).astype(F32).astype(BF16)
        b_ref[:, col] = (((row & 127) == it) & (row >= 0)).astype(F32).astype(BF16)
    flag = nt(a_ref[...], b_ref[...]) > 0.5
    flagb = flag.astype(F32).astype(BF16)
    tri = (iota((L, L), 0) < iota((L, L), 1)).astype(F32).astype(BF16)
    low = (iota((L, L), 1) < iota((L, L), 0)).astype(F32).astype(BF16)
    ones = jnp.ones((L, L), BF16)
    total = nn(flagb, ones)
    pos = nn(flagb, tri) + nn(low, total.astype(BF16))
    pos = pos.astype(I32)
    posr_ref[...] = jnp.where(flag, pos, -1)
    totrow = nt(jnp.ones((8, L), BF16), flagb)
    start_ref[...] = nn(totrow.astype(BF16), tri).astype(I32)
    ph = (pos >> 8).astype(F32).astype(BF16)
    plo = (pos & 255).astype(F32).astype(BF16)
    for i in range(E // L):
        col = slice(i * L, (i + 1) * L)
        ent = ent_ref[0:1, col]
        mask = a_ref[:, col].astype(F32)
        b = b_ref[:, col]
        hi = jnp.sum(nn(ph, b) * mask, axis=0, keepdims=True)
        lo = jnp.sum(nn(plo, b) * mask, axis=0, keepdims=True)
        pe = jnp.where(ent >= 0, hi.astype(I32) * QLO + lo.astype(I32), BIG)
        pe_ref[0:1, col] = pe
        good = jnp.broadcast_to(pe, (QLO, L))
        oh_ref[:, col] = ((good & 255) == iota((QLO, L), 0)).astype(F32).astype(BF16)
        qm = (jnp.broadcast_to(pe >> 8, (24, L)) == iota((24, L), 0)).astype(F32)
        lhs_ref[0:24, col] = qm.astype(BF16)
        lhs_ref[24:48, col] = (qm * (ent >> 7).astype(F32)).astype(BF16)
        lhs_ref[48:72, col] = (qm * (ent & 127).astype(F32)).astype(BF16)
        lhs_ref[72:96, col] = (qm if i >= ME // L else jnp.zeros_like(qm)).astype(BF16)
    res = nt(lhs_ref[...], oh_ref[...])
    cnt = res[0:24]
    den = jnp.maximum(cnt, 1.0)
    blk = (res[24:48] / den + 0.5).astype(I32)
    lo = (res[48:72] / den + 0.5).astype(I32)
    src = jnp.where(cnt > 0.5, blk * L + lo, -1)
    for q in range(24):
        src_ref[2 * q : 2 * q + 1, :] = src[q : q + 1, 0:L]
        src_ref[2 * q + 1 : 2 * q + 2, :] = src[q : q + 1, L : 2 * L]
    hq_ref[...] = res[72:96]


def zat(c):
    return pl.ds(pl.multiple_of((c >> 1) * S, S), S), pl.ds(pl.multiple_of((c & 1) * L, L), L)


def compress(y_ref, yoff, z_ref, src_ref, start_ref):
    z_ref[...] = jnp.zeros_like(z_ref)

    def step(b, _):
        y = y_ref[:, at(b + yoff)]
        c0 = start_ref[0, b] >> 7
        for t in range(2):
            c = c0 + t
            row = jnp.broadcast_to(src_ref[pl.ds(c, 1), :], (S, L))
            r, l = zat(c)
            z_ref[r, l] = jnp.where((row >> 7) == b, lanes(y, row & 127), z_ref[r, l])
        return 0

    lax.fori_loop(0, NB, step, 0, unroll=6)


def expand(b, y, z_ref, posr_ref, start_ref):
    row = jnp.broadcast_to(posr_ref[pl.ds(b, 1), :], (S, L))
    c0 = start_ref[0, b] >> 7
    for t in range(2):
        c = c0 + t
        r, l = zat(c)
        y = jnp.where((row >> 7) == c, lanes(z_ref[r, l], row & 127), y)
    return y


def gather_entries(z_ref, oh_ref, pe_ref, g_ref, first, last):
    zh, zl = split(z_ref[...])
    for i in range(first // QLO, last // QLO):
        col = slice(i * QLO, (i + 1) * QLO)
        oh = oh_ref[:, col]
        g = nn(zh, oh) + nn(zl, oh)
        q = jnp.broadcast_to(pe_ref[0:1, col] >> 8, (S, QLO))
        acc = jnp.zeros((S, QLO), F32)
        for h in range(QHI):
            acc = jnp.where(q == h, g[h * S : (h + 1) * S], acc)
        g_ref[:, col] = acc


def scatter_entries(g_ref, oh_ref, pe_ref, lh_ref, ll_ref, first, last):
    for i in range(first // L, last // L):
        col = slice(i * L, (i + 1) * L)
        g = g_ref[:, col]
        hi = g.astype(BF16).astype(F32)
        lo = g - hi
        q = jnp.broadcast_to(pe_ref[0:1, col] >> 8, (S, L))
        for h in range(QHI):
            m = q == h
            lh_ref[h * S : (h + 1) * S, col] = jnp.where(m, hi, 0.0).astype(BF16)
            ll_ref[h * S : (h + 1) * S, col] = jnp.where(m, lo, 0.0).astype(BF16)
    oh = oh_ref[:, first:last]
    return nt(lh_ref[:, first:last], oh) + nt(ll_ref[:, first:last], oh)


def hanging_values(z_ref, oh_ref, pe_ref, w_ref, g_ref, lh_ref, ll_ref, hq_ref):
    gather_entries(z_ref, oh_ref, pe_ref, g_ref, 0, ME)
    g_ref[:, ME + HPAD :] = jnp.zeros((S, HE - HPAD), F32)
    for j in range(HB):
        acc = jnp.zeros((S, L), F32)
        for k in range(MASTERS):
            col = slice(k * HPAD + j * L, k * HPAD + (j + 1) * L)
            acc = acc + g_ref[:, col] * w_ref[0:1, col]
        g_ref[:, ME + j * L : ME + (j + 1) * L] = acc
    cz = scatter_entries(g_ref, oh_ref, pe_ref, lh_ref, ll_ref, ME, E)
    for h in range(QHI):
        r = slice(h * S, (h + 1) * S)
        m = jnp.broadcast_to(hq_ref[h : h + 1, :], (S, QLO)) > 0.5
        z_ref[r, :] = jnp.where(m, cz[r], z_ref[r, :])


def add_to_masters(z_ref, oh_ref, pe_ref, w_ref, g_ref, lh_ref, ll_ref):
    gather_entries(z_ref, oh_ref, pe_ref, g_ref, ME, E)
    for j in range(HB):
        y = g_ref[:, ME + j * L : ME + (j + 1) * L]
        for k in range(MASTERS):
            col = slice(k * HPAD + j * L, k * HPAD + (j + 1) * L)
            g_ref[:, col] = y * w_ref[0:1, col]
    z_ref[...] += scatter_entries(g_ref, oh_ref, pe_ref, lh_ref, ll_ref, 0, ME)


def prepare_kernel(
    ent_ref, w_ref, block_ref,
    oh_ref, pe_ref, src_ref, posr_ref, hq_ref, start_ref, u_ref, left_ref, right_ref,
    a_ref, b_ref, lhs_ref, z_ref, g_ref, lh_ref, ll_ref, start_s, sem,
):
    hang_tables(ent_ref, a_ref, b_ref, lhs_ref, oh_ref, pe_ref, src_ref, posr_ref, hq_ref, start_ref)
    copy = pltpu.make_async_copy(start_ref, start_s, sem)
    copy.start()
    copy.wait()
    compress(block_ref, 0, z_ref, src_ref, start_s)
    hanging_values(z_ref, oh_ref, pe_ref, w_ref, g_ref, lh_ref, ll_ref, hq_ref)

    def step(b, _):
        u_ref[:, at(b)] = expand(b, block_ref[:, at(b)], z_ref, posr_ref, start_s)
        return 0

    lax.fori_loop(0, NB, step, 0, unroll=6)
    left_ref[...] = u_ref[:, 0:RIM]
    right_ref[...] = u_ref[:, LOC - RIM :]


def sds(shape, dtype=F32):
    return jax.ShapeDtypeStruct(shape, dtype)


HANG_SCRATCH = [
    pltpu.VMEM((QHI * S, QLO), F32),
    pltpu.VMEM((S, E), F32),
    pltpu.VMEM((QHI * S, E), BF16),
    pltpu.VMEM((QHI * S, E), BF16),
]


def prepare(ent, w, block):
    return pl.pallas_call(
        prepare_kernel,
        out_shape=(
            sds((QLO, E), BF16),
            sds((1, E), I32),
            sds((48, L), I32),
            sds((L, L), I32),
            sds((24, QLO)),
            sds((8, L), I32),
            sds((S, LOC)),
            sds((S, RIM)),
            sds((S, RIM)),
        ),
        in_specs=[VM] * 3,
        out_specs=(VM,) * 9,
        scratch_shapes=[
            pltpu.VMEM((L, E), BF16),
            pltpu.VMEM((L, E), BF16),
            pltpu.VMEM((96, E), BF16),
            *HANG_SCRATCH,
            pltpu.SMEM((8, L), I32),
            pltpu.SemaphoreType.DMA,
        ],
        compiler_params=pltpu.CompilerParams(vmem_limit_bytes=VLIM),
        name="prepare",
    )(ent, w, block)


def cells_kernel(own_ref, left_ref, right_ref, tab_ref, pot_ref, b0_ref, all_ref, meta_ref, meta_s, list_s, sem):
    for i, (ref, shift) in enumerate(((own_ref, 0), (left_ref, -LOC), (right_ref, LOC))):
        r = slice(i * CELLS, (i + 1) * CELLS)
        dofs = ref[:, 0:NPAD].astype(I32) + shift
        real = iota((CELLS, NPAD), 1) < NODES
        all_ref[r, 0:NPAD] = jnp.where(real, dofs, BIG).astype(F32)
        all_ref[r, NPAD:] = ref[:, NPAD:]
        low = jnp.min(jnp.where(real, dofs, BIG).astype(F32), axis=1, keepdims=True)
        top = jnp.max(jnp.where(real, dofs, -BIG).astype(F32), axis=1, keepdims=True)
        live = ref[:, 2 * NPAD + 1 : 2 * NPAD + 2] > 0.5
        used = live & (top >= RIM) & (low < RIM + LOC)
        base = jnp.clip(low.astype(I32) >> 7, 0, TOPB)
        meta_ref[r, :] = jnp.broadcast_to(jnp.where(used, base, -1), (CELLS, L))
    copy = pltpu.make_async_copy(meta_ref, meta_s, sem)
    copy.start()
    copy.wait()

    def scan(c, n):
        b = meta_s[c, 0]
        list_s[n] = c
        b0_ref[n] = b
        return n + jnp.where(b >= 0, 1, 0)

    n = lax.fori_loop(0, SLOTS, scan, 0, unroll=4)

    def blank(i, _):
        list_s[n + i] = 0
        b0_ref[n + i] = 0
        return 0

    lax.fori_loop(0, GROUP, blank, 0)
    groups = (n + GROUP - 1) // GROUP
    b0_ref[SLOTS + 2 * GROUP - 1] = groups

    def one(slot):
        c = list_s[slot]
        b0 = b0_ref[slot]
        valid = slot < n
        vals = all_ref[pl.ds(c, 1), :]
        rel = vals[:, 0:NPAD].astype(I32) - b0 * L
        rel = jnp.where(valid & (rel < WB * L), rel, BIG)
        hi = rel >> 7
        lo = rel & 127
        it = iota((L, NPAD), 0)
        oh = ((jnp.broadcast_to(lo, (L, NPAD)) == it)).astype(F32).astype(BF16)
        node = iota((8, NPAD), 1)
        m = jnp.broadcast_to(hi, (8, NPAD)) == iota((8, NPAD), 0)
        first = jnp.where(m, (node >> 7) + 1, 0).astype(F32)
        second = jnp.where(m, node & 127, 0).astype(F32)
        res = nt(jnp.concatenate([first, second], 0).astype(BF16), oh)
        nh = res[0:8].astype(I32)
        inv = jnp.where(nh > 0, (nh - 1) * L + res[8:16].astype(I32), BIG)
        tab_ref[slot, 8:16, :] = inv
        for j in range(NJ):
            tab_ref[slot, j : j + 1, :] = rel[:, j * L : (j + 1) * L]
            pot_ref[slot, j : j + 1, :] = vals[:, NPAD + j * L : NPAD + (j + 1) * L]
        pot_ref[slot, 3:4, :] = jnp.broadcast_to(vals[:, 2 * NPAD : 2 * NPAD + 1], (1, L))

    def four(i, _):
        for k in range(4):
            one(i * 4 + k)
        return 0

    lax.fori_loop(0, groups * (GROUP // 4), four, 0)


def cell_tables(own, left, right):
    return pl.pallas_call(
        cells_kernel,
        out_shape=(sds((SLOTS, 16, L), I32), sds((SLOTS, 8, L)), sds((SLOTS + 2 * GROUP,), I32)),
        in_specs=[VM] * 3,
        out_specs=(VM, VM, SM),
        scratch_shapes=[
            pltpu.VMEM((SLOTS, 7 * L), F32),
            pltpu.VMEM((SLOTS, L), I32),
            pltpu.SMEM((SLOTS, L), I32),
            pltpu.SMEM((SLOTS + 2 * GROUP,), I32),
            pltpu.SemaphoreType.DMA,
        ],
        compiler_params=pltpu.CompilerParams(vmem_limit_bytes=VLIM),
        name="cell_tables",
    )(own, left, right)


def step_kernel(number, *refs):
    (u_ref, gl_ref, gr_ref, prev_ref, tab_ref, pot_ref, kt_ref,
     oh_ref, pe_ref, src_ref, posr_ref, hq_ref, w_ref, b0_ref, start_ref, me_ref) = refs[:16]
    outs = refs[16 : 16 + (4 if number == 3 else 3)]
    ext_ref, acc_ref, x_ref, p_ref, kh_ref, kl_ref, z_ref, g_ref, lh_ref, ll_ref = refs[16 + len(outs) :]
    kh_ref[...], kl_ref[...] = split(kt_ref[...])
    ext_ref[:, 0:RIM] = gl_ref[...]
    ext_ref[:, RIM : RIM + LOC] = u_ref[...]
    ext_ref[:, RIM + LOC :] = gr_ref[...]
    acc_ref[...] = jnp.zeros_like(acc_ref)
    groups = b0_ref[SLOTS + 2 * GROUP - 1]

    def load(slot):
        b0 = b0_ref[slot]
        for j in range(NJ):
            row = jnp.broadcast_to(tab_ref[slot, j : j + 1, :], (8, L))
            lo, hi = row & 127, row >> 7
            for s in range(2):
                acc = jnp.zeros((8, L), F32)
                for k in range(WB):
                    acc = jnp.where(hi == k, lanes(ext_ref[8 * s : 8 * s + 8, at(b0 + k)], lo), acc)
                x_ref[pl.ds(slot * S + 8 * s, 8), j * L : (j + 1) * L] = acc

    def loads(i, _):
        for k in range(4):
            load(i * 4 + k)
        return 0

    lax.fori_loop(0, groups * (GROUP // 4), loads, 0)

    def product(i, _):
        r = pl.ds(pl.multiple_of(i * (GROUP * S), GROUP * S), GROUP * S)
        xh, xl = split(x_ref[r, :])
        kh, kl = kh_ref[...], kl_ref[...]
        p_ref[r, :] = nn(xh, kh) + (nn(xl, kh) + nn(xh, kl))
        return 0

    lax.fori_loop(0, groups, product, 0)

    def store(slot):
        b0 = b0_ref[slot]
        scale = jnp.broadcast_to(pot_ref[slot, 3:4, :], (8, L))
        vals = []
        for s in range(2):
            r = pl.ds(slot * S + 8 * s, 8)
            vals.append([])
            for j in range(NJ):
                col = slice(j * L, (j + 1) * L)
                pot = jnp.broadcast_to(pot_ref[slot, j : j + 1, :], (8, L))
                vals[s].append(scale * p_ref[r, col] + pot * x_ref[r, col])
        for k in range(WB):
            row = jnp.broadcast_to(tab_ref[slot, 8 + k : 9 + k, :], (8, L))
            lo, hi = row & 127, row >> 7
            for s in range(2):
                acc = jnp.zeros((8, L), F32)
                for j in range(NJ):
                    acc = jnp.where(hi == j, lanes(vals[s][j], lo), acc)
                acc_ref[8 * s : 8 * s + 8, at(b0 + k)] += acc

    def stores(i, _):
        for k in range(4):
            store(i * 4 + k)
        return 0

    lax.fori_loop(0, groups * (GROUP // 4), stores, 0)

    compress(acc_ref, RB, z_ref, src_ref, start_ref)
    add_to_masters(z_ref, oh_ref, pe_ref, w_ref, g_ref, lh_ref, ll_ref)
    hanging_values(z_ref, oh_ref, pe_ref, w_ref, g_ref, lh_ref, ll_ref, hq_ref)
    new_ref = outs[0] if number < 3 else ext_ref

    def finish(b, _):
        t = expand(b, acc_ref[:, at(b + RB)], z_ref, posr_ref, start_ref)
        r = (t - CENTRE * u_ref[:, at(b)]) * ((1.0 if number == 1 else 2.0) / HALF)
        if number > 1:
            r = r - prev_ref[:, at(b)]
        new_ref[:, at(b)] = r
        return 0

    lax.fori_loop(0, NB, finish, 0, unroll=6)
    if number < 3:
        outs[1][...] = new_ref[:, 0:RIM]
        outs[2][...] = new_ref[:, LOC - RIM :]
    else:
        me = me_ref[0]
        q = LOC // 4
        for k in range(4):
            outs[k][...] = new_ref[:, pl.ds(pl.multiple_of(((me + k) & 3) * q, L), q)]


def apply_step(number, u, gl, gr, prev, tab, pot, b0, kt, hang, w, start, me):
    oh, pe, src, posr, hq = hang
    if number == 3:
        shapes = (sds((S, LOC // 4)),) * 4
    else:
        shapes = (sds((S, LOC)), sds((S, RIM)), sds((S, RIM)))
    return pl.pallas_call(
        functools.partial(step_kernel, number),
        out_shape=shapes,
        in_specs=[VM] * 13 + [SM] * 3,
        out_specs=(VM,) * len(shapes),
        scratch_shapes=[
            pltpu.VMEM((S, EXT), F32),
            pltpu.VMEM((S, EXT), F32),
            pltpu.VMEM((SLOTS * S, NPAD), F32),
            pltpu.VMEM((SLOTS * S, NPAD), F32),
            pltpu.VMEM((NPAD, NPAD), BF16),
            pltpu.VMEM((NPAD, NPAD), BF16),
            *HANG_SCRATCH,
        ],
        compiler_params=pltpu.CompilerParams(vmem_limit_bytes=VLIM),
        name=f"step{number}",
    )(u, gl, gr, prev, tab, pot, kt, oh, pe, src, posr, hq, w, b0, start, me)


def gram_kernel(q0_ref, q1_ref, q2_ref, q3_ref, me_ref, gram_ref, all_ref):
    me = me_ref[0]
    for k, ref in enumerate((q0_ref, q1_ref, q2_ref, q3_ref)):
        all_ref[pl.ds(pl.multiple_of(((me - k) & 3) * S, S), S), :] = ref[...]
    a = all_ref[...]
    gram_ref[...] = lax.dot_general(a, a, NT, preferred_element_type=F32, precision=lax.Precision.HIGHEST)


def gram_of(qs, me):
    n = qs[0].shape[1]
    return pl.pallas_call(
        gram_kernel,
        out_shape=(sds((4 * S, 4 * S)), sds((4 * S, n))),
        in_specs=[VM] * 4 + [SM],
        out_specs=(VM, VM),
        compiler_params=pltpu.CompilerParams(vmem_limit_bytes=VLIM),
        name="gram",
    )(*qs, me)


def basis_kernel(total, gram_ref, all_ref, me_ref, o0_ref, o1_ref, o2_ref, o3_ref, m_ref, r_ref):
    n = 4 * S
    eye = (iota((n, n), 0) == iota((n, n), 1)).astype(F32)
    m_ref[...] = jnp.concatenate([gram_ref[...], eye], 1)
    row_id = iota((n, 2 * n), 0)

    m = m_ref[...]
    diag = jnp.zeros((n, 1), F32)
    for j in range(n):
        pivot = m[j : j + 1, :]
        d = pivot[:, j : j + 1]
        f = m[:, j : j + 1] / d
        m = m - jnp.where(row_id > j, f, 0.0) * pivot
    dg = jnp.sum(jnp.where(row_id == iota((n, 2 * n), 1), m, 0.0), axis=1, keepdims=True)
    inv = m[:, n:] * lax.rsqrt(dg) * jnp.sqrt(jnp.float32(total))
    r_ref[...] = jnp.dot(inv, all_ref[...], preferred_element_type=F32, precision=lax.Precision.HIGHEST)
    me = me_ref[0]
    for k, ref in enumerate((o0_ref, o1_ref, o2_ref, o3_ref)):
        ref[...] = r_ref[pl.ds(pl.multiple_of(((me + k) & 3) * S, S), S), :]


def basis_of(gram, rows, me, total):
    n = rows.shape[1]
    return pl.pallas_call(
        functools.partial(basis_kernel, total),
        out_shape=(sds((S, n)),) * 4,
        in_specs=[VM, VM, SM],
        out_specs=(VM,) * 4,
        scratch_shapes=[pltpu.VMEM((4 * S, 8 * S), F32), pltpu.VMEM((4 * S, n), F32)],
        compiler_params=pltpu.CompilerParams(vmem_limit_bytes=VLIM),
        name="basis",
    )(gram, rows, me)


def join_kernel(q0_ref, q1_ref, q2_ref, q3_ref, me_ref, out_ref):
    me = me_ref[0]
    n = q0_ref.shape[1]
    for k, ref in enumerate((q0_ref, q1_ref, q2_ref, q3_ref)):
        out_ref[:, pl.ds(pl.multiple_of(((me - k) & 3) * n, L), n)] = ref[...]


def join(qs, me):
    return pl.pallas_call(
        join_kernel,
        out_shape=sds((S, LOC)),
        in_specs=[VM] * 4 + [SM],
        out_specs=VM,
        compiler_params=pltpu.CompilerParams(vmem_limit_bytes=VLIM),
        name="join",
    )(*qs, me)


def shift(x, axis, by, wrap):
    size = lax.axis_size(axis)
    pairs = [(i, (i + by) % size) for i in range(size) if wrap or 0 <= i + by < size]
    return lax.ppermute(x, axis, pairs)


def swap(x, axis, bits):
    size = lax.axis_size(axis)
    return lax.ppermute(x, axis, [(i, i ^ bits) for i in range(size)])


def summed(g):
    g = g + swap(g, "dom", 1)
    for axis, unit in (("dom", 2), ("dom", 8), ("band", 1)):
        others = [swap(g, axis, unit * k) for k in (1, 2, 3)]
        g = (g + others[0]) + (others[1] + others[2])
    return g


def body(
    block,
    stiffness,
    cell_scale,
    potential,
    cell_dofs,
    cell_count,
    hang_rows,
    hang_masters,
    hang_weights,
):
    me = lax.axis_index("band").astype(I32).reshape(1)
    pad = ((0, 0), (0, NPAD - NODES))
    alive = (jnp.arange(CELLS) < cell_count[0]).astype(F32)
    extra = jnp.concatenate([cell_scale[:, None], alive[:, None], jnp.zeros((CELLS, L - 2), F32)], 1)
    own = jnp.concatenate(
        [jnp.pad(cell_dofs.T.astype(F32), pad), jnp.pad(potential.T, pad), extra], axis=1
    )
    from_left = shift(own, "dom", 1, False)
    from_right = shift(own, "dom", -1, False)

    kt = jnp.pad(stiffness.T, ((0, NPAD - NODES), (0, NPAD - NODES)))
    hpad = ((0, 0), (0, HPAD - HANG))
    ent = jnp.concatenate(
        [
            jnp.pad(hang_masters, hpad, constant_values=-1).reshape(1, ME),
            jnp.pad(hang_rows[None], ((0, 0), (0, HE - HANG)), constant_values=-1),
        ],
        axis=1,
    )
    w = jnp.pad(hang_weights, hpad).reshape(1, ME)

    *hang, start, u0, first, last = prepare(ent, w, block)
    tab, pot, b0 = cell_tables(own, from_left, from_right)

    def ghosts(first, last):
        return shift(last, "dom", 1, False), shift(first, "dom", -1, False)

    args = (tab, pot, b0, kt, hang, w, start, me)
    gl, gr = ghosts(first, last)
    u1, first, last = apply_step(1, u0, gl, gr, u0, *args)
    gl, gr = ghosts(first, last)
    u2, first, last = apply_step(2, u1, gl, gr, u0, *args)
    gl, gr = ghosts(first, last)
    qs = apply_step(3, u2, gl, gr, u1, *args)
    qs = [qs[0]] + [shift(qs[k], "band", k, True) for k in (1, 2, 3)]
    gram, rows = gram_of(qs, me)
    gram = summed(gram)
    outs = basis_of(gram, rows, me, LOC * lax.axis_size("dom"))
    outs = [outs[0]] + [shift(outs[k], "band", k, True) for k in (1, 2, 3)]
    return join(outs, me)


def solution(mesh):
    return jax.shard_map(
        body,
        mesh=mesh,
        in_specs=(
            P("band", "dom"),
            P(),
            P("dom"),
            P(None, "dom"),
            P(None, "dom"),
            P("dom"),
            P("dom"),
            P(None, "dom"),
            P(None, "dom"),
        ),
        out_specs=P("band", "dom"),
        check_vma=False,
    )
```

time: 1110 us -> 198 us (0.18)
  other arithmetic: 518 us -> 0.95 us
  local copies, waits for them, and re-layouts: 417 us -> 13.5 us
  blocking collectives: 112 us -> 0 us
  Pallas kernels: 0 us -> 88.4 us
  starting transfers between devices: 37.7 us -> 64.3 us
  waiting for transfers between devices: 2.24 us -> 27 us
  matrix products: 18.6 us -> 0 us
    scatter-add x12 -> x0, other arithmetic: 460 us -> none  [the longest x3 366 us: apply(): accum = empty.at[:, cell_dofs].add(out)]
    gather x13 -> x0, local copies, waits for them, and re-layouts: 217 us -> none  [the longest x6 164 us: products(): gathered = extended[:, dofs]]
    pallas_call x0 -> x8, Pallas kernels: none -> 88.4 us  [the longest x3 60.7 us: apply_step(): pl.pallas_call(functools.partial(step_kernel, number), out_shape=shapes,...]
    scatter x10 -> x0, local copies, waits for them, and re-layouts: 85.6 us -> none  [the longest x6 45.1 us: condense(): y.at[:, hang_rows].set(jnp.zeros((states, hang_rows.shape[0]), jnp.float32))]
    psum x1 -> x0, blocking collectives: 77.9 us -> none  [body(): intersection = lax.psum(intersection, ('dom', 'band'))]
    slice x21 -> x0, local copies, waits for them, and re-layouts: 44.5 us -> none  [the longest x3 15.5 us: apply(): owned = accum[:, RIM:RIM + local]]
    all_to_all x2 -> x0, blocking collectives: 33.8 us -> none  [the longest x1 18 us: body(): lax.all_to_all(filtered, 'band', split_axis=1, concat_axis=0, tiled=True)]
    mul x4 -> x0, local copies, waits for them, and re-layouts: 33.8 us -> none  [the longest x3 33.7 us: apply(): products(extended, cell_dofs, cell_scale, potential) * alive[None, None, :]]
  transfers between devices with their start and end apart: 12 -> 24, of which waited for: 3 -> 14; matrix products, arithmetic and copies ran while one was open for 4% -> 3% of each run, Pallas kernels for 0% -> 10%
where the time goes in v1:
time: 198 us; the launch traced here: 195 us
  Pallas kernels  88.4 us (45%)
  starting transfers between devices  64.3 us (32%)
  waiting for transfers between devices  27 us (14%)
  local copies, waits for them, and re-layouts  13.5 us (7%)
    pallas_call x3, Pallas kernels, apply_step(): pl.pallas_call(functools.partial(step_kernel, number), out_shape=shapes,...  60.7 us
    ppermute x14, starting transfers between devices, shift(): return lax.ppermute(x, axis, pairs)  38.4 us
    ppermute x10, starting transfers between devices, swap(): return lax.ppermute(x, axis, [(i, i ^ bits) for i in range(size)])  25.9 us
    ppermute x14, waiting for transfers between devices, shift(): return lax.ppermute(x, axis, pairs)  15 us
    ppermute x10, waiting for transfers between devices, swap(): return lax.ppermute(x, axis, [(i, i ^ bits) for i in range(size)])  12 us
    pallas_call x1, Pallas kernels, prepare(): pl.pallas_call(prepare_kernel, out_shape=(sds((QLO, E), BF16), sds((1, E)...  11.3 us
    unnamed x23, local copies, waits for them, and re-layouts  9.95 us
    pallas_call x1, Pallas kernels, cell_tables(): pl.pallas_call(cells_kernel, out_shape=(sds((SLOTS, 16, L), I32), sds((SL...  8.2 us
  transfers between devices with their start and end apart: 24, of which 14 were waited for; matrix products, arithmetic and copies ran while one was open for 3% of the time, Pallas kernels for 10%

profile of v1, /device:TPU:0, one launch (start us, length us, event | category | flops | bytes accessed | tf_op | source)
XLA Modules:
  0.0 194.9 jit_solution(10003089921589818707)
XLA Ops:
  4.6 3.7 %collective-permute-start.2 = (f32[64,896]{1,0:T(8,128)S(1)}, f32[64,896]{1,0:T(8,128)}, u32[]{:S(2)}, u32[]{:S(2)}) collective-permute-start(f32[64,896]{1,0:T(8,128)S(1)} %concatenate.7.own_ref), channel_id=1, source_target_pairs={{0,4},{4,8},{8,12},{12,16},{16,20},{20,24},{24,28},{28,32},{32,36}... | collective-permute-start | bytes 688136 | tf_op jit(solution)/shard_map/ppermute | solution.py:539
  11.7 11.3 %prepare.1 = (bf16[256,4608]{1,0:T(8,128)(2,1)S(1)}, s32[1,4608]{1,0:T(1,128)S(1)}, s32[48,128]{1,0:T(8,128)S(1)}, s32[128,128]{1,0:T(8,128)S(1)}, f32[24,256]{1...) custom-call(s32[1,4608]{1,0:T(1,128)S(1)} %fusion.1.ent_ref, ...), custom_call_target="tpu_custom_call" | custom-call | tf_op jit(solution)/shard_map/prepare/pallas_call | solution.py:237
  25.4 3.1 %collective-permute-start = (f32[16,2048]{1,0:T(8,128)}, f32[16,2048]{1,0:T(8,128)}, u32[]{:S(2)}, u32[]{:S(2)}) collective-permute-start(f32[16,2048]{1,0:T(8,128)} %get-tuple-element.34), channel_id=1, source_target_pairs={{0,4},{4,8},{8,12},{12,16},{16,20},{20,24},{24,28},{28,32},{32,36}... | collective-permute-start | bytes 393224 | tf_op jit(solution)/shard_map/ppermute | solution.py:539
  29.8 2.1 %copy.11 = f32[343,343]{0,1:T(8,128)} copy(f32[343,343]{1,0:T(8,128)} %param.10) | data formatting | bytes 941192 | tf_op args[1]
  33.0 8.2 %cell_tables.1 = (s32[192,16,128]{2,1,0:T(8,128)S(1)}, f32[192,8,128]{2,1,0:T(8,128)S(1)}, s32[224]{0:T(256)S(1)}) custom-call(f32[64,896]{1,0:T(8,128)S(1)} %concatenate.7.own_ref, f32[64,896]{1,0:T(8,128)} %collective-permute-done.2.left_ref, f32[64,896]{1,0:T(8,128)} %collective-permute-done.3.right_ref), custom_call_target="tpu_custom_call" | custom-call | tf_op jit(solution)/shard_map/cell_tables/pallas_call | solution.py:332
  44.1 20.4 %step1.1 = (f32[16,13824]{1,0:T(8,128)S(1)}, f32[16,2048]{1,0:T(8,128)S(1)}, f32[16,2048]{1,0:T(8,128)S(1)}) custom-call(f32[16,13824]{1,0:T(8,128)S(1)} %get-tuple-element.33.refs_0_.refs_3_, f32[16,2048]{1,0:T(8,128)} %collective-permute-done.refs_1_, f32[16,2048]{1,0:T(8,128)} %collective-permute-done.1.refs_2_, ...), custom_call_target="tpu_custom_call" | custom-call | tf_op jit(solution)/shard_map/step1/pallas_call | solution.py:445
  64.5 7.1 %collective-permute-start.4 = (f32[16,2048]{1,0:T(8,128)S(1)}, f32[16,2048]{1,0:T(8,128)S(1)}, u32[]{:S(2)}, u32[]{:S(2)}) collective-permute-start(f32[16,2048]{1,0:T(8,128)S(1)} %get-tuple-element.46), channel_id=1, source_target_pairs={{0,4},{4,8},{8,12},{12,16},{16,20},{20,24},{24,28},{28,32},{32,36}... | collective-permute-start | bytes 393224 | tf_op jit(solution)/shard_map/ppermute | solution.py:539
  73.0 1.9 collective-permute-done.5.refs_2_
  74.9 20.2 %step2.1 = (f32[16,13824]{1,0:T(8,128)S(1)}, f32[16,2048]{1,0:T(8,128)S(1)}, f32[16,2048]{1,0:T(8,128)S(1)}) custom-call(f32[16,13824]{1,0:T(8,128)S(1)} %get-tuple-element.45.refs_0_.refs_3_, f32[16,2048]{1,0:T(8,128)S(1)} %collective-permute-done.4.refs_1_, f32[16,2048]{1,0:T(8,128)S(1)} %collective-permute-done.5.refs_2_, ...), custom_call_target="tpu_custom_call" | custom-call | tf_op jit(solution)/shard_map/step2/pallas_call | solution.py:445
  95.1 8.0 %collective-permute-start.6 = (f32[16,2048]{1,0:T(8,128)S(1)}, f32[16,2048]{1,0:T(8,128)S(1)}, u32[]{:S(2)}, u32[]{:S(2)}) collective-permute-start(f32[16,2048]{1,0:T(8,128)S(1)} %get-tuple-element.49), channel_id=1, source_target_pairs={{0,4},{4,8},{8,12},{12,16},{16,20},{20,24},{24,28},{28,32},{32,36}... | collective-permute-start | bytes 393224 | tf_op jit(solution)/shard_map/ppermute | solution.py:539
  106.3 20.1 %step3.1 = (f32[16,3456]{1,0:T(8,128)S(1)}, f32[16,3456]{1,0:T(8,128)S(1)}, f32[16,3456]{1,0:T(8,128)S(1)}, f32[16,3456]{1,0:T(8,128)S(1)}) custom-call(f32[16,13824]{1,0:T(8,128)S(1)} %get-tuple-element.48.refs_0_, f32[16,2048]{1,0:T(8,128)S(1)} %collective-permute-done.6.refs_1_, f32[16,2048]{1,0:T(8,128)S(1)} %collective-permute-done.7.refs_2_, ...), custom_call_target="tpu_custom_call" | custom-call | tf_op jit(solution)/shard_map/step3/pallas_call | solution.py:445
  126.4 2.0 %collective-permute-start.8 = (f32[16,3456]{1,0:T(8,128)S(1)}, f32[16,3456]{1,0:T(8,128)S(1)}, u32[]{:S(2)}, u32[]{:S(2)}) collective-permute-start(f32[16,3456]{1,0:T(8,128)S(1)} %get-tuple-element.52), channel_id=1, source_target_pairs={{0,1},{1,2},{2,3},{3,0},{4,5},{5,6},{6,7},{7,4},{8,9},{9,10},{10,1... | collective-permute-start | bytes 663560 | tf_op jit(solution)/shard_map/ppermute | solution.py:539
  128.4 3.6 %collective-permute-start.9 = (f32[16,3456]{1,0:T(8,128)S(1)}, f32[16,3456]{1,0:T(8,128)S(1)}, u32[]{:S(2)}, u32[]{:S(2)}) collective-permute-start(f32[16,3456]{1,0:T(8,128)S(1)} %get-tuple-element.53), channel_id=1, source_target_pairs={{0,2},{1,3},{2,0},{3,1},{4,6},{5,7},{6,4},{7,5},{8,10},{9,11},{10,... | collective-permute-start | bytes 663560 | tf_op jit(solution)/shard_map/ppermute | solution.py:539
  134.4 3.9 %collective-permute-done.9.q2_ref = f32[16,3456]{1,0:T(8,128)S(1)} collective-permute-done((f32[16,3456]{1,0:T(8,128)S(1)}, f32[16,3456]{1,0:T(8,128)S(1)}, u32[]{:S(2)}, u32[]{:S(2)}) %collective-permute-start.9) | collective-permute-done | bytes 221216 | tf_op jit(solution)/shard_map/ppermute | solution.py:539
  139.2 4.9 %collective-permute-start.11 = (f32[64,64]{1,0:T(8,128)S(1)}, f32[64,64]{1,0:T(8,128)S(1)}, u32[]{:S(2)}, u32[]{:S(2)}) collective-permute-start(f32[64,64]{1,0:T(8,128)S(1)} %get-tuple-element.55), channel_id=1, source_target_pairs={{0,4},{4,0},{8,12},{12,8},{16,20},{20,16},{24,28},{28,24},{32,36},... | collective-permute-start | bytes 49160 | tf_op jit(solution)/shard_map/ppermute | solution.py:544
  145.0 11.7 %collective-permute-start.14 = (f32[64,64]{1,0:T(8,128)S(1)}, f32[64,64]{1,0:T(8,128)S(1)}, u32[]{:S(2)}, u32[]{:S(2)}) collective-permute-start(f32[64,64]{1,0:T(8,128)S(1)} %add.42), channel_id=1, source_target_pairs={{0,24},{4,28},{8,16},{12,20},{16,8},{20,12},{24,0},{28,4},{32,56},... | collective-permute-start | bytes 49160 | tf_op jit(solution)/shard_map/ppermute | solution.py:544
  158.6 3.5 %collective-permute-done.13 = f32[64,64]{1,0:T(8,128)S(1)} collective-permute-done((f32[64,64]{1,0:T(8,128)S(1)}, f32[64,64]{1,0:T(8,128)S(1)}, u32[]{:S(2)}, u32[]{:S(2)}) %collective-permute-start.13) | collective-permute-done | bytes 16416 | tf_op jit(solution)/shard_map/ppermute | solution.py:544
  163.5 2.1 %collective-permute-start.16 = (f32[64,64]{1,0:T(8,128)S(1)}, f32[64,64]{1,0:T(8,128)S(1)}, u32[]{:S(2)}, u32[]{:S(2)}) collective-permute-start(f32[64,64]{1,0:T(8,128)S(1)} %add_add_fusion.2), channel_id=1, source_target_pairs={{0,64},{4,68},{8,72},{12,76},{16,80},{20,84},{24,88},{28,92},{32,9... | collective-permute-start | bytes 49160 | tf_op jit(solution)/shard_map/ppermute | solution.py:544
  169.5 2.2 %collective-permute-start.20 = (f32[64,64]{1,0:T(8,128)S(1)}, f32[64,64]{1,0:T(8,128)S(1)}, u32[]{:S(2)}, u32[]{:S(2)}) collective-permute-start(f32[64,64]{1,0:T(8,128)S(1)} %add_add_fusion.1), channel_id=1, source_target_pairs={{0,3},{1,2},{2,1},{3,0},{4,7},{5,6},{6,5},{7,4},{8,11},{9,10},{10,... | collective-permute-start | bytes 49160 | tf_op jit(solution)/shard_map/ppermute | solution.py:544
  174.7 2.5 %collective-permute-done.19 = f32[64,64]{1,0:T(8,128)S(1)} collective-permute-done((f32[64,64]{1,0:T(8,128)S(1)}, f32[64,64]{1,0:T(8,128)S(1)}, u32[]{:S(2)}, u32[]{:S(2)}) %collective-permute-start.19) | collective-permute-done | bytes 16416 | tf_op jit(solution)/shard_map/ppermute | solution.py:544
  177.2 6.3 %basis.1 = (f32[16,3456]{1,0:T(8,128)S(1)}, f32[16,3456]{1,0:T(8,128)S(1)}, f32[16,3456]{1,0:T(8,128)S(1)}, f32[16,3456]{1,0:T(8,128)S(1)}) custom-call(f32[64,64]{1,0:T(8,128)S(1)} %add_add_fusion.gram_ref, f32[64,3456]{1,0:T(8,128)S(1)} %get-tuple-element.56.all_ref, s32[1]{0:T(128)} %bitcast.5.refs_15_.me_ref), custom_call_target="tpu_custom_call" | custom-call | tf_op jit(solution)/shard_map/basis/pallas_call | solution.py:507
  184.0 2.2 %collective-permute-start.22 = (f32[16,3456]{1,0:T(8,128)S(1)}, f32[16,3456]{1,0:T(8,128)S(1)}, u32[]{:S(2)}, u32[]{:S(2)}) collective-permute-start(f32[16,3456]{1,0:T(8,128)S(1)} %get-tuple-element.59), channel_id=1, source_target_pairs={{0,2},{1,3},{2,0},{3,1},{4,6},{5,7},{6,4},{7,5},{8,10},{9,11},{10,... | collective-permute-start | bytes 663560 | tf_op jit(solution)/shard_map/ppermute | solution.py:539
  186.2 2.0 %collective-permute-start.23 = (f32[16,3456]{1,0:T(8,128)S(1)}, f32[16,3456]{1,0:T(8,128)S(1)}, u32[]{:S(2)}, u32[]{:S(2)}) collective-permute-start(f32[16,3456]{1,0:T(8,128)S(1)} %get-tuple-element.60), channel_id=1, source_target_pairs={{0,3},{1,0},{2,1},{3,2},{4,7},{5,4},{6,5},{7,6},{8,11},{9,8},{10,9... | collective-permute-start | bytes 663560 | tf_op jit(solution)/shard_map/ppermute | solution.py:539
  188.2 5.0 %collective-permute-done.21.q1_ref = f32[16,3456]{1,0:T(8,128)S(1)} collective-permute-done((f32[16,3456]{1,0:T(8,128)S(1)}, f32[16,3456]{1,0:T(8,128)S(1)}, u32[]{:S(2)}, u32[]{:S(2)}) %collective-permute-start.21) | collective-permute-done | bytes 221216 | tf_op jit(solution)/shard_map/ppermute | solution.py:539
  (69 shorter events, 36.0 us)
Async XLA Ops:
  3.3 29.6 %collective-permute-start.3 = (f32[64,896]{1,0:T(8,128)S(1)}, f32[64,896]{1,0:T(8,128)}, u32[]{:S(2)}, u32[]{:S(2)}) collective-permute-start(f32[64,896]{1,0:T(8,128)S(1)} %concatenate.7.own_ref), channel_id=1, source_target_pairs={{4,0},{8,4},{12,8},{16,12},{20,16},{24,20},{28,24},{32,28},{36,32}... | collective-permute-start | bytes 688136 | tf_op jit(solution)/shard_map/ppermute | solution.py:539
  4.6 28.4 %collective-permute-start.2 = (f32[64,896]{1,0:T(8,128)S(1)}, f32[64,896]{1,0:T(8,128)}, u32[]{:S(2)}, u32[]{:S(2)}) collective-permute-start(f32[64,896]{1,0:T(8,128)S(1)} %concatenate.7.own_ref), channel_id=1, source_target_pairs={{0,4},{4,8},{8,12},{12,16},{16,20},{20,24},{24,28},{28,32},{32,36}... | collective-permute-start | bytes 688136 | tf_op jit(solution)/shard_map/ppermute | solution.py:539
  25.4 15.8 %collective-permute-start = (f32[16,2048]{1,0:T(8,128)}, f32[16,2048]{1,0:T(8,128)}, u32[]{:S(2)}, u32[]{:S(2)}) collective-permute-start(f32[16,2048]{1,0:T(8,128)} %get-tuple-element.34), channel_id=1, source_target_pairs={{0,4},{4,8},{8,12},{12,16},{16,20},{20,24},{24,28},{28,32},{32,36}... | collective-permute-start | bytes 393224 | tf_op jit(solution)/shard_map/ppermute | solution.py:539
  28.5 12.7 %collective-permute-start.1 = (f32[16,2048]{1,0:T(8,128)}, f32[16,2048]{1,0:T(8,128)}, u32[]{:S(2)}, u32[]{:S(2)}) collective-permute-start(f32[16,2048]{1,0:T(8,128)} %get-tuple-element.35), channel_id=1, source_target_pairs={{4,0},{8,4},{12,8},{16,12},{20,16},{24,20},{28,24},{32,28},{36,32}... | collective-permute-start | bytes 393224 | tf_op jit(solution)/shard_map/ppermute | solution.py:539
  64.5 8.5 %collective-permute-start.4 = (f32[16,2048]{1,0:T(8,128)S(1)}, f32[16,2048]{1,0:T(8,128)S(1)}, u32[]{:S(2)}, u32[]{:S(2)}) collective-permute-start(f32[16,2048]{1,0:T(8,128)S(1)} %get-tuple-element.46), channel_id=1, source_target_pairs={{0,4},{4,8},{8,12},{12,16},{16,20},{20,24},{24,28},{28,32},{32,36}... | collective-permute-start | bytes 393224 | tf_op jit(solution)/shard_map/ppermute | solution.py:539
  71.6 3.2 %collective-permute-start.5 = (f32[16,2048]{1,0:T(8,128)S(1)}, f32[16,2048]{1,0:T(8,128)S(1)}, u32[]{:S(2)}, u32[]{:S(2)}) collective-permute-start(f32[16,2048]{1,0:T(8,128)S(1)} %get-tuple-element.47), channel_id=1, source_target_pairs={{4,0},{8,4},{12,8},{16,12},{20,16},{24,20},{28,24},{32,28},{36,32}... | collective-permute-start | bytes 393224 | tf_op jit(solution)/shard_map/ppermute | solution.py:539
  95.1 9.3 %collective-permute-start.6 = (f32[16,2048]{1,0:T(8,128)S(1)}, f32[16,2048]{1,0:T(8,128)S(1)}, u32[]{:S(2)}, u32[]{:S(2)}) collective-permute-start(f32[16,2048]{1,0:T(8,128)S(1)} %get-tuple-element.49), channel_id=1, source_target_pairs={{0,4},{4,8},{8,12},{12,16},{16,20},{20,24},{24,28},{28,32},{32,36}... | collective-permute-start | bytes 393224 | tf_op jit(solution)/shard_map/ppermute | solution.py:539
  103.1 3.2 %collective-permute-start.7 = (f32[16,2048]{1,0:T(8,128)S(1)}, f32[16,2048]{1,0:T(8,128)S(1)}, u32[]{:S(2)}, u32[]{:S(2)}) collective-permute-start(f32[16,2048]{1,0:T(8,128)S(1)} %get-tuple-element.50), channel_id=1, source_target_pairs={{4,0},{8,4},{12,8},{16,12},{20,16},{24,20},{28,24},{32,28},{36,32}... | collective-permute-start | bytes 393224 | tf_op jit(solution)/shard_map/ppermute | solution.py:539
  126.4 8.0 %collective-permute-start.8 = (f32[16,3456]{1,0:T(8,128)S(1)}, f32[16,3456]{1,0:T(8,128)S(1)}, u32[]{:S(2)}, u32[]{:S(2)}) collective-permute-start(f32[16,3456]{1,0:T(8,128)S(1)} %get-tuple-element.52), channel_id=1, source_target_pairs={{0,1},{1,2},{2,3},{3,0},{4,5},{5,6},{6,7},{7,4},{8,9},{9,10},{10,1... | collective-permute-start | bytes 663560 | tf_op jit(solution)/shard_map/ppermute | solution.py:539
  128.4 9.9 %collective-permute-start.9 = (f32[16,3456]{1,0:T(8,128)S(1)}, f32[16,3456]{1,0:T(8,128)S(1)}, u32[]{:S(2)}, u32[]{:S(2)}) collective-permute-start(f32[16,3456]{1,0:T(8,128)S(1)} %get-tuple-element.53), channel_id=1, source_target_pairs={{0,2},{1,3},{2,0},{3,1},{4,6},{5,7},{6,4},{7,5},{8,10},{9,11},{10,... | collective-permute-start | bytes 663560 | tf_op jit(solution)/shard_map/ppermute | solution.py:539
  132.0 6.4 %collective-permute-start.10 = (f32[16,3456]{1,0:T(8,128)S(1)}, f32[16,3456]{1,0:T(8,128)S(1)}, u32[]{:S(2)}, u32[]{:S(2)}) collective-permute-start(f32[16,3456]{1,0:T(8,128)S(1)} %get-tuple-element.54), channel_id=1, source_target_pairs={{0,3},{1,0},{2,1},{3,2},{4,7},{5,4},{6,5},{7,6},{8,11},{9,8},{10,9... | collective-permute-start | bytes 663560 | tf_op jit(solution)/shard_map/ppermute | solution.py:539
  139.2 5.8 %collective-permute-start.11 = (f32[64,64]{1,0:T(8,128)S(1)}, f32[64,64]{1,0:T(8,128)S(1)}, u32[]{:S(2)}, u32[]{:S(2)}) collective-permute-start(f32[64,64]{1,0:T(8,128)S(1)} %get-tuple-element.55), channel_id=1, source_target_pairs={{0,4},{4,0},{8,12},{12,8},{16,20},{20,16},{24,28},{28,24},{32,36},... | collective-permute-start | bytes 49160 | tf_op jit(solution)/shard_map/ppermute | solution.py:544
  145.0 13.6 %collective-permute-start.14 = (f32[64,64]{1,0:T(8,128)S(1)}, f32[64,64]{1,0:T(8,128)S(1)}, u32[]{:S(2)}, u32[]{:S(2)}) collective-permute-start(f32[64,64]{1,0:T(8,128)S(1)} %add.42), channel_id=1, source_target_pairs={{0,24},{4,28},{8,16},{12,20},{16,8},{20,12},{24,0},{28,4},{32,56},... | collective-permute-start | bytes 49160 | tf_op jit(solution)/shard_map/ppermute | solution.py:544
  156.7 5.4 %collective-permute-start.13 = (f32[64,64]{1,0:T(8,128)S(1)}, f32[64,64]{1,0:T(8,128)S(1)}, u32[]{:S(2)}, u32[]{:S(2)}) collective-permute-start(f32[64,64]{1,0:T(8,128)S(1)} %add.42), channel_id=1, source_target_pairs={{0,16},{4,20},{8,24},{12,28},{16,0},{20,4},{24,8},{28,12},{32,48},... | collective-permute-start | bytes 49160 | tf_op jit(solution)/shard_map/ppermute | solution.py:544
  156.7 5.4 %collective-permute-start.12 = (f32[64,64]{1,0:T(8,128)S(1)}, f32[64,64]{1,0:T(8,128)S(1)}, u32[]{:S(2)}, u32[]{:S(2)}) collective-permute-start(f32[64,64]{1,0:T(8,128)S(1)} %add.42), channel_id=1, source_target_pairs={{0,8},{4,12},{8,0},{12,4},{16,24},{20,28},{24,16},{28,20},{32,40},... | collective-permute-start | bytes 49160 | tf_op jit(solution)/shard_map/ppermute | solution.py:544
  162.1 5.2 %collective-permute-start.17 = (f32[64,64]{1,0:T(8,128)S(1)}, f32[64,64]{1,0:T(8,128)S(1)}, u32[]{:S(2)}, u32[]{:S(2)}) collective-permute-start(f32[64,64]{1,0:T(8,128)S(1)} %add_add_fusion.2), channel_id=1, source_target_pairs={{0,96},{4,100},{8,104},{12,108},{16,112},{20,116},{24,120},{28,124... | collective-permute-start | bytes 49160 | tf_op jit(solution)/shard_map/ppermute | solution.py:544
  163.5 5.7 %collective-permute-start.16 = (f32[64,64]{1,0:T(8,128)S(1)}, f32[64,64]{1,0:T(8,128)S(1)}, u32[]{:S(2)}, u32[]{:S(2)}) collective-permute-start(f32[64,64]{1,0:T(8,128)S(1)} %add_add_fusion.2), channel_id=1, source_target_pairs={{0,64},{4,68},{8,72},{12,76},{16,80},{20,84},{24,88},{28,92},{32,9... | collective-permute-start | bytes 49160 | tf_op jit(solution)/shard_map/ppermute | solution.py:544
  165.6 3.9 %collective-permute-start.15 = (f32[64,64]{1,0:T(8,128)S(1)}, f32[64,64]{1,0:T(8,128)S(1)}, u32[]{:S(2)}, u32[]{:S(2)}) collective-permute-start(f32[64,64]{1,0:T(8,128)S(1)} %add_add_fusion.2), channel_id=1, source_target_pairs={{0,32},{4,36},{8,40},{12,44},{16,48},{20,52},{24,56},{28,60},{32,0... | collective-permute-start | bytes 49160 | tf_op jit(solution)/shard_map/ppermute | solution.py:544
  169.5 5.2 %collective-permute-start.20 = (f32[64,64]{1,0:T(8,128)S(1)}, f32[64,64]{1,0:T(8,128)S(1)}, u32[]{:S(2)}, u32[]{:S(2)}) collective-permute-start(f32[64,64]{1,0:T(8,128)S(1)} %add_add_fusion.1), channel_id=1, source_target_pairs={{0,3},{1,2},{2,1},{3,0},{4,7},{5,6},{6,5},{7,4},{8,11},{9,10},{10,... | collective-permute-start | bytes 49160 | tf_op jit(solution)/shard_map/ppermute | solution.py:544
  171.8 5.4 %collective-permute-start.19 = (f32[64,64]{1,0:T(8,128)S(1)}, f32[64,64]{1,0:T(8,128)S(1)}, u32[]{:S(2)}, u32[]{:S(2)}) collective-permute-start(f32[64,64]{1,0:T(8,128)S(1)} %add_add_fusion.1), channel_id=1, source_target_pairs={{0,2},{1,3},{2,0},{3,1},{4,6},{5,7},{6,4},{7,5},{8,10},{9,11},{10,... | collective-permute-start | bytes 49160 | tf_op jit(solution)/shard_map/ppermute | solution.py:544
  172.9 4.3 %collective-permute-start.18 = (f32[64,64]{1,0:T(8,128)S(1)}, f32[64,64]{1,0:T(8,128)S(1)}, u32[]{:S(2)}, u32[]{:S(2)}) collective-permute-start(f32[64,64]{1,0:T(8,128)S(1)} %add_add_fusion.1), channel_id=1, source_target_pairs={{0,1},{1,0},{2,3},{3,2},{4,5},{5,4},{6,7},{7,6},{8,9},{9,8},{10,11... | collective-permute-start | bytes 49160 | tf_op jit(solution)/shard_map/ppermute | solution.py:544
  183.5 9.7 %collective-permute-start.21 = (f32[16,3456]{1,0:T(8,128)S(1)}, f32[16,3456]{1,0:T(8,128)S(1)}, u32[]{:S(2)}, u32[]{:S(2)}) collective-permute-start(f32[16,3456]{1,0:T(8,128)S(1)} %get-tuple-element.58), channel_id=1, source_target_pairs={{0,1},{1,2},{2,3},{3,0},{4,5},{5,6},{6,7},{7,4},{8,9},{9,10},{10,1... | collective-permute-start | bytes 663560 | tf_op jit(solution)/shard_map/ppermute | solution.py:539
  184.0 9.2 %collective-permute-start.22 = (f32[16,3456]{1,0:T(8,128)S(1)}, f32[16,3456]{1,0:T(8,128)S(1)}, u32[]{:S(2)}, u32[]{:S(2)}) collective-permute-start(f32[16,3456]{1,0:T(8,128)S(1)} %get-tuple-element.59), channel_id=1, source_target_pairs={{0,2},{1,3},{2,0},{3,1},{4,6},{5,7},{6,4},{7,5},{8,10},{9,11},{10,... | collective-permute-start | bytes 663560 | tf_op jit(solution)/shard_map/ppermute | solution.py:539
  186.2 7.7 %collective-permute-start.23 = (f32[16,3456]{1,0:T(8,128)S(1)}, f32[16,3456]{1,0:T(8,128)S(1)}, u32[]{:S(2)}, u32[]{:S(2)}) collective-permute-start(f32[16,3456]{1,0:T(8,128)S(1)} %get-tuple-element.60), channel_id=1, source_target_pairs={{0,3},{1,0},{2,1},{3,2},{4,7},{5,4},{6,5},{7,6},{8,11},{9,8},{10,9... | collective-permute-start | bytes 663560 | tf_op jit(solution)/shard_map/ppermute | solution.py:539
  (9 other events, 6.4 us)

commit v2 on v1

v2 whole, which is shorter than its diff:
```python
import functools
import jax
import jax.numpy as jnp
from jax import lax
from jax.experimental import pallas as pl
from jax.experimental.pallas import tpu as pltpu
from jax.sharding import PartitionSpec as P

RIM = 2048
NODES = 343
HANG = 864
MASTERS = 4
LOC = 13824
CELLS = 64
S = 16
L = 128
EXT = LOC + 2 * RIM
NB = LOC // L
RB = RIM // L
NPAD = 384
NJ = NPAD // L
WIDE = 7
NARROW = 3
PACK = 352
GROUP = 16
SLOTS = 14 * GROUP
HPAD = 896
HB = HPAD // L
ME = MASTERS * HPAD
HE = 1024
E = ME + HE
QLO = 512
QB = QLO // L
QHI = 9
BIG = 1 << 20
CENTRE = 4.5
HALF = 3.5
F32 = jnp.float32
BF16 = jnp.bfloat16
I32 = jnp.int32
VLIM = 40 * 1024 * 1024

VM = pl.BlockSpec(memory_space=pltpu.VMEM)
SM = pl.BlockSpec(memory_space=pltpu.SMEM)
NT = (((1,), (1,)), ((), ()))


def iota(shape, dim):
    return lax.broadcasted_iota(I32, shape, dim)


def lanes(x, idx):
    return jnp.take_along_axis(x, idx, axis=1, mode="promise_in_bounds")


def nn(a, b):
    return jnp.dot(a, b, preferred_element_type=F32)


def nt(a, b):
    return lax.dot_general(a, b, NT, preferred_element_type=F32)


def split(x):
    hi = x.astype(BF16)
    return hi, (x - hi.astype(F32)).astype(BF16)


def at(b):
    return pl.ds(pl.multiple_of(b * L, L), L)


def one_hot(row, n):
    return (jnp.broadcast_to(row, (n, row.shape[1])) == iota((n, row.shape[1]), 0)).astype(F32)


def hang_tables(ent_ref, a_ref, b_ref, lhs_ref, oh_ref, pe_ref, src_ref, posr_ref, hq_ref, start_ref):
    for i in range(E // L):
        col = slice(i * L, (i + 1) * L)
        row = ent_ref[0:1, col]
        a_ref[:, col] = one_hot(row >> 7, L).astype(BF16)
        b_ref[:, col] = one_hot(row & 127, L).astype(BF16)
    flag = nt(a_ref[...], b_ref[...]) > 0.5
    flagb = flag.astype(F32).astype(BF16)
    tri = (iota((L, L), 0) < iota((L, L), 1)).astype(F32).astype(BF16)
    low = (iota((L, L), 1) < iota((L, L), 0)).astype(F32).astype(BF16)
    total = nn(flagb, jnp.ones((L, L), BF16))
    pos = (nn(flagb, tri) + nn(low, total.astype(BF16))).astype(I32)
    posr_ref[...] = jnp.where(flag, pos, -1)
    totrow = nt(jnp.ones((8, L), BF16), flagb)
    start_ref[...] = nn(totrow.astype(BF16), tri).astype(I32)
    ph = (pos >> 7).astype(F32).astype(BF16)
    plo = (pos & 127).astype(F32).astype(BF16)
    for i in range(E // L):
        col = slice(i * L, (i + 1) * L)
        ent = ent_ref[0:1, col]
        mask = a_ref[:, col].astype(F32)
        b = b_ref[:, col]
        hi = jnp.sum(nn(ph, b) * mask, axis=0, keepdims=True)
        lo = jnp.sum(nn(plo, b) * mask, axis=0, keepdims=True)
        pe = jnp.where(ent >= 0, hi.astype(I32) * L + lo.astype(I32), BIG)
        pe_ref[0:1, col] = pe
        oh_ref[:, col] = one_hot(pe & (QLO - 1), QLO).astype(BF16)
        qm = one_hot(pe // QLO, 16)
        lhs_ref[0:16, col] = qm.astype(BF16)
        lhs_ref[16:32, col] = (qm * (ent >> 7).astype(F32)).astype(BF16)
        lhs_ref[32:48, col] = (qm * (ent & 127).astype(F32)).astype(BF16)
        lhs_ref[48:64, col] = (qm if i >= ME // L else jnp.zeros_like(qm)).astype(BF16)
    res = nt(lhs_ref[...], oh_ref[...])
    cnt = res[0:16]
    den = jnp.maximum(cnt, 1.0)
    blk = (res[16:32] / den + 0.5).astype(I32)
    lo = (res[32:48] / den + 0.5).astype(I32)
    src = jnp.where(cnt > 0.5, blk * L + lo, -1)
    for q in range(QHI):
        for t in range(QB):
            src_ref[QB * q + t : QB * q + t + 1, :] = src[q : q + 1, t * L : (t + 1) * L]
    hq_ref[...] = res[48:64]


def zat(c):
    return pl.ds(pl.multiple_of((c // QB) * S, S), S), pl.ds(pl.multiple_of((c % QB) * L, L), L)


UNROLL = 12


def compress(read, z_ref, src_ref, start_ref):
    z_ref[...] = jnp.zeros_like(z_ref)

    def step(i, cur):
        for k in range(UNROLL):
            b = i * UNROLL + k
            y = read(b)
            c = start_ref[0, b] >> 7
            ahead = start_ref[0, b + 1] >> 7
            parts = []
            for t in range(2):
                row = jnp.broadcast_to(src_ref[pl.ds(c + t, 1), :], (S, L))
                parts.append(((row >> 7) == b, lanes(y, row & 127)))
            cur = jnp.where(parts[0][0], parts[0][1], cur)
            r, l = zat(c)
            z_ref[r, l] = cur
            after = jnp.where(parts[1][0], parts[1][1], 0.0)
            cur = jnp.where(ahead > c, after, cur)
        return cur

    cur = lax.fori_loop(0, NB // UNROLL, step, jnp.zeros((S, L), F32))
    r, l = zat(start_ref[0, NB] >> 7)
    z_ref[r, l] = cur


def expand(b, y, z_ref, posr_ref, start_ref):
    row = jnp.broadcast_to(posr_ref[pl.ds(b, 1), :], (S, L))
    c0 = start_ref[0, b] >> 7
    for t in range(2):
        c = c0 + t
        r, l = zat(c)
        y = jnp.where((row >> 7) == c, lanes(z_ref[r, l], row & 127), y)
    return y


def gather_entries(z_ref, oh_ref, pe_ref, g_ref, first, last):
    zz = jnp.concatenate(split(z_ref[...]), axis=0)
    n = QHI * S
    w = 256
    for i in range(first // w, last // w):
        col = slice(i * w, (i + 1) * w)
        g = nn(zz, oh_ref[:, col])
        q = jnp.broadcast_to(pe_ref[0:1, col] // QLO, (S, w))
        hi = g[0:S]
        lo = g[n : n + S]
        for h in range(1, QHI):
            m = q == h
            hi = jnp.where(m, g[h * S : (h + 1) * S], hi)
            lo = jnp.where(m, g[n + h * S : n + (h + 1) * S], lo)
        g_ref[:, col] = hi + lo


def scatter_entries(g_ref, oh_ref, pe_ref, lhs_ref, first, last):
    n = QHI * S
    for i in range(first // L, last // L):
        col = slice(i * L, (i + 1) * L)
        g = g_ref[:, col]
        hi = g.astype(BF16).astype(F32)
        lo = g - hi
        q = jnp.broadcast_to(pe_ref[0:1, col] // QLO, (S, L))
        for h in range(QHI):
            m = q == h
            lhs_ref[h * S : (h + 1) * S, col] = jnp.where(m, hi, 0.0).astype(BF16)
            lhs_ref[n + h * S : n + (h + 1) * S, col] = jnp.where(m, lo, 0.0).astype(BF16)
    res = nt(lhs_ref[:, first:last], oh_ref[:, first:last])
    return res[:n] + res[n:]


def hanging_values(z_ref, oh_ref, pe_ref, w_ref, g_ref, lhs_ref, hq_ref):
    gather_entries(z_ref, oh_ref, pe_ref, g_ref, 0, ME)
    g_ref[:, ME + HPAD :] = jnp.zeros((S, HE - HPAD), F32)
    for j in range(HB):
        acc = jnp.zeros((S, L), F32)
        for k in range(MASTERS):
            col = slice(k * HPAD + j * L, k * HPAD + (j + 1) * L)
            acc = acc + g_ref[:, col] * w_ref[0:1, col]
        g_ref[:, ME + j * L : ME + (j + 1) * L] = acc
    cz = scatter_entries(g_ref, oh_ref, pe_ref, lhs_ref, ME, E)
    for h in range(QHI):
        r = slice(h * S, (h + 1) * S)
        m = jnp.broadcast_to(hq_ref[h : h + 1, :], (S, QLO)) > 0.5
        z_ref[r, :] = jnp.where(m, cz[r], z_ref[r, :])


def add_to_masters(z_ref, oh_ref, pe_ref, w_ref, g_ref, lhs_ref):
    gather_entries(z_ref, oh_ref, pe_ref, g_ref, ME, E)
    for j in range(HB):
        y = g_ref[:, ME + j * L : ME + (j + 1) * L]
        for k in range(MASTERS):
            col = slice(k * HPAD + j * L, k * HPAD + (j + 1) * L)
            g_ref[:, col] = y * w_ref[0:1, col]
    z_ref[...] += scatter_entries(g_ref, oh_ref, pe_ref, lhs_ref, 0, ME)


def prepare_kernel(
    rows_ref, masters_ref, weights_ref, block_ref,
    oh_ref, pe_ref, w_ref, src_ref, posr_ref, hq_ref, start_ref, u_ref, left_ref, right_ref,
    ent_ref, a_ref, b_ref, tab_ref, z_ref, g_ref, lhs_ref, start_s, sem,
):
    ent_ref[...] = jnp.full((1, E), -1, I32)
    w_ref[...] = jnp.zeros((1, ME), F32)
    for k in range(MASTERS):
        col = slice(k * HPAD, k * HPAD + HANG)
        ent_ref[0:1, col] = masters_ref[k : k + 1, :]
        w_ref[0:1, col] = weights_ref[k : k + 1, :]
    ent_ref[0:1, ME : ME + HANG] = rows_ref[...]
    hang_tables(ent_ref, a_ref, b_ref, tab_ref, oh_ref, pe_ref, src_ref, posr_ref, hq_ref, start_ref)
    copy = pltpu.make_async_copy(start_ref, start_s, sem)
    copy.start()
    copy.wait()
    compress(lambda b: block_ref[:, at(b)], z_ref, src_ref, start_s)
    hanging_values(z_ref, oh_ref, pe_ref, w_ref, g_ref, lhs_ref, hq_ref)

    def step(i, _):
        for k in range(UNROLL):
            b = i * UNROLL + k
            u_ref[:, at(b)] = expand(b, block_ref[:, at(b)], z_ref, posr_ref, start_s)
        return 0

    lax.fori_loop(0, NB // UNROLL, step, 0)
    left_ref[...] = u_ref[:, 0:RIM]
    right_ref[...] = u_ref[:, LOC - RIM :]


def sds(shape, dtype=F32):
    return jax.ShapeDtypeStruct(shape, dtype)


HANG_SCRATCH = [
    pltpu.VMEM((QHI * S, QLO), F32),
    pltpu.VMEM((S, E), F32),
    pltpu.VMEM((2 * QHI * S, E), BF16),
]


def prepare(rows, masters, weights, block):
    return pl.pallas_call(
        prepare_kernel,
        out_shape=(
            sds((QLO, E), BF16),
            sds((1, E), I32),
            sds((1, ME)),
            sds((QB * QHI + 4, L), I32),
            sds((L, L), I32),
            sds((16, QLO)),
            sds((8, L), I32),
            sds((S, LOC)),
            sds((S, RIM)),
            sds((S, RIM)),
        ),
        in_specs=[VM] * 4,
        out_specs=(VM,) * 10,
        scratch_shapes=[
            pltpu.VMEM((1, E), I32),
            pltpu.VMEM((L, E), BF16),
            pltpu.VMEM((L, E), BF16),
            pltpu.VMEM((64, E), BF16),
            *HANG_SCRATCH,
            pltpu.SMEM((8, L), I32),
            pltpu.SemaphoreType.DMA,
        ],
        compiler_params=pltpu.CompilerParams(vmem_limit_bytes=VLIM),
        name="prepare",
    )(rows, masters, weights, block)


def cells_kernel(
    own_ref, left_ref, right_ref, k_ref,
    tab_ref, pot_ref, kh_ref, kl_ref, base_ref,
    in_ref, all_ref, meta_ref, pad_ref, meta_s, list_s, wide_s, sem,
):
    in_ref[PACK:, :] = jnp.zeros((NPAD - PACK, L), F32)
    lane = iota((CELLS, L), 1)
    tail = NODES - 2 * L
    for i, (ref, shift) in enumerate(((own_ref, 0), (left_ref, -LOC), (right_ref, LOC))):
        r = slice(i * CELLS, (i + 1) * CELLS)
        in_ref[0:PACK, :] = ref[...]
        lows, tops = [], []
        for j in range(NJ):
            t = in_ref[j * L : (j + 1) * L, :].T
            dofs = t[0:CELLS] + float(shift)
            real = lane < (L if j < 2 else tail)
            low = jnp.where(real, dofs, float(BIG))
            all_ref[r, j * L : (j + 1) * L] = low
            all_ref[r, NPAD + j * L : NPAD + (j + 1) * L] = t[CELLS:]
            lows.append(jnp.min(low, axis=1, keepdims=True).astype(I32))
            tops.append(jnp.max(jnp.where(real, dofs, -float(BIG)), axis=1, keepdims=True).astype(I32))
        all_ref[r, 2 * NPAD :] = jnp.broadcast_to(t[0:CELLS, tail : tail + 1], (CELLS, L))
        live = t[CELLS:, tail : tail + 1] > 0.5
        low = jnp.minimum(jnp.minimum(lows[0], lows[1]), lows[2])
        top = jnp.maximum(jnp.maximum(tops[0], tops[1]), tops[2])
        used = live & (top >= RIM) & (low < RIM + LOC)
        starts = [jnp.minimum(x >> 7, EXT // L - NARROW) for x in lows]
        narrow = ((tops[0] >> 7) - starts[0] < NARROW) & ((tops[1] >> 7) - starts[1] < NARROW)
        narrow = narrow & ((tops[2] >> 7) - starts[2] < NARROW)
        base = jnp.minimum(low >> 7, EXT // L - WIDE)
        meta = jnp.where(used, jnp.where(narrow, 0, 1), -1)
        for j in range(NJ):
            meta = jnp.where(lane == 1 + j, jnp.where(narrow, starts[j], base), meta)
        meta_ref[r, :] = meta
    copy = pltpu.make_async_copy(meta_ref, meta_s, sem)
    copy.start()
    pad_ref[...] = jnp.zeros_like(pad_ref)
    pad_ref[0:NODES, 0:NODES] = k_ref[...]
    kh_ref[...], kl_ref[...] = split(pad_ref[...])
    copy.wait()

    def scan(c, counts):
        kind = meta_s[c, 0]
        n, m = counts
        list_s[n] = c
        wide_s[m] = c
        return n + jnp.where(kind == 0, 1, 0), m + jnp.where(kind == 1, 1, 0)

    n, m = lax.fori_loop(0, 3 * CELLS, scan, (0, 0), unroll=4)
    gn = (n + GROUP - 1) // GROUP
    gw = (m + GROUP - 1) // GROUP
    first = (gn + 1) * GROUP
    last = first + gw * GROUP

    def blank(i, _):
        list_s[i] = -1
        return 0

    def move(i, _):
        list_s[first + i] = wide_s[i]
        return 0

    lax.fori_loop(n, first, blank, 0)
    lax.fori_loop(0, m, move, 0)
    lax.fori_loop(first + m, last, blank, 0)
    base_ref[4 * SLOTS] = gn
    base_ref[4 * SLOTS + 1] = gw

    def one(slot):
        c = list_s[slot]
        valid = c >= 0
        c = jnp.maximum(c, 0)
        vals = all_ref[pl.ds(c, 1), :]
        for j in range(NJ):
            b = jnp.where(valid, meta_s[c, 1 + j], 0)
            base_ref[4 * slot + j] = b
            rel = vals[:, j * L : (j + 1) * L].astype(I32) - b * L
            rel = jnp.where(valid & (rel < WIDE * L), rel, BIG)
            oh = one_hot(rel & 127, L).astype(BF16)
            m = jnp.broadcast_to(rel >> 7, (8, L)) == iota((8, L), 0)
            node = jnp.where(m, iota((8, L), 1) + 1, 0).astype(F32).astype(BF16)
            tab_ref[slot, 8 + 8 * j : 16 + 8 * j, :] = nt(node, oh).astype(I32) - 1
            tab_ref[slot, j : j + 1, :] = rel
            pot_ref[slot, j : j + 1, :] = vals[:, NPAD + j * L : NPAD + (j + 1) * L]
        pot_ref[slot, 3:4, :] = vals[:, 2 * NPAD :]

    def some(i, _):
        for k in range(8):
            one(i * 8 + k)
        return 0

    lax.fori_loop(0, last // 8, some, 0)


def cell_tables(own, left, right, stiffness):
    return pl.pallas_call(
        cells_kernel,
        out_shape=(
            sds((SLOTS, 32, L), I32),
            sds((SLOTS, 8, L)),
            sds((NPAD, NPAD), BF16),
            sds((NPAD, NPAD), BF16),
            sds((4 * SLOTS + L,), I32),
        ),
        in_specs=[VM] * 4,
        out_specs=(VM, VM, VM, VM, SM),
        scratch_shapes=[
            pltpu.VMEM((NPAD, L), F32),
            pltpu.VMEM((3 * CELLS, 7 * L), F32),
            pltpu.VMEM((3 * CELLS, L), I32),
            pltpu.VMEM((NPAD, NPAD), F32),
            pltpu.SMEM((3 * CELLS, L), I32),
            pltpu.SMEM((SLOTS + GROUP,), I32),
            pltpu.SMEM((3 * CELLS + GROUP,), I32),
            pltpu.SemaphoreType.DMA,
        ],
        compiler_params=pltpu.CompilerParams(vmem_limit_bytes=VLIM),
        name="cell_tables",
    )(own, left, right, stiffness)


def step_kernel(number, *refs):
    (u_ref, gl_ref, gr_ref, prev_ref, tab_ref, pot_ref, kh_ref, kl_ref,
     oh_ref, pe_ref, w_ref, src_ref, posr_ref, hq_ref, base_ref, start_ref, me_ref) = refs[:17]
    outs = refs[17 : 17 + (4 if number == 3 else 3)]
    ext_ref, acc0_ref, acc1_ref, x_ref, p_ref, z_ref, g_ref, lhs_ref = refs[17 + len(outs) :]
    accs = (acc0_ref, acc1_ref)
    ext_ref[:, 0:RIM] = gl_ref[...]
    ext_ref[:, RIM : RIM + LOC] = u_ref[...]
    ext_ref[:, RIM + LOC :] = gr_ref[...]
    for ref in accs:
        ref[...] = jnp.zeros_like(ref)
    gn = base_ref[4 * SLOTS]
    gw = base_ref[4 * SLOTS + 1]

    def load(slot, width):
        for j in range(NJ):
            b = base_ref[4 * slot + j]
            row = jnp.broadcast_to(tab_ref[slot, j : j + 1, :], (8, L))
            lo, hi = row & 127, row >> 7
            for s in range(2):
                r = slice(8 * s, 8 * s + 8)
                acc = lanes(ext_ref[r, at(b)], lo)
                for t in range(1, width):
                    acc = jnp.where(hi == t, lanes(ext_ref[r, at(b + t)], lo), acc)
                x_ref[pl.ds(pl.multiple_of(slot * S + 8 * s, 8), 8), j * L : (j + 1) * L] = acc

    def store(slot, parity, width):
        acc_ref = accs[parity]
        scale = jnp.broadcast_to(pot_ref[slot, 3:4, :], (8, L))
        for j in range(NJ):
            b = base_ref[4 * slot + j]
            col = slice(j * L, (j + 1) * L)
            pot = jnp.broadcast_to(pot_ref[slot, j : j + 1, :], (8, L))
            vals = []
            for s in range(2):
                r = pl.ds(pl.multiple_of(slot * S + 8 * s, 8), 8)
                vals.append(scale * p_ref[r, col] + pot * x_ref[r, col])
            adds = []
            for t in range(width):
                row = jnp.broadcast_to(tab_ref[slot, 8 + 8 * j + t : 9 + 8 * j + t, :], (8, L))
                m, lo = row >= 0, row & 127
                adds.append([jnp.where(m, lanes(vals[s], lo), 0.0) for s in range(2)])
            olds = [[acc_ref[8 * s : 8 * s + 8, at(b + t)] for s in range(2)] for t in range(width)]
            for t in range(width):
                for s in range(2):
                    acc_ref[8 * s : 8 * s + 8, at(b + t)] = olds[t][s] + adds[t][s]

    def rows_of(i):
        return pl.ds(pl.multiple_of(i * (GROUP * S), GROUP * S), GROUP * S)

    def product(i):
        xh, xl = split(x_ref[rows_of(i), :])
        kh, kl = kh_ref[...], kl_ref[...]
        return nt(xh, kh) + (nt(xl, kh) + nt(xh, kl))

    def load_group(i, width):
        def four(q, _):
            for k in range(4):
                load(i * GROUP + q * 4 + k, width)
            return 0

        lax.fori_loop(0, GROUP // 4, four, 0)

    def store_group(i, width):
        def four(q, _):
            for k in range(4):
                store(i * GROUP + q * 4 + k, k % 2, width)
            return 0

        lax.fori_loop(0, GROUP // 4, four, 0)

    load_group(0, NARROW)

    def pipeline(i, _):
        prod = product(i)
        before = jnp.where(i == 0, gn, i - 1)
        for k in range(GROUP):
            store(before * GROUP + k, k % 2, NARROW)
        p_ref[rows_of(i), :] = prod
        for k in range(GROUP):
            load((i + 1) * GROUP + k, NARROW)
        return 0

    lax.fori_loop(0, gn, pipeline, 0)
    store_group(jnp.maximum(gn - 1, 0), NARROW)

    def wide(i, _):
        load_group(i, WIDE)
        p_ref[rows_of(i), :] = product(i)
        store_group(i, WIDE)
        return 0

    lax.fori_loop(gn + 1, gn + 1 + gw, wide, 0)

    def read(b):
        return acc0_ref[:, at(b + RB)] + acc1_ref[:, at(b + RB)]

    compress(read, z_ref, src_ref, start_ref)
    add_to_masters(z_ref, oh_ref, pe_ref, w_ref, g_ref, lhs_ref)
    hanging_values(z_ref, oh_ref, pe_ref, w_ref, g_ref, lhs_ref, hq_ref)
    new_ref = outs[0] if number < 3 else ext_ref

    def finish(i, _):
        for k in range(UNROLL):
            b = i * UNROLL + k
            t = expand(b, read(b), z_ref, posr_ref, start_ref)
            r = (t - CENTRE * u_ref[:, at(b)]) * ((1.0 if number == 1 else 2.0) / HALF)
            if number > 1:
                r = r - prev_ref[:, at(b)]
            new_ref[:, at(b)] = r
        return 0

    lax.fori_loop(0, NB // UNROLL, finish, 0)
    if number < 3:
        outs[1][...] = new_ref[:, 0:RIM]
        outs[2][...] = new_ref[:, LOC - RIM :]
    else:
        me = me_ref[0]
        q = LOC // 4
        for k in range(4):
            outs[k][...] = new_ref[:, pl.ds(pl.multiple_of(((me + k) & 3) * q, L), q)]


def apply_step(number, u, gl, gr, prev, cell, base, hang, start, me):
    if number == 3:
        shapes = (sds((S, LOC // 4)),) * 4
    else:
        shapes = (sds((S, LOC)), sds((S, RIM)), sds((S, RIM)))
    return pl.pallas_call(
        functools.partial(step_kernel, number),
        out_shape=shapes,
        in_specs=[VM] * 14 + [SM] * 3,
        out_specs=(VM,) * len(shapes),
        scratch_shapes=[
            pltpu.VMEM((S, EXT), F32),
            pltpu.VMEM((S, EXT), F32),
            pltpu.VMEM((S, EXT), F32),
            pltpu.VMEM((SLOTS * S, NPAD), F32),
            pltpu.VMEM((SLOTS * S, NPAD), F32),
            *HANG_SCRATCH,
        ],
        compiler_params=pltpu.CompilerParams(vmem_limit_bytes=VLIM),
        name=f"step{number}",
    )(u, gl, gr, prev, *cell, *hang, base, start, me)


def gram_kernel(q0_ref, q1_ref, q2_ref, q3_ref, me_ref, gram_ref, all_ref):
    me = me_ref[0]
    for k, ref in enumerate((q0_ref, q1_ref, q2_ref, q3_ref)):
        all_ref[pl.ds(pl.multiple_of(((me - k) & 3) * S, S), S), :] = ref[...]
    a = all_ref[...]
    gram_ref[...] = lax.dot_general(a, a, NT, preferred_element_type=F32, precision=lax.Precision.HIGHEST)


def gram_of(qs, me):
    n = qs[0].shape[1]
    return pl.pallas_call(
        gram_kernel,
        out_shape=(sds((4 * S, 4 * S)), sds((4 * S, n))),
        in_specs=[VM] * 4 + [SM],
        out_specs=(VM, VM),
        compiler_params=pltpu.CompilerParams(vmem_limit_bytes=VLIM),
        name="gram",
    )(*qs, me)


def basis_kernel(total, gram_ref, all_ref, me_ref, o0_ref, o1_ref, o2_ref, o3_ref, m_ref, r_ref):
    n = 4 * S
    eye = (iota((n, n), 0) == iota((n, n), 1)).astype(F32)
    m_ref[...] = jnp.concatenate([gram_ref[...], eye], 1)
    row_id = iota((n, 2 * n), 0)

    m = m_ref[...]
    diag = jnp.zeros((n, 1), F32)
    for j in range(n):
        pivot = m[j : j + 1, :]
        d = pivot[:, j : j + 1]
        f = m[:, j : j + 1] / d
        m = m - jnp.where(row_id > j, f, 0.0) * pivot
    dg = jnp.sum(jnp.where(row_id == iota((n, 2 * n), 1), m, 0.0), axis=1, keepdims=True)
    inv = m[:, n:] * lax.rsqrt(dg) * jnp.sqrt(jnp.float32(total))
    r_ref[...] = jnp.dot(inv, all_ref[...], preferred_element_type=F32, precision=lax.Precision.HIGHEST)
    me = me_ref[0]
    for k, ref in enumerate((o0_ref, o1_ref, o2_ref, o3_ref)):
        ref[...] = r_ref[pl.ds(pl.multiple_of(((me + k) & 3) * S, S), S), :]


def basis_of(gram, rows, me, total):
    n = rows.shape[1]
    return pl.pallas_call(
        functools.partial(basis_kernel, total),
        out_shape=(sds((S, n)),) * 4,
        in_specs=[VM, VM, SM],
        out_specs=(VM,) * 4,
        scratch_shapes=[pltpu.VMEM((4 * S, 8 * S), F32), pltpu.VMEM((4 * S, n), F32)],
        compiler_params=pltpu.CompilerParams(vmem_limit_bytes=VLIM),
        name="basis",
    )(gram, rows, me)


def join_kernel(q0_ref, q1_ref, q2_ref, q3_ref, me_ref, out_ref):
    me = me_ref[0]
    n = q0_ref.shape[1]
    for k, ref in enumerate((q0_ref, q1_ref, q2_ref, q3_ref)):
        out_ref[:, pl.ds(pl.multiple_of(((me - k) & 3) * n, L), n)] = ref[...]


def join(qs, me):
    return pl.pallas_call(
        join_kernel,
        out_shape=sds((S, LOC)),
        in_specs=[VM] * 4 + [SM],
        out_specs=VM,
        compiler_params=pltpu.CompilerParams(vmem_limit_bytes=VLIM),
        name="join",
    )(*qs, me)


def shift(x, axis, by, wrap):
    size = lax.axis_size(axis)
    pairs = [(i, (i + by) % size) for i in range(size) if wrap or 0 <= i + by < size]
    return lax.ppermute(x, axis, pairs)


def swap(x, axis, bits):
    size = lax.axis_size(axis)
    return lax.ppermute(x, axis, [(i, i ^ bits) for i in range(size)])


def summed(g):
    g = g + swap(g, "dom", 1)
    for axis, unit in (("dom", 2), ("dom", 8), ("band", 1)):
        others = [swap(g, axis, unit * k) for k in (1, 2, 3)]
        g = (g + others[0]) + (others[1] + others[2])
    return g


def body(
    block,
    stiffness,
    cell_scale,
    potential,
    cell_dofs,
    cell_count,
    hang_rows,
    hang_masters,
    hang_weights,
):
    me = lax.axis_index("band").astype(I32).reshape(1)
    alive = (jnp.arange(CELLS) < cell_count[0]).astype(F32)
    own = jnp.concatenate(
        [
            jnp.concatenate([cell_dofs.astype(F32), potential], axis=1),
            jnp.concatenate([cell_scale, alive])[None],
            jnp.zeros((PACK - NODES - 1, L), F32),
        ],
        axis=0,
    )
    from_left = shift(own, "dom", 1, False)
    from_right = shift(own, "dom", -1, False)
    *hang, start, u0, first, last = prepare(hang_rows[None], hang_masters, hang_weights, block)

    def ghosts(first, last):
        return shift(last, "dom", 1, False), shift(first, "dom", -1, False)

    gl, gr = ghosts(first, last)
    *cell, base = cell_tables(own, from_left, from_right, stiffness)
    args = (cell, base, hang, start, me)
    u1, first, last = apply_step(1, u0, gl, gr, u0, *args)
    gl, gr = ghosts(first, last)
    u2, first, last = apply_step(2, u1, gl, gr, u0, *args)
    gl, gr = ghosts(first, last)
    qs = apply_step(3, u2, gl, gr, u1, *args)
    qs = [qs[0]] + [shift(qs[k], "band", k, True) for k in (1, 2, 3)]
    gram, rows = gram_of(qs, me)
    gram = summed(gram)
    outs = basis_of(gram, rows, me, LOC * lax.axis_size("dom"))
    outs = [outs[0]] + [shift(outs[k], "band", k, True) for k in (1, 2, 3)]
    return join(outs, me)


def solution(mesh):
    return jax.shard_map(
        body,
        mesh=mesh,
        in_specs=(
            P("band", "dom"),
            P(),
            P("dom"),
            P(None, "dom"),
            P(None, "dom"),
            P("dom"),
            P("dom"),
            P(None, "dom"),
            P(None, "dom"),
        ),
        out_specs=P("band", "dom"),
        check_vma=False,
    )
```

time: 198 us -> 171 us (0.86); the launches traced: 195 us -> 170 us
  Pallas kernels: 88.4 us -> 69.1 us
  starting transfers between devices: 64.3 us -> 60 us
  local copies, waits for them, and re-layouts: 13.5 us -> 9.99 us
    pallas_call x3, Pallas kernels: 60.7 us -> 42.4 us  [apply_step(): pl.pallas_call(functools.partial(step_kernel, number), out_shape=shapes,...]
    ppermute x14, starting transfers between devices: 38.4 us -> 34.2 us  [shift(): return lax.ppermute(x, axis, pairs)]
    pad x3 -> x0, local copies, waits for them, and re-layouts: 1.99 us -> none  [the longest x1 1.08 us: body(): kt = jnp.pad(stiffness.T, ((0, NPAD - NODES), (0, NPAD - NODES)))]
    unnamed x23 -> x13, local copies, waits for them, and re-layouts: 9.95 us -> 9.11 us
  transfers between devices with their start and end apart: 24 -> 24, of which waited for: 14 -> 14; matrix products, arithmetic and copies ran while one was open for 3% -> 0% of each run, Pallas kernels for 10% -> 11%
where the time goes in v2:
time: 171 us; the launch traced here: 170 us
  Pallas kernels  69.1 us (40%)
  starting transfers between devices  60 us (35%)
  waiting for transfers between devices  28.4 us (17%)
  local copies, waits for them, and re-layouts  9.99 us (6%)
  other arithmetic  1.84 us (1%)
    pallas_call x3, Pallas kernels, apply_step(): pl.pallas_call(functools.partial(step_kernel, number), out_shape=shapes,...  42.4 us
    ppermute x14, starting transfers between devices, shift(): return lax.ppermute(x, axis, pairs)  34.2 us
    ppermute x10, starting transfers between devices, swap(): return lax.ppermute(x, axis, [(i, i ^ bits) for i in range(size)])  25.8 us
    ppermute x14, waiting for transfers between devices, shift(): return lax.ppermute(x, axis, pairs)  16.1 us
    ppermute x10, waiting for transfers between devices, swap(): return lax.ppermute(x, axis, [(i, i ^ bits) for i in range(size)])  12.3 us
    pallas_call x1, Pallas kernels, prepare(): pl.pallas_call(prepare_kernel, out_shape=(sds((QLO, E), BF16), sds((1, E)...  9.6 us
    unnamed x13, local copies, waits for them, and re-layouts  9.11 us
    pallas_call x1, Pallas kernels, cell_tables(): pl.pallas_call(cells_kernel, out_shape=(sds((SLOTS, 32, L), I32), sds((SL...  8.89 us
  transfers between devices with their start and end apart: 24, of which 14 were waited for; matrix products, arithmetic and copies ran while one was open for 0% of the time, Pallas kernels for 11%

profile of v2, /device:TPU:0, one launch (start us, length us, event | category | flops | bytes accessed | tf_op | source)
XLA Modules:
  0.0 170.2 jit_solution(2389145799151634768)
XLA Ops:
  5.0 3.0 %collective-permute-start.2 = (f32[352,128]{1,0:T(8,128)S(1)}, f32[352,128]{1,0:T(8,128)S(1)}, u32[]{:S(2)}, u32[]{:S(2)}) collective-permute-start(f32[352,128]{1,0:T(8,128)S(1)} %maximum_maximum_fusion.own_ref), channel_id=1, source_target_pairs={{0,4},{4,8},{8,12},{12,16},{16,20},{20,24},{24,28},{28,32},{32,36}... | collective-permute-start | bytes 540680 | tf_op jit(solution)/shard_map/ppermute | solution.py:636
  11.3 9.6 %prepare.1 = (bf16[512,4608]{1,0:T(8,128)(2,1)S(1)}, s32[1,4608]{1,0:T(1,128)S(1)}, f32[1,3584]{1,0:T(1,128)S(1)}, s32[40,128]{1,0:T(8,128)S(1)}, s32[128,128]{1...) custom-call(s32[1,864]{1,0:T(1,128)S(1)} %broadcast_in_dim.9.rows_re, ...), custom_call_target="tpu_custom_call" | custom-call | tf_op jit(solution)/shard_map/prepare/pallas_call | solution.py:264
  20.9 2.1 %copy-done = bf16[512,4608]{1,0:T(8,128)(2,1)} copy-done((bf16[512,4608]{1,0:T(8,128)(2,1)}, bf16[512,4608]{1,0:T(8,128)(2,1)S(1)}, u32[]{:S(2)}) %copy-start) | copy-done | bytes 4718616
  23.1 3.1 %collective-permute-start = (f32[16,2048]{1,0:T(8,128)S(1)}, f32[16,2048]{1,0:T(8,128)S(1)}, u32[]{:S(2)}, u32[]{:S(2)}) collective-permute-start(f32[16,2048]{1,0:T(8,128)S(1)} %get-tuple-element.37), channel_id=1, source_target_pairs={{0,4},{4,8},{8,12},{12,16},{16,20},{20,24},{24,28},{28,32},{32,36}... | collective-permute-start | bytes 393224 | tf_op jit(solution)/shard_map/ppermute | solution.py:636
  28.5 8.9 %cell_tables.1 = (s32[224,32,128]{2,1,0:T(8,128)S(1)}, f32[224,8,128]{2,1,0:T(8,128)S(1)}, bf16[384,384]{1,0:T(8,128)(2,1)S(1)}, bf16[384,384]{1,0:T(8,128)(2,1)S(1)}, s32[1024]{0:T(1024)S(1)}) custom-call(f32[352,128]{1,0:T(8,128)S(1)} %maximum_maximum_fusion.own_ref, f32[352,128]{1,0:T(8,128)S(1)} %collective-permute-done.2.left_ref, ...), custom_call_target="tpu_custom_call" | custom-call | tf_op jit(solution)/shard_map/cell_tables/pallas_call | solution.py:389
  37.5 2.3 %copy-done.1 = bf16[512,4608]{1,0:T(8,128)(2,1)S(1)} copy-done((bf16[512,4608]{1,0:T(8,128)(2,1)S(1)}, bf16[512,4608]{1,0:T(8,128)(2,1)}, u32[]{:S(2)}) %copy-start.1) | copy-done | bytes 4718616
  39.8 14.2 %step1.1 = (f32[16,13824]{1,0:T(8,128)S(1)}, f32[16,2048]{1,0:T(8,128)S(1)}, f32[16,2048]{1,0:T(8,128)S(1)}) custom-call(f32[16,13824]{1,0:T(8,128)S(1)} %get-tuple-element.36.refs_0_.refs_3_, f32[16,2048]{1,0:T(8,128)S(1)} %collective-permute-done.refs_1_, f32[16,2048]{1,0:T(8,128)S(1)} %collective-permute-done.1.refs_2_, ...), custom_call_target="tpu_custom_call" | custom-call | tf_op jit(solution)/shard_map/step1/pallas_call | solution.py:543
  54.0 3.1 %collective-permute-start.4 = (f32[16,2048]{1,0:T(8,128)S(1)}, f32[16,2048]{1,0:T(8,128)S(1)}, u32[]{:S(2)}, u32[]{:S(2)}) collective-permute-start(f32[16,2048]{1,0:T(8,128)S(1)} %get-tuple-element.52), channel_id=1, source_target_pairs={{0,4},{4,8},{8,12},{12,16},{16,20},{20,24},{24,28},{28,32},{32,36}... | collective-permute-start | bytes 393224 | tf_op jit(solution)/shard_map/ppermute | solution.py:636
  58.3 3.2 %collective-permute-done.5.refs_2_ = f32[16,2048]{1,0:T(8,128)S(1)} collective-permute-done((f32[16,2048]{1,0:T(8,128)S(1)}, f32[16,2048]{1,0:T(8,128)S(1)}, u32[]{:S(2)}, u32[]{:S(2)}) %collective-permute-start.5) | collective-permute-done | bytes 131104 | tf_op jit(solution)/shard_map/ppermute | solution.py:636
  61.5 14.0 %step2.1 = (f32[16,13824]{1,0:T(8,128)S(1)}, f32[16,2048]{1,0:T(8,128)S(1)}, f32[16,2048]{1,0:T(8,128)S(1)}) custom-call(f32[16,13824]{1,0:T(8,128)S(1)} %get-tuple-element.51.refs_0_.refs_3_, f32[16,2048]{1,0:T(8,128)S(1)} %collective-permute-done.4.refs_1_, f32[16,2048]{1,0:T(8,128)S(1)} %collective-permute-done.5.refs_2_, ...), custom_call_target="tpu_custom_call" | custom-call | tf_op jit(solution)/shard_map/step2/pallas_call | solution.py:543
  75.5 8.5 %collective-permute-start.6 = (f32[16,2048]{1,0:T(8,128)S(1)}, f32[16,2048]{1,0:T(8,128)S(1)}, u32[]{:S(2)}, u32[]{:S(2)}) collective-permute-start(f32[16,2048]{1,0:T(8,128)S(1)} %get-tuple-element.55), channel_id=1, source_target_pairs={{0,4},{4,8},{8,12},{12,16},{16,20},{20,24},{24,28},{28,32},{32,36}... | collective-permute-start | bytes 393224 | tf_op jit(solution)/shard_map/ppermute | solution.py:636
  87.3 14.3 %step3.1 = (f32[16,3456]{1,0:T(8,128)S(1)}, f32[16,3456]{1,0:T(8,128)S(1)}, f32[16,3456]{1,0:T(8,128)S(1)}, f32[16,3456]{1,0:T(8,128)S(1)}) custom-call(f32[16,13824]{1,0:T(8,128)S(1)} %get-tuple-element.54.refs_0_, f32[16,2048]{1,0:T(8,128)S(1)} %collective-permute-done.6.refs_1_, f32[16,2048]{1,0:T(8,128)S(1)} %collective-permute-done.7.refs_2_, ...), custom_call_target="tpu_custom_call" | custom-call | tf_op jit(solution)/shard_map/step3/pallas_call | solution.py:543
  103.5 3.6 %collective-permute-start.9 = (f32[16,3456]{1,0:T(8,128)S(1)}, f32[16,3456]{1,0:T(8,128)S(1)}, u32[]{:S(2)}, u32[]{:S(2)}) collective-permute-start(f32[16,3456]{1,0:T(8,128)S(1)} %get-tuple-element.59), channel_id=1, source_target_pairs={{0,2},{1,3},{2,0},{3,1},{4,6},{5,7},{6,4},{7,5},{8,10},{9,11},{10,... | collective-permute-start | bytes 663560 | tf_op jit(solution)/shard_map/ppermute | solution.py:636
  109.6 3.8 %collective-permute-done.9.q2_ref = f32[16,3456]{1,0:T(8,128)S(1)} collective-permute-done((f32[16,3456]{1,0:T(8,128)S(1)}, f32[16,3456]{1,0:T(8,128)S(1)}, u32[]{:S(2)}, u32[]{:S(2)}) %collective-permute-start.9) | collective-permute-done | bytes 221216 | tf_op jit(solution)/shard_map/ppermute | solution.py:636
  114.3 6.4 %collective-permute-start.11 = (f32[64,64]{1,0:T(8,128)S(1)}, f32[64,64]{1,0:T(8,128)S(1)}, u32[]{:S(2)}, u32[]{:S(2)}) collective-permute-start(f32[64,64]{1,0:T(8,128)S(1)} %get-tuple-element.61), channel_id=1, source_target_pairs={{0,4},{4,0},{8,12},{12,8},{16,20},{20,16},{24,28},{28,24},{32,36},... | collective-permute-start | bytes 49160 | tf_op jit(solution)/shard_map/ppermute | solution.py:641
  121.6 10.1 %collective-permute-start.14 = (f32[64,64]{1,0:T(8,128)S(1)}, f32[64,64]{1,0:T(8,128)S(1)}, u32[]{:S(2)}, u32[]{:S(2)}) collective-permute-start(f32[64,64]{1,0:T(8,128)S(1)} %add.30), channel_id=1, source_target_pairs={{0,24},{4,28},{8,16},{12,20},{16,8},{20,12},{24,0},{28,4},{32,56},... | collective-permute-start | bytes 49160 | tf_op jit(solution)/shard_map/ppermute | solution.py:641
  133.5 3.5 %collective-permute-done.13 = f32[64,64]{1,0:T(8,128)S(1)} collective-permute-done((f32[64,64]{1,0:T(8,128)S(1)}, f32[64,64]{1,0:T(8,128)S(1)}, u32[]{:S(2)}, u32[]{:S(2)}) %collective-permute-start.13) | collective-permute-done | bytes 16416 | tf_op jit(solution)/shard_map/ppermute | solution.py:641
  137.2 3.7 %collective-permute-start.16 = (f32[64,64]{1,0:T(8,128)S(1)}, f32[64,64]{1,0:T(8,128)S(1)}, u32[]{:S(2)}, u32[]{:S(2)}) collective-permute-start(f32[64,64]{1,0:T(8,128)S(1)} %add_add_fusion.2), channel_id=1, source_target_pairs={{0,64},{4,68},{8,72},{12,76},{16,80},{20,84},{24,88},{28,92},{32,9... | collective-permute-start | bytes 49160 | tf_op jit(solution)/shard_map/ppermute | solution.py:641
  142.8 2.0 %collective-permute-done.15 = f32[64,64]{1,0:T(8,128)S(1)} collective-permute-done((f32[64,64]{1,0:T(8,128)S(1)}, f32[64,64]{1,0:T(8,128)S(1)}, u32[]{:S(2)}, u32[]{:S(2)}) %collective-permute-start.15) | collective-permute-done | bytes 16416 | tf_op jit(solution)/shard_map/ppermute | solution.py:641
  144.8 2.2 %collective-permute-start.20 = (f32[64,64]{1,0:T(8,128)S(1)}, f32[64,64]{1,0:T(8,128)S(1)}, u32[]{:S(2)}, u32[]{:S(2)}) collective-permute-start(f32[64,64]{1,0:T(8,128)S(1)} %add_add_fusion.1), channel_id=1, source_target_pairs={{0,3},{1,2},{2,1},{3,0},{4,7},{5,6},{6,5},{7,4},{8,11},{9,10},{10,... | collective-permute-start | bytes 49160 | tf_op jit(solution)/shard_map/ppermute | solution.py:641
  150.0 2.5 %collective-permute-done.19 = f32[64,64]{1,0:T(8,128)S(1)} collective-permute-done((f32[64,64]{1,0:T(8,128)S(1)}, f32[64,64]{1,0:T(8,128)S(1)}, u32[]{:S(2)}, u32[]{:S(2)}) %collective-permute-start.19) | collective-permute-done | bytes 16416 | tf_op jit(solution)/shard_map/ppermute | solution.py:641
  152.5 6.3 %basis.1 = (f32[16,3456]{1,0:T(8,128)S(1)}, f32[16,3456]{1,0:T(8,128)S(1)}, f32[16,3456]{1,0:T(8,128)S(1)}, f32[16,3456]{1,0:T(8,128)S(1)}) custom-call(f32[64,64]{1,0:T(8,128)S(1)} %add_add_fusion.gram_ref, f32[64,3456]{1,0:T(8,128)S(1)} %get-tuple-element.62.all_ref, s32[1]{0:T(128)} %bitcast.2.refs_16_.me_ref), custom_call_target="tpu_custom_call" | custom-call | tf_op jit(solution)/shard_map/basis/pallas_call | solution.py:604
  159.3 2.5 %collective-permute-start.22 = (f32[16,3456]{1,0:T(8,128)S(1)}, f32[16,3456]{1,0:T(8,128)S(1)}, u32[]{:S(2)}, u32[]{:S(2)}) collective-permute-start(f32[16,3456]{1,0:T(8,128)S(1)} %get-tuple-element.65), channel_id=1, source_target_pairs={{0,2},{1,3},{2,0},{3,1},{4,6},{5,7},{6,4},{7,5},{8,10},{9,11},{10,... | collective-permute-start | bytes 663560 | tf_op jit(solution)/shard_map/ppermute | solution.py:636
  163.5 4.9 %collective-permute-done.21.q1_ref = f32[16,3456]{1,0:T(8,128)S(1)} collective-permute-done((f32[16,3456]{1,0:T(8,128)S(1)}, f32[16,3456]{1,0:T(8,128)S(1)}, u32[]{:S(2)}, u32[]{:S(2)}) %collective-permute-start.21) | collective-permute-done | bytes 221216 | tf_op jit(solution)/shard_map/ppermute | solution.py:636
  (57 shorter events, 31.5 us)
Async XLA Ops:
  3.7 23.8 %collective-permute-start.3 = (f32[352,128]{1,0:T(8,128)S(1)}, f32[352,128]{1,0:T(8,128)S(1)}, u32[]{:S(2)}, u32[]{:S(2)}) collective-permute-start(f32[352,128]{1,0:T(8,128)S(1)} %maximum_maximum_fusion.own_ref), channel_id=1, source_target_pairs={{4,0},{8,4},{12,8},{16,12},{20,16},{24,20},{28,24},{32,28},{36,32}... | collective-permute-start | bytes 540680 | tf_op jit(solution)/shard_map/ppermute | solution.py:636
  5.0 22.5 %collective-permute-start.2 = (f32[352,128]{1,0:T(8,128)S(1)}, f32[352,128]{1,0:T(8,128)S(1)}, u32[]{:S(2)}, u32[]{:S(2)}) collective-permute-start(f32[352,128]{1,0:T(8,128)S(1)} %maximum_maximum_fusion.own_ref), channel_id=1, source_target_pairs={{0,4},{4,8},{8,12},{12,16},{16,20},{20,24},{24,28},{28,32},{32,36}... | collective-permute-start | bytes 540680 | tf_op jit(solution)/shard_map/ppermute | solution.py:636
  23.1 14.4 %collective-permute-start = (f32[16,2048]{1,0:T(8,128)S(1)}, f32[16,2048]{1,0:T(8,128)S(1)}, u32[]{:S(2)}, u32[]{:S(2)}) collective-permute-start(f32[16,2048]{1,0:T(8,128)S(1)} %get-tuple-element.37), channel_id=1, source_target_pairs={{0,4},{4,8},{8,12},{12,16},{16,20},{20,24},{24,28},{28,32},{32,36}... | collective-permute-start | bytes 393224 | tf_op jit(solution)/shard_map/ppermute | solution.py:636
  26.2 11.3 %collective-permute-start.1 = (f32[16,2048]{1,0:T(8,128)S(1)}, f32[16,2048]{1,0:T(8,128)S(1)}, u32[]{:S(2)}, u32[]{:S(2)}) collective-permute-start(f32[16,2048]{1,0:T(8,128)S(1)} %get-tuple-element.38), channel_id=1, source_target_pairs={{4,0},{8,4},{12,8},{16,12},{20,16},{24,20},{28,24},{32,28},{36,32}... | collective-permute-start | bytes 393224 | tf_op jit(solution)/shard_map/ppermute | solution.py:636
  54.0 4.4 %collective-permute-start.4 = (f32[16,2048]{1,0:T(8,128)S(1)}, f32[16,2048]{1,0:T(8,128)S(1)}, u32[]{:S(2)}, u32[]{:S(2)}) collective-permute-start(f32[16,2048]{1,0:T(8,128)S(1)} %get-tuple-element.52), channel_id=1, source_target_pairs={{0,4},{4,8},{8,12},{12,16},{16,20},{20,24},{24,28},{28,32},{32,36}... | collective-permute-start | bytes 393224 | tf_op jit(solution)/shard_map/ppermute | solution.py:636
  57.0 4.5 %collective-permute-start.5 = (f32[16,2048]{1,0:T(8,128)S(1)}, f32[16,2048]{1,0:T(8,128)S(1)}, u32[]{:S(2)}, u32[]{:S(2)}) collective-permute-start(f32[16,2048]{1,0:T(8,128)S(1)} %get-tuple-element.53), channel_id=1, source_target_pairs={{4,0},{8,4},{12,8},{16,12},{20,16},{24,20},{28,24},{32,28},{36,32}... | collective-permute-start | bytes 393224 | tf_op jit(solution)/shard_map/ppermute | solution.py:636
  75.5 9.8 %collective-permute-start.6 = (f32[16,2048]{1,0:T(8,128)S(1)}, f32[16,2048]{1,0:T(8,128)S(1)}, u32[]{:S(2)}, u32[]{:S(2)}) collective-permute-start(f32[16,2048]{1,0:T(8,128)S(1)} %get-tuple-element.55), channel_id=1, source_target_pairs={{0,4},{4,8},{8,12},{12,16},{16,20},{20,24},{24,28},{28,32},{32,36}... | collective-permute-start | bytes 393224 | tf_op jit(solution)/shard_map/ppermute | solution.py:636
  84.0 3.2 %collective-permute-start.7 = (f32[16,2048]{1,0:T(8,128)S(1)}, f32[16,2048]{1,0:T(8,128)S(1)}, u32[]{:S(2)}, u32[]{:S(2)}) collective-permute-start(f32[16,2048]{1,0:T(8,128)S(1)} %get-tuple-element.56), channel_id=1, source_target_pairs={{4,0},{8,4},{12,8},{16,12},{20,16},{24,20},{28,24},{32,28},{36,32}... | collective-permute-start | bytes 393224 | tf_op jit(solution)/shard_map/ppermute | solution.py:636
  101.5 8.0 %collective-permute-start.8 = (f32[16,3456]{1,0:T(8,128)S(1)}, f32[16,3456]{1,0:T(8,128)S(1)}, u32[]{:S(2)}, u32[]{:S(2)}) collective-permute-start(f32[16,3456]{1,0:T(8,128)S(1)} %get-tuple-element.58), channel_id=1, source_target_pairs={{0,1},{1,2},{2,3},{3,0},{4,5},{5,6},{6,7},{7,4},{8,9},{9,10},{10,1... | collective-permute-start | bytes 663560 | tf_op jit(solution)/shard_map/ppermute | solution.py:636
  103.5 9.9 %collective-permute-start.9 = (f32[16,3456]{1,0:T(8,128)S(1)}, f32[16,3456]{1,0:T(8,128)S(1)}, u32[]{:S(2)}, u32[]{:S(2)}) collective-permute-start(f32[16,3456]{1,0:T(8,128)S(1)} %get-tuple-element.59), channel_id=1, source_target_pairs={{0,2},{1,3},{2,0},{3,1},{4,6},{5,7},{6,4},{7,5},{8,10},{9,11},{10,... | collective-permute-start | bytes 663560 | tf_op jit(solution)/shard_map/ppermute | solution.py:636
  107.1 6.3 %collective-permute-start.10 = (f32[16,3456]{1,0:T(8,128)S(1)}, f32[16,3456]{1,0:T(8,128)S(1)}, u32[]{:S(2)}, u32[]{:S(2)}) collective-permute-start(f32[16,3456]{1,0:T(8,128)S(1)} %get-tuple-element.60), channel_id=1, source_target_pairs={{0,3},{1,0},{2,1},{3,2},{4,7},{5,4},{6,5},{7,6},{8,11},{9,8},{10,9... | collective-permute-start | bytes 663560 | tf_op jit(solution)/shard_map/ppermute | solution.py:636
  114.3 7.3 %collective-permute-start.11 = (f32[64,64]{1,0:T(8,128)S(1)}, f32[64,64]{1,0:T(8,128)S(1)}, u32[]{:S(2)}, u32[]{:S(2)}) collective-permute-start(f32[64,64]{1,0:T(8,128)S(1)} %get-tuple-element.61), channel_id=1, source_target_pairs={{0,4},{4,0},{8,12},{12,8},{16,20},{20,16},{24,28},{28,24},{32,36},... | collective-permute-start | bytes 49160 | tf_op jit(solution)/shard_map/ppermute | solution.py:641
  121.6 12.0 %collective-permute-start.14 = (f32[64,64]{1,0:T(8,128)S(1)}, f32[64,64]{1,0:T(8,128)S(1)}, u32[]{:S(2)}, u32[]{:S(2)}) collective-permute-start(f32[64,64]{1,0:T(8,128)S(1)} %add.30), channel_id=1, source_target_pairs={{0,24},{4,28},{8,16},{12,20},{16,8},{20,12},{24,0},{28,4},{32,56},... | collective-permute-start | bytes 49160 | tf_op jit(solution)/shard_map/ppermute | solution.py:641
  131.6 5.4 %collective-permute-start.13 = (f32[64,64]{1,0:T(8,128)S(1)}, f32[64,64]{1,0:T(8,128)S(1)}, u32[]{:S(2)}, u32[]{:S(2)}) collective-permute-start(f32[64,64]{1,0:T(8,128)S(1)} %add.30), channel_id=1, source_target_pairs={{0,16},{4,20},{8,24},{12,28},{16,0},{20,4},{24,8},{28,12},{32,48},... | collective-permute-start | bytes 49160 | tf_op jit(solution)/shard_map/ppermute | solution.py:641
  131.7 5.4 %collective-permute-start.12 = (f32[64,64]{1,0:T(8,128)S(1)}, f32[64,64]{1,0:T(8,128)S(1)}, u32[]{:S(2)}, u32[]{:S(2)}) collective-permute-start(f32[64,64]{1,0:T(8,128)S(1)} %add.30), channel_id=1, source_target_pairs={{0,8},{4,12},{8,0},{12,4},{16,24},{20,28},{24,16},{28,20},{32,40},... | collective-permute-start | bytes 49160 | tf_op jit(solution)/shard_map/ppermute | solution.py:641
  137.1 5.2 %collective-permute-start.17 = (f32[64,64]{1,0:T(8,128)S(1)}, f32[64,64]{1,0:T(8,128)S(1)}, u32[]{:S(2)}, u32[]{:S(2)}) collective-permute-start(f32[64,64]{1,0:T(8,128)S(1)} %add_add_fusion.2), channel_id=1, source_target_pairs={{0,96},{4,100},{8,104},{12,108},{16,112},{20,116},{24,120},{28,124... | collective-permute-start | bytes 49160 | tf_op jit(solution)/shard_map/ppermute | solution.py:641
  137.2 5.6 %collective-permute-start.16 = (f32[64,64]{1,0:T(8,128)S(1)}, f32[64,64]{1,0:T(8,128)S(1)}, u32[]{:S(2)}, u32[]{:S(2)}) collective-permute-start(f32[64,64]{1,0:T(8,128)S(1)} %add_add_fusion.2), channel_id=1, source_target_pairs={{0,64},{4,68},{8,72},{12,76},{16,80},{20,84},{24,88},{28,92},{32,9... | collective-permute-start | bytes 49160 | tf_op jit(solution)/shard_map/ppermute | solution.py:641
  140.9 3.9 %collective-permute-start.15 = (f32[64,64]{1,0:T(8,128)S(1)}, f32[64,64]{1,0:T(8,128)S(1)}, u32[]{:S(2)}, u32[]{:S(2)}) collective-permute-start(f32[64,64]{1,0:T(8,128)S(1)} %add_add_fusion.2), channel_id=1, source_target_pairs={{0,32},{4,36},{8,40},{12,44},{16,48},{20,52},{24,56},{28,60},{32,0... | collective-permute-start | bytes 49160 | tf_op jit(solution)/shard_map/ppermute | solution.py:641
  144.8 5.2 %collective-permute-start.20 = (f32[64,64]{1,0:T(8,128)S(1)}, f32[64,64]{1,0:T(8,128)S(1)}, u32[]{:S(2)}, u32[]{:S(2)}) collective-permute-start(f32[64,64]{1,0:T(8,128)S(1)} %add_add_fusion.1), channel_id=1, source_target_pairs={{0,3},{1,2},{2,1},{3,0},{4,7},{5,6},{6,5},{7,4},{8,11},{9,10},{10,... | collective-permute-start | bytes 49160 | tf_op jit(solution)/shard_map/ppermute | solution.py:641
  147.0 5.4 %collective-permute-start.19 = (f32[64,64]{1,0:T(8,128)S(1)}, f32[64,64]{1,0:T(8,128)S(1)}, u32[]{:S(2)}, u32[]{:S(2)}) collective-permute-start(f32[64,64]{1,0:T(8,128)S(1)} %add_add_fusion.1), channel_id=1, source_target_pairs={{0,2},{1,3},{2,0},{3,1},{4,6},{5,7},{6,4},{7,5},{8,10},{9,11},{10,... | collective-permute-start | bytes 49160 | tf_op jit(solution)/shard_map/ppermute | solution.py:641
  148.4 4.0 %collective-permute-start.18 = (f32[64,64]{1,0:T(8,128)S(1)}, f32[64,64]{1,0:T(8,128)S(1)}, u32[]{:S(2)}, u32[]{:S(2)}) collective-permute-start(f32[64,64]{1,0:T(8,128)S(1)} %add_add_fusion.1), channel_id=1, source_target_pairs={{0,1},{1,0},{2,3},{3,2},{4,5},{5,4},{6,7},{7,6},{8,9},{9,8},{10,11... | collective-permute-start | bytes 49160 | tf_op jit(solution)/shard_map/ppermute | solution.py:641
  158.8 9.6 %collective-permute-start.21 = (f32[16,3456]{1,0:T(8,128)S(1)}, f32[16,3456]{1,0:T(8,128)S(1)}, u32[]{:S(2)}, u32[]{:S(2)}) collective-permute-start(f32[16,3456]{1,0:T(8,128)S(1)} %get-tuple-element.64), channel_id=1, source_target_pairs={{0,1},{1,2},{2,3},{3,0},{4,5},{5,6},{6,7},{7,4},{8,9},{9,10},{10,1... | collective-permute-start | bytes 663560 | tf_op jit(solution)/shard_map/ppermute | solution.py:636
  159.3 9.1 %collective-permute-start.22 = (f32[16,3456]{1,0:T(8,128)S(1)}, f32[16,3456]{1,0:T(8,128)S(1)}, u32[]{:S(2)}, u32[]{:S(2)}) collective-permute-start(f32[16,3456]{1,0:T(8,128)S(1)} %get-tuple-element.65), channel_id=1, source_target_pairs={{0,2},{1,3},{2,0},{3,1},{4,6},{5,7},{6,4},{7,5},{8,10},{9,11},{10,... | collective-permute-start | bytes 663560 | tf_op jit(solution)/shard_map/ppermute | solution.py:636
  161.8 7.4 %collective-permute-start.23 = (f32[16,3456]{1,0:T(8,128)S(1)}, f32[16,3456]{1,0:T(8,128)S(1)}, u32[]{:S(2)}, u32[]{:S(2)}) collective-permute-start(f32[16,3456]{1,0:T(8,128)S(1)} %get-tuple-element.66), channel_id=1, source_target_pairs={{0,3},{1,0},{2,1},{3,2},{4,7},{5,4},{6,5},{7,6},{8,11},{9,8},{10,9... | collective-permute-start | bytes 663560 | tf_op jit(solution)/shard_map/ppermute | solution.py:636
  (6 other events, 8.1 us)

commit v3 on v2

--- a/solution.py
+++ b/solution.py
@@ -21,7 +21,8 @@
 NJ = NPAD // L
 WIDE = 7
 NARROW = 3
-PACK = 352
+PACK = 72
+PW = 2 * NPAD + L
 GROUP = 16
 SLOTS = 14 * GROUP
 HPAD = 896
@@ -39,9 +40,12 @@
 BF16 = jnp.bfloat16
 I32 = jnp.int32
 VLIM = 40 * 1024 * 1024
+SMALL = 20 * 1024 * 1024
+WHOLE = 64 * 1024 * 1024
 
 VM = pl.BlockSpec(memory_space=pltpu.VMEM)
 SM = pl.BlockSpec(memory_space=pltpu.SMEM)
+HBM = pl.BlockSpec(memory_space=pltpu.HBM)
 NT = (((1,), (1,)), ((), ()))
 
 
@@ -220,12 +224,28 @@
 
 
 def prepare_kernel(
+    rows_hbm, masters_hbm, weights_hbm, block_hbm,
+    oh_ref, pe_ref, w_ref, src_ref, posr_ref, hq_ref, start_ref, u_ref, left_ref, right_ref,
     rows_ref, masters_ref, weights_ref, block_ref,
-    oh_ref, pe_ref, w_ref, src_ref, posr_ref, hq_ref, start_ref, u_ref, left_ref, right_ref,
-    ent_ref, a_ref, b_ref, tab_ref, z_ref, g_ref, lhs_ref, start_s, sem,
+    ent_ref, a_ref, b_ref, tab_ref, z_ref, g_ref, lhs_ref, start_s, sem, sems,
 ):
+    loads = [
+        pltpu.make_async_copy(src, dst, sems.at[i])
+        for i, (src, dst) in enumerate(
+            (
+                (rows_hbm, rows_ref),
+                (masters_hbm, masters_ref),
+                (weights_hbm, weights_ref),
+                (block_hbm, block_ref),
+            )
+        )
+    ]
+    for load in loads:
+        load.start()
     ent_ref[...] = jnp.full((1, E), -1, I32)
     w_ref[...] = jnp.zeros((1, ME), F32)
+    for load in loads[:3]:
+        load.wait()
     for k in range(MASTERS):
         col = slice(k * HPAD, k * HPAD + HANG)
         ent_ref[0:1, col] = masters_ref[k : k + 1, :]
@@ -235,6 +255,7 @@
     copy = pltpu.make_async_copy(start_ref, start_s, sem)
     copy.start()
     copy.wait()
+    loads[3].wait()
     compress(lambda b: block_ref[:, at(b)], z_ref, src_ref, start_s)
     hanging_values(z_ref, oh_ref, pe_ref, w_ref, g_ref, lhs_ref, hq_ref)
 
@@ -275,9 +296,13 @@
             sds((S, RIM)),
             sds((S, RIM)),
         ),
-        in_specs=[VM] * 4,
+        in_specs=[HBM] * 4,
         out_specs=(VM,) * 10,
         scratch_shapes=[
+            pltpu.VMEM((1, HANG), I32),
+            pltpu.VMEM((MASTERS, HANG), I32),
+            pltpu.VMEM((MASTERS, HANG), F32),
+            pltpu.VMEM((S, LOC), F32),
             pltpu.VMEM((1, E), I32),
             pltpu.VMEM((L, E), BF16),
             pltpu.VMEM((L, E), BF16),
@@ -285,35 +310,84 @@
             *HANG_SCRATCH,
             pltpu.SMEM((8, L), I32),
             pltpu.SemaphoreType.DMA,
+            pltpu.SemaphoreType.DMA((4,)),
         ],
         compiler_params=pltpu.CompilerParams(vmem_limit_bytes=VLIM),
         name="prepare",
     )(rows, masters, weights, block)
 
 
+def pack_kernel(dofs_hbm, pot_hbm, scale_hbm, count_ref, own_ref, dofs_ref, pot_ref, scale_ref, sems):
+    moves = ((dofs_hbm, dofs_ref), (pot_hbm, pot_ref), (scale_hbm, scale_ref))
+    loads = [pltpu.make_async_copy(src, dst, sems.at[i]) for i, (src, dst) in enumerate(moves)]
+    for load in loads:
+        load.start()
+    for load in loads:
+        load.wait()
+    own_ref[0:CELLS, 0:NODES] = dofs_ref[...].astype(F32)
+    own_ref[0:CELLS, NPAD : NPAD + NODES] = pot_ref[...]
+    own_ref[CELLS:PACK, 0:CELLS] = jnp.broadcast_to(scale_ref[...], (PACK - CELLS, CELLS))
+    own_ref[CELLS:PACK, L : 2 * L] = jnp.full((PACK - CELLS, L), count_ref[0]).astype(F32)
+
+
+def pack(dofs, pot, scale, count):
+    return pl.pallas_call(
+        pack_kernel,
+        out_shape=sds((PACK, PW)),
+        in_specs=[HBM] * 3 + [SM],
+        out_specs=VM,
+        scratch_shapes=[
+            pltpu.VMEM((CELLS, NODES), I32),
+            pltpu.VMEM((CELLS, NODES), F32),
+            pltpu.VMEM((1, CELLS), F32),
+            pltpu.SemaphoreType.DMA((3,)),
+        ],
+        compiler_params=pltpu.CompilerParams(vmem_limit_bytes=WHOLE),
+        name="pack",
+    )(dofs, pot, scale, count)
+
+
+def inverse(rels):
+    oh = jnp.concatenate([one_hot(rel & 127, L) for rel in rels], axis=1).astype(BF16)
+    rows = []
+    for j, rel in enumerate(rels):
+        m = jnp.broadcast_to(rel >> 7, (8, L)) == iota((8, L), 0)
+        node = jnp.where(m, iota((8, L), 1) + 1, 0).astype(F32)
+        zero = jnp.zeros((8, L), F32)
+        rows.append(jnp.concatenate([node if i == j else zero for i in range(len(rels))], axis=1))
+    return nt(jnp.concatenate(rows, axis=0).astype(BF16), oh).astype(I32) - 1
+
+
 def cells_kernel(
-    own_ref, left_ref, right_ref, k_ref,
+    own_ref, left_ref, right_ref, dom_ref, k_hbm,
     tab_ref, pot_ref, kh_ref, kl_ref, base_ref,
-    in_ref, all_ref, meta_ref, pad_ref, meta_s, list_s, wide_s, sem,
+    all_ref, meta_ref, k_ref, pad_ref, meta_s, list_s, wide_s, sem, sem_k,
 ):
-    in_ref[PACK:, :] = jnp.zeros((NPAD - PACK, L), F32)
+    load = pltpu.make_async_copy(k_hbm, k_ref, sem_k)
+    load.start()
     lane = iota((CELLS, L), 1)
+    cell = iota((CELLS, L), 0)
     tail = NODES - 2 * L
-    for i, (ref, shift) in enumerate(((own_ref, 0), (left_ref, -LOC), (right_ref, LOC))):
+    sources = ((own_ref, 0, None), (left_ref, -LOC, 0), (right_ref, LOC, 1))
+    for i, (ref, shift, side) in enumerate(sources):
         r = slice(i * CELLS, (i + 1) * CELLS)
-        in_ref[0:PACK, :] = ref[...]
         lows, tops = [], []
         for j in range(NJ):
-            t = in_ref[j * L : (j + 1) * L, :].T
-            dofs = t[0:CELLS] + float(shift)
+            dofs = ref[0:CELLS, j * L : (j + 1) * L] + float(shift)
             real = lane < (L if j < 2 else tail)
             low = jnp.where(real, dofs, float(BIG))
             all_ref[r, j * L : (j + 1) * L] = low
-            all_ref[r, NPAD + j * L : NPAD + (j + 1) * L] = t[CELLS:]
+            pot = ref[0:CELLS, NPAD + j * L : NPAD + (j + 1) * L]
+            all_ref[r, NPAD + j * L : NPAD + (j + 1) * L] = jnp.where(real, pot, 0.0)
             lows.append(jnp.min(low, axis=1, keepdims=True).astype(I32))
             tops.append(jnp.max(jnp.where(real, dofs, -float(BIG)), axis=1, keepdims=True).astype(I32))
-        all_ref[r, 2 * NPAD :] = jnp.broadcast_to(t[0:CELLS, tail : tail + 1], (CELLS, L))
-        live = t[CELLS:, tail : tail + 1] > 0.5
+        scales = jnp.broadcast_to(ref[CELLS : CELLS + 1, 0:L], (CELLS, L))
+        scale = jnp.sum(jnp.where(lane == cell, scales, 0.0), axis=1, keepdims=True)
+        all_ref[r, 2 * NPAD :] = jnp.broadcast_to(scale, (CELLS, L))
+        count = jnp.broadcast_to(ref[CELLS : CELLS + 1, L : 2 * L], (CELLS, L))
+        live = cell.astype(F32) < count
+        if side is not None:
+            live = live & jnp.full((CELLS, L), dom_ref[1 + side] > 0)
         low = jnp.minimum(jnp.minimum(lows[0], lows[1]), lows[2])
         top = jnp.maximum(jnp.maximum(tops[0], tops[1]), tops[2])
         used = live & (top >= RIM) & (low < RIM + LOC)
@@ -328,6 +402,7 @@
     copy = pltpu.make_async_copy(meta_ref, meta_s, sem)
     copy.start()
     pad_ref[...] = jnp.zeros_like(pad_ref)
+    load.wait()
     pad_ref[0:NODES, 0:NODES] = k_ref[...]
     kh_ref[...], kl_ref[...] = split(pad_ref[...])
     copy.wait()
@@ -364,18 +439,19 @@
         valid = c >= 0
         c = jnp.maximum(c, 0)
         vals = all_ref[pl.ds(c, 1), :]
+        rels = []
         for j in range(NJ):
             b = jnp.where(valid, meta_s[c, 1 + j], 0)
             base_ref[4 * slot + j] = b
             rel = vals[:, j * L : (j + 1) * L].astype(I32) - b * L
             rel = jnp.where(valid & (rel < WIDE * L), rel, BIG)
-            oh = one_hot(rel & 127, L).astype(BF16)
-            m = jnp.broadcast_to(rel >> 7, (8, L)) == iota((8, L), 0)
-            node = jnp.where(m, iota((8, L), 1) + 1, 0).astype(F32).astype(BF16)
-            tab_ref[slot, 8 + 8 * j : 16 + 8 * j, :] = nt(node, oh).astype(I32) - 1
+            rels.append(rel)
             tab_ref[slot, j : j + 1, :] = rel
             pot_ref[slot, j : j + 1, :] = vals[:, NPAD + j * L : NPAD + (j + 1) * L]
         pot_ref[slot, 3:4, :] = vals[:, 2 * NPAD :]
+        inv = inverse(rels)
+        for j in range(NJ):
+            tab_ref[slot, 3 + 3 * j : 6 + 3 * j, :] = inv[8 * j : 8 * j + NARROW]
 
     def some(i, _):
         for k in range(8):
@@ -385,31 +461,32 @@
     lax.fori_loop(0, last // 8, some, 0)
 
 
-def cell_tables(own, left, right, stiffness):
+def cell_tables(own, left, right, dom, stiffness):
     return pl.pallas_call(
         cells_kernel,
         out_shape=(
-            sds((SLOTS, 32, L), I32),
+            sds((SLOTS, 16, L), I32),
             sds((SLOTS, 8, L)),
             sds((NPAD, NPAD), BF16),
             sds((NPAD, NPAD), BF16),
             sds((4 * SLOTS + L,), I32),
         ),
-        in_specs=[VM] * 4,
+        in_specs=[VM] * 3 + [SM, HBM],
         out_specs=(VM, VM, VM, VM, SM),
         scratch_shapes=[
-            pltpu.VMEM((NPAD, L), F32),
-            pltpu.VMEM((3 * CELLS, 7 * L), F32),
+            pltpu.VMEM((3 * CELLS, PW), F32),
             pltpu.VMEM((3 * CELLS, L), I32),
+            pltpu.VMEM((NODES, NODES), F32),
             pltpu.VMEM((NPAD, NPAD), F32),
             pltpu.SMEM((3 * CELLS, L), I32),
             pltpu.SMEM((SLOTS + GROUP,), I32),
             pltpu.SMEM((3 * CELLS + GROUP,), I32),
             pltpu.SemaphoreType.DMA,
+            pltpu.SemaphoreType.DMA,
         ],
-        compiler_params=pltpu.CompilerParams(vmem_limit_bytes=VLIM),
+        compiler_params=pltpu.CompilerParams(vmem_limit_bytes=SMALL),
         name="cell_tables",
-    )(own, left, right, stiffness)
+    )(own, left, right, dom, stiffness)
 
 
 def step_kernel(number, *refs):
@@ -418,9 +495,9 @@
     outs = refs[17 : 17 + (4 if number == 3 else 3)]
     ext_ref, acc0_ref, acc1_ref, x_ref, p_ref, z_ref, g_ref, lhs_ref = refs[17 + len(outs) :]
     accs = (acc0_ref, acc1_ref)
-    ext_ref[:, 0:RIM] = gl_ref[...]
+    ext_ref[:, 0:RIM] = jnp.where(me_ref[1] > 0, gl_ref[...], 0.0)
     ext_ref[:, RIM : RIM + LOC] = u_ref[...]
-    ext_ref[:, RIM + LOC :] = gr_ref[...]
+    ext_ref[:, RIM + LOC :] = jnp.where(me_ref[2] > 0, gr_ref[...], 0.0)
     for ref in accs:
         ref[...] = jnp.zeros_like(ref)
     gn = base_ref[4 * SLOTS]
@@ -441,6 +518,11 @@
     def store(slot, parity, width):
         acc_ref = accs[parity]
         scale = jnp.broadcast_to(pot_ref[slot, 3:4, :], (8, L))
+        if width == NARROW:
+            inv = [[tab_ref[slot, 3 + 3 * j + t : 4 + 3 * j + t, :] for t in range(width)] for j in range(NJ)]
+        else:
+            full = inverse([tab_ref[slot, j : j + 1, :] for j in range(NJ)])
+            inv = [[full[8 * j + t : 8 * j + t + 1] for t in range(width)] for j in range(NJ)]
         for j in range(NJ):
             b = base_ref[4 * slot + j]
             col = slice(j * L, (j + 1) * L)
@@ -451,7 +533,7 @@
                 vals.append(scale * p_ref[r, col] + pot * x_ref[r, col])
             adds = []
             for t in range(width):
-                row = jnp.broadcast_to(tab_ref[slot, 8 + 8 * j + t : 9 + 8 * j + t, :], (8, L))
+                row = jnp.broadcast_to(inv[j][t], (8, L))
                 m, lo = row >= 0, row & 127
                 adds.append([jnp.where(m, lanes(vals[s], lo), 0.0) for s in range(2)])
             olds = [[acc_ref[8 * s : 8 * s + 8, at(b + t)] for s in range(2)] for t in range(width)]
@@ -630,10 +712,9 @@
     )(*qs, me)
 
 
-def shift(x, axis, by, wrap):
+def shift(x, axis, by):
     size = lax.axis_size(axis)
-    pairs = [(i, (i + by) % size) for i in range(size) if wrap or 0 <= i + by < size]
-    return lax.ppermute(x, axis, pairs)
+    return lax.ppermute(x, axis, [(i, (i + by) % size) for i in range(size)])
 
 
 def swap(x, axis, bits):
@@ -660,36 +741,30 @@
     hang_masters,
     hang_weights,
 ):
-    me = lax.axis_index("band").astype(I32).reshape(1)
-    alive = (jnp.arange(CELLS) < cell_count[0]).astype(F32)
-    own = jnp.concatenate(
-        [
-            jnp.concatenate([cell_dofs.astype(F32), potential], axis=1),
-            jnp.concatenate([cell_scale, alive])[None],
-            jnp.zeros((PACK - NODES - 1, L), F32),
-        ],
-        axis=0,
-    )
-    from_left = shift(own, "dom", 1, False)
-    from_right = shift(own, "dom", -1, False)
+    dom = lax.axis_index("dom")
+    inside = [lax.axis_index("band"), dom > 0, dom < lax.axis_size("dom") - 1]
+    me = jnp.stack([jnp.asarray(x).astype(I32) for x in inside])
+    own = pack(cell_dofs.T, potential.T, cell_scale[None], cell_count)
+    from_left = shift(own, "dom", 1)
+    from_right = shift(own, "dom", -1)
     *hang, start, u0, first, last = prepare(hang_rows[None], hang_masters, hang_weights, block)
 
     def ghosts(first, last):
-        return shift(last, "dom", 1, False), shift(first, "dom", -1, False)
+        return shift(last, "dom", 1), shift(first, "dom", -1)
 
     gl, gr = ghosts(first, last)
-    *cell, base = cell_tables(own, from_left, from_right, stiffness)
+    *cell, base = cell_tables(own, from_left, from_right, me, stiffness)
     args = (cell, base, hang, start, me)
     u1, first, last = apply_step(1, u0, gl, gr, u0, *args)
     gl, gr = ghosts(first, last)
     u2, first, last = apply_step(2, u1, gl, gr, u0, *args)
     gl, gr = ghosts(first, last)
     qs = apply_step(3, u2, gl, gr, u1, *args)
-    qs = [qs[0]] + [shift(qs[k], "band", k, True) for k in (1, 2, 3)]
+    qs = [qs[0]] + [shift(qs[k], "band", k) for k in (1, 2, 3)]
     gram, rows = gram_of(qs, me)
     gram = summed(gram)
     outs = basis_of(gram, rows, me, LOC * lax.axis_size("dom"))
-    outs = [outs[0]] + [shift(outs[k], "band", k, True) for k in (1, 2, 3)]
+    outs = [outs[0]] + [shift(outs[k], "band", k) for k in (1, 2, 3)]
     return join(outs, me)
 
 

time: 171 us -> 156 us (0.912); the launches traced: 170 us -> 158 us
  starting transfers between devices: 60 us -> 51.3 us
  Pallas kernels: 69.1 us -> 66.8 us
  other arithmetic: 1.84 us -> 0.11 us
    ppermute x10, starting transfers between devices: 25.8 us -> 17.1 us  [swap(): return lax.ppermute(x, axis, [(i, i ^ bits) for i in range(size)])]
    pallas_call x3, Pallas kernels: 42.4 us -> 38.3 us  [apply_step(): pl.pallas_call(functools.partial(step_kernel, number), out_shape=shapes,...]
    pallas_call x1 -> x2, Pallas kernels: 8.89 us -> 8.96 us  [the longest x1 7.28 us: cell_tables(): pl.pallas_call(cells_kernel, out_shape=(sds((SLOTS, 16, L), I32), sds((SL...]
    unnamed x13 -> x14, local copies, waits for them, and re-layouts: 9.11 us -> 9.04 us
  transfers between devices with their start and end apart: 24 -> 24, of which waited for: 14 -> 13; matrix products, arithmetic and copies ran while one was open for 0% -> 0% of each run, Pallas kernels for 11% -> 11%
where the time goes in v3:
time: 156 us; the launch traced here: 158 us
  Pallas kernels  66.8 us (43%)
  starting transfers between devices  51.3 us (33%)
  waiting for transfers between devices  29.1 us (19%)
  local copies, waits for them, and re-layouts  9.73 us (6%)
    pallas_call x3, Pallas kernels, apply_step(): pl.pallas_call(functools.partial(step_kernel, number), out_shape=shapes,...  38.3 us
    ppermute x14, starting transfers between devices, shift(): return lax.ppermute(x, axis, [(i, (i + by) % size) for i in range(size)])  34.2 us
    ppermute x10, starting transfers between devices, swap(): return lax.ppermute(x, axis, [(i, i ^ bits) for i in range(size)])  17.1 us
    ppermute x14, waiting for transfers between devices, shift(): return lax.ppermute(x, axis, [(i, (i + by) % size) for i in range(size)])  16.2 us
    ppermute x10, waiting for transfers between devices, swap(): return lax.ppermute(x, axis, [(i, i ^ bits) for i in range(size)])  12.9 us
    pallas_call x1, Pallas kernels, prepare(): pl.pallas_call(prepare_kernel, out_shape=(sds((QLO, E), BF16), sds((1, E)...  9.75 us
    unnamed x14, local copies, waits for them, and re-layouts  9.04 us
    pallas_call x1, Pallas kernels, cell_tables(): pl.pallas_call(cells_kernel, out_shape=(sds((SLOTS, 16, L), I32), sds((SL...  7.28 us
  transfers between devices with their start and end apart: 24, of which 13 were waited for; matrix products, arithmetic and copies ran while one was open for 0% of the time, Pallas kernels for 11%

profile of v3, /device:TPU:0, one launch (start us, length us, event | category | flops | bytes accessed | tf_op | source)
XLA Modules:
  0.0 157.8 jit_solution(10075191668258596813)
XLA Ops:
  2.3 4.8 %collective-permute-start.3 = (f32[72,896]{1,0:T(8,128)}, f32[72,896]{1,0:T(8,128)S(1)}, u32[]{:S(2)}, u32[]{:S(2)}) collective-permute-start(f32[72,896]{1,0:T(8,128)} %pack.1.own_ref), channel_id=1, source_target_pairs={{0,124},{4,0},{8,4},{12,8},{16,12},{20,16},{24,20},{28,24},{32,28}... | collective-permute-start | bytes 774152 | tf_op jit(solution)/shard_map/ppermute | solution.py:717
  10.4 9.7 %prepare.1 = (bf16[512,4608]{1,0:T(8,128)(2,1)S(1)}, s32[1,4608]{1,0:T(1,128)S(1)}, f32[1,3584]{1,0:T(1,128)S(1)}, s32[40,128]{1,0:T(8,128)S(1)}, s32[128,128]{1...) custom-call(s32[1,864]{1,0:T(1,128)S(1)} %broadcast_in_dim.6.rows_hb, ...), custom_call_target="tpu_custom_call" | custom-call | tf_op jit(solution)/shard_map/prepare/pallas_call | solution.py:285
  20.2 2.1 %copy-done = bf16[512,4608]{1,0:T(8,128)(2,1)} copy-done((bf16[512,4608]{1,0:T(8,128)(2,1)}, bf16[512,4608]{1,0:T(8,128)(2,1)S(1)}, u32[]{:S(2)}) %copy-start) | copy-done | bytes 4718616
  22.3 5.1 %collective-permute-start.1 = (f32[16,2048]{1,0:T(8,128)S(1)}, f32[16,2048]{1,0:T(8,128)S(1)}, u32[]{:S(2)}, u32[]{:S(2)}) collective-permute-start(f32[16,2048]{1,0:T(8,128)S(1)} %get-tuple-element.38), channel_id=1, source_target_pairs={{0,124},{4,0},{8,4},{12,8},{16,12},{20,16},{24,20},{28,24},{32,28}... | collective-permute-start | bytes 393224 | tf_op jit(solution)/shard_map/ppermute | solution.py:717
  29.5 7.3 %cell_tables.1 = (s32[224,16,128]{2,1,0:T(8,128)S(1)}, f32[224,8,128]{2,1,0:T(8,128)S(1)}, bf16[384,384]{1,0:T(8,128)(2,1)S(1)}, bf16[384,384]{1,0:T(8,128)(2,1)S(1)}, s32[1024]{0:T(1024)S(1)}) custom-call(f32[72,896]{1,0:T(8,128)S(1)} %copy-done.2, f32[72,896]{1,0:T(8,128)S(1)} %collective-permute-done.2.left_ref, ...), custom_call_target="tpu_custom_call" | custom-call | tf_op jit(solution)/shard_map/cell_tables/pallas_call | solution.py:465
  36.8 2.3 %copy-done.1 = bf16[512,4608]{1,0:T(8,128)(2,1)S(1)} copy-done((bf16[512,4608]{1,0:T(8,128)(2,1)S(1)}, bf16[512,4608]{1,0:T(8,128)(2,1)}, u32[]{:S(2)}) %copy-start.1) | copy-done | bytes 4718616
  39.1 12.8 %step1.1 = (f32[16,13824]{1,0:T(8,128)S(1)}, f32[16,2048]{1,0:T(8,128)S(1)}, f32[16,2048]{1,0:T(8,128)S(1)}) custom-call(f32[16,13824]{1,0:T(8,128)S(1)} %get-tuple-element.36.refs_0_.refs_3_, f32[16,2048]{1,0:T(8,128)S(1)} %collective-permute-done.refs_1_, f32[16,2048]{1,0:T(8,128)S(1)} %collective-permute-done.1.refs_2_, ...), custom_call_target="tpu_custom_call" | custom-call | tf_op jit(solution)/shard_map/step1/pallas_call | solution.py:625
  52.0 5.1 %collective-permute-start.5 = (f32[16,2048]{1,0:T(8,128)S(1)}, f32[16,2048]{1,0:T(8,128)S(1)}, u32[]{:S(2)}, u32[]{:S(2)}) collective-permute-start(f32[16,2048]{1,0:T(8,128)S(1)} %get-tuple-element.53), channel_id=1, source_target_pairs={{0,124},{4,0},{8,4},{12,8},{16,12},{20,16},{24,20},{28,24},{32,28}... | collective-permute-start | bytes 393224 | tf_op jit(solution)/shard_map/ppermute | solution.py:717
  57.0 2.6 %collective-permute-done.4.refs_1_ = f32[16,2048]{1,0:T(8,128)S(1)} collective-permute-done((f32[16,2048]{1,0:T(8,128)S(1)}, f32[16,2048]{1,0:T(8,128)S(1)}, u32[]{:S(2)}, u32[]{:S(2)}) %collective-permute-start.4) | collective-permute-done | bytes 131104 | tf_op jit(solution)/shard_map/ppermute | solution.py:717
  59.7 12.6 %step2.1 = (f32[16,13824]{1,0:T(8,128)S(1)}, f32[16,2048]{1,0:T(8,128)S(1)}, f32[16,2048]{1,0:T(8,128)S(1)}) custom-call(f32[16,13824]{1,0:T(8,128)S(1)} %get-tuple-element.51.refs_0_.refs_3_, f32[16,2048]{1,0:T(8,128)S(1)} %collective-permute-done.4.refs_1_, f32[16,2048]{1,0:T(8,128)S(1)} %collective-permute-done.5.refs_2_, ...), custom_call_target="tpu_custom_call" | custom-call | tf_op jit(solution)/shard_map/step2/pallas_call | solution.py:625
  72.4 7.9 %collective-permute-start.7 = (f32[16,2048]{1,0:T(8,128)S(1)}, f32[16,2048]{1,0:T(8,128)S(1)}, u32[]{:S(2)}, u32[]{:S(2)}) collective-permute-start(f32[16,2048]{1,0:T(8,128)S(1)} %get-tuple-element.56), channel_id=1, source_target_pairs={{0,124},{4,0},{8,4},{12,8},{16,12},{20,16},{24,20},{28,24},{32,28}... | collective-permute-start | bytes 393224 | tf_op jit(solution)/shard_map/ppermute | solution.py:717
  80.3 2.6 %collective-permute-done.6.refs_1_ = f32[16,2048]{1,0:T(8,128)S(1)} collective-permute-done((f32[16,2048]{1,0:T(8,128)S(1)}, f32[16,2048]{1,0:T(8,128)S(1)}, u32[]{:S(2)}, u32[]{:S(2)}) %collective-permute-start.6) | collective-permute-done | bytes 131104 | tf_op jit(solution)/shard_map/ppermute | solution.py:717
  82.8 12.9 %step3.1 = (f32[16,3456]{1,0:T(8,128)S(1)}, f32[16,3456]{1,0:T(8,128)S(1)}, f32[16,3456]{1,0:T(8,128)S(1)}, f32[16,3456]{1,0:T(8,128)S(1)}) custom-call(f32[16,13824]{1,0:T(8,128)S(1)} %get-tuple-element.54.refs_0_, f32[16,2048]{1,0:T(8,128)S(1)} %collective-permute-done.6.refs_1_, f32[16,2048]{1,0:T(8,128)S(1)} %collective-permute-done.7.refs_2_, ...), custom_call_target="tpu_custom_call" | custom-call | tf_op jit(solution)/shard_map/step3/pallas_call | solution.py:625
  97.7 3.6 %collective-permute-start.9 = (f32[16,3456]{1,0:T(8,128)S(1)}, f32[16,3456]{1,0:T(8,128)S(1)}, u32[]{:S(2)}, u32[]{:S(2)}) collective-permute-start(f32[16,3456]{1,0:T(8,128)S(1)} %get-tuple-element.59), channel_id=1, source_target_pairs={{0,2},{1,3},{2,0},{3,1},{4,6},{5,7},{6,4},{7,5},{8,10},{9,11},{10,... | collective-permute-start | bytes 663560 | tf_op jit(solution)/shard_map/ppermute | solution.py:717
  103.7 3.8 %collective-permute-done.9.q2_ref = f32[16,3456]{1,0:T(8,128)S(1)} collective-permute-done((f32[16,3456]{1,0:T(8,128)S(1)}, f32[16,3456]{1,0:T(8,128)S(1)}, u32[]{:S(2)}, u32[]{:S(2)}) %collective-permute-start.9) | collective-permute-done | bytes 221216 | tf_op jit(solution)/shard_map/ppermute | solution.py:717
  110.3 7.7 %collective-permute-start.14 = (f32[64,64]{1,0:T(8,128)S(1)}, f32[64,64]{1,0:T(8,128)S(1)}, u32[]{:S(2)}, u32[]{:S(2)}) collective-permute-start(f32[64,64]{1,0:T(8,128)S(1)} %add.30), channel_id=1, source_target_pairs={{0,24},{4,28},{8,16},{12,20},{16,8},{20,12},{24,0},{28,4},{32,56},... | collective-permute-start | bytes 49160 | tf_op jit(solution)/shard_map/ppermute | solution.py:722
  119.9 3.5 %collective-permute-done.13 = f32[64,64]{1,0:T(8,128)S(1)} collective-permute-done((f32[64,64]{1,0:T(8,128)S(1)}, f32[64,64]{1,0:T(8,128)S(1)}, u32[]{:S(2)}, u32[]{:S(2)}) %collective-permute-start.13) | collective-permute-done | bytes 16416 | tf_op jit(solution)/shard_map/ppermute | solution.py:722
  123.4 2.5 %collective-permute-start.17 = (f32[64,64]{1,0:T(8,128)S(1)}, f32[64,64]{1,0:T(8,128)S(1)}, u32[]{:S(2)}, u32[]{:S(2)}) collective-permute-start(f32[64,64]{1,0:T(8,128)S(1)} %add_add_fusion.2), channel_id=1, source_target_pairs={{0,96},{4,100},{8,104},{12,108},{16,112},{20,116},{24,120},{28,124... | collective-permute-start | bytes 49160 | tf_op jit(solution)/shard_map/ppermute | solution.py:722
  128.6 2.7 %collective-permute-done.16 = f32[64,64]{1,0:T(8,128)S(1)} collective-permute-done((f32[64,64]{1,0:T(8,128)S(1)}, f32[64,64]{1,0:T(8,128)S(1)}, u32[]{:S(2)}, u32[]{:S(2)}) %collective-permute-start.16) | collective-permute-done | bytes 16416 | tf_op jit(solution)/shard_map/ppermute | solution.py:722
  131.3 2.2 %collective-permute-start.20 = (f32[64,64]{1,0:T(8,128)S(1)}, f32[64,64]{1,0:T(8,128)S(1)}, u32[]{:S(2)}, u32[]{:S(2)}) collective-permute-start(f32[64,64]{1,0:T(8,128)S(1)} %add_add_fusion.1), channel_id=1, source_target_pairs={{0,3},{1,2},{2,1},{3,0},{4,7},{5,6},{6,5},{7,4},{8,11},{9,10},{10,... | collective-permute-start | bytes 49160 | tf_op jit(solution)/shard_map/ppermute | solution.py:722
  136.5 2.5 %collective-permute-done.19 = f32[64,64]{1,0:T(8,128)S(1)} collective-permute-done((f32[64,64]{1,0:T(8,128)S(1)}, f32[64,64]{1,0:T(8,128)S(1)}, u32[]{:S(2)}, u32[]{:S(2)}) %collective-permute-start.19) | collective-permute-done | bytes 16416 | tf_op jit(solution)/shard_map/ppermute | solution.py:722
  139.0 6.9 %basis.1 = (f32[16,3456]{1,0:T(8,128)S(1)}, f32[16,3456]{1,0:T(8,128)S(1)}, f32[16,3456]{1,0:T(8,128)S(1)}, f32[16,3456]{1,0:T(8,128)S(1)}) custom-call(f32[64,64]{1,0:T(8,128)S(1)} %add_add_fusion.gram_ref, f32[64,3456]{1,0:T(8,128)S(1)} %get-tuple-element.62.all_ref, s32[3]{0:T(128)S(1)} %pad_add_fusion.dom_ref.refs_16_.me_ref), custom_call_target="tpu_custom_call" | custom-call | tf_op jit(solution)/shard_map/basis/pallas_call | solution.py:686
  146.3 2.5 %collective-permute-start.22 = (f32[16,3456]{1,0:T(8,128)S(1)}, f32[16,3456]{1,0:T(8,128)S(1)}, u32[]{:S(2)}, u32[]{:S(2)}) collective-permute-start(f32[16,3456]{1,0:T(8,128)S(1)} %get-tuple-element.65), channel_id=1, source_target_pairs={{0,2},{1,3},{2,0},{3,1},{4,6},{5,7},{6,4},{7,5},{8,10},{9,11},{10,... | collective-permute-start | bytes 663560 | tf_op jit(solution)/shard_map/ppermute | solution.py:717
  150.6 4.9 %collective-permute-done.21.q1_ref = f32[16,3456]{1,0:T(8,128)S(1)} collective-permute-done((f32[16,3456]{1,0:T(8,128)S(1)}, f32[16,3456]{1,0:T(8,128)S(1)}, u32[]{:S(2)}, u32[]{:S(2)}) %collective-permute-start.21) | collective-permute-done | bytes 221216 | tf_op jit(solution)/shard_map/ppermute | solution.py:717
  (53 shorter events, 26.6 us)
Async XLA Ops:
  2.3 25.1 %collective-permute-start.3 = (f32[72,896]{1,0:T(8,128)}, f32[72,896]{1,0:T(8,128)S(1)}, u32[]{:S(2)}, u32[]{:S(2)}) collective-permute-start(f32[72,896]{1,0:T(8,128)} %pack.1.own_ref), channel_id=1, source_target_pairs={{0,124},{4,0},{8,4},{12,8},{16,12},{20,16},{24,20},{28,24},{32,28}... | collective-permute-start | bytes 774152 | tf_op jit(solution)/shard_map/ppermute | solution.py:717
  7.1 20.3 %collective-permute-start.2 = (f32[72,896]{1,0:T(8,128)}, f32[72,896]{1,0:T(8,128)S(1)}, u32[]{:S(2)}, u32[]{:S(2)}) collective-permute-start(f32[72,896]{1,0:T(8,128)} %pack.1.own_ref), channel_id=1, source_target_pairs={{0,4},{4,8},{8,12},{12,16},{16,20},{20,24},{24,28},{28,32},{32,36}... | collective-permute-start | bytes 774152 | tf_op jit(solution)/shard_map/ppermute | solution.py:717
  22.3 14.4 %collective-permute-start = (f32[16,2048]{1,0:T(8,128)S(1)}, f32[16,2048]{1,0:T(8,128)S(1)}, u32[]{:S(2)}, u32[]{:S(2)}) collective-permute-start(f32[16,2048]{1,0:T(8,128)S(1)} %get-tuple-element.37), channel_id=1, source_target_pairs={{0,4},{4,8},{8,12},{12,16},{16,20},{20,24},{24,28},{28,32},{32,36}... | collective-permute-start | bytes 393224 | tf_op jit(solution)/shard_map/ppermute | solution.py:717
  22.3 14.4 %collective-permute-start.1 = (f32[16,2048]{1,0:T(8,128)S(1)}, f32[16,2048]{1,0:T(8,128)S(1)}, u32[]{:S(2)}, u32[]{:S(2)}) collective-permute-start(f32[16,2048]{1,0:T(8,128)S(1)} %get-tuple-element.38), channel_id=1, source_target_pairs={{0,124},{4,0},{8,4},{12,8},{16,12},{20,16},{24,20},{28,24},{32,28}... | collective-permute-start | bytes 393224 | tf_op jit(solution)/shard_map/ppermute | solution.py:717
  51.9 7.8 %collective-permute-start.4 = (f32[16,2048]{1,0:T(8,128)S(1)}, f32[16,2048]{1,0:T(8,128)S(1)}, u32[]{:S(2)}, u32[]{:S(2)}) collective-permute-start(f32[16,2048]{1,0:T(8,128)S(1)} %get-tuple-element.52), channel_id=1, source_target_pairs={{0,4},{4,8},{8,12},{12,16},{16,20},{20,24},{24,28},{28,32},{32,36}... | collective-permute-start | bytes 393224 | tf_op jit(solution)/shard_map/ppermute | solution.py:717
  52.0 7.7 %collective-permute-start.5 = (f32[16,2048]{1,0:T(8,128)S(1)}, f32[16,2048]{1,0:T(8,128)S(1)}, u32[]{:S(2)}, u32[]{:S(2)}) collective-permute-start(f32[16,2048]{1,0:T(8,128)S(1)} %get-tuple-element.53), channel_id=1, source_target_pairs={{0,124},{4,0},{8,4},{12,8},{16,12},{20,16},{24,20},{28,24},{32,28}... | collective-permute-start | bytes 393224 | tf_op jit(solution)/shard_map/ppermute | solution.py:717
  72.3 10.5 %collective-permute-start.6 = (f32[16,2048]{1,0:T(8,128)S(1)}, f32[16,2048]{1,0:T(8,128)S(1)}, u32[]{:S(2)}, u32[]{:S(2)}) collective-permute-start(f32[16,2048]{1,0:T(8,128)S(1)} %get-tuple-element.55), channel_id=1, source_target_pairs={{0,4},{4,8},{8,12},{12,16},{16,20},{20,24},{24,28},{28,32},{32,36}... | collective-permute-start | bytes 393224 | tf_op jit(solution)/shard_map/ppermute | solution.py:717
  72.4 10.4 %collective-permute-start.7 = (f32[16,2048]{1,0:T(8,128)S(1)}, f32[16,2048]{1,0:T(8,128)S(1)}, u32[]{:S(2)}, u32[]{:S(2)}) collective-permute-start(f32[16,2048]{1,0:T(8,128)S(1)} %get-tuple-element.56), channel_id=1, source_target_pairs={{0,124},{4,0},{8,4},{12,8},{16,12},{20,16},{24,20},{28,24},{32,28}... | collective-permute-start | bytes 393224 | tf_op jit(solution)/shard_map/ppermute | solution.py:717
  95.7 8.0 %collective-permute-start.8 = (f32[16,3456]{1,0:T(8,128)S(1)}, f32[16,3456]{1,0:T(8,128)S(1)}, u32[]{:S(2)}, u32[]{:S(2)}) collective-permute-start(f32[16,3456]{1,0:T(8,128)S(1)} %get-tuple-element.58), channel_id=1, source_target_pairs={{0,1},{1,2},{2,3},{3,0},{4,5},{5,6},{6,7},{7,4},{8,9},{9,10},{10,1... | collective-permute-start | bytes 663560 | tf_op jit(solution)/shard_map/ppermute | solution.py:717
  97.7 9.9 %collective-permute-start.9 = (f32[16,3456]{1,0:T(8,128)S(1)}, f32[16,3456]{1,0:T(8,128)S(1)}, u32[]{:S(2)}, u32[]{:S(2)}) collective-permute-start(f32[16,3456]{1,0:T(8,128)S(1)} %get-tuple-element.59), channel_id=1, source_target_pairs={{0,2},{1,3},{2,0},{3,1},{4,6},{5,7},{6,4},{7,5},{8,10},{9,11},{10,... | collective-permute-start | bytes 663560 | tf_op jit(solution)/shard_map/ppermute | solution.py:717
  101.3 6.3 %collective-permute-start.10 = (f32[16,3456]{1,0:T(8,128)S(1)}, f32[16,3456]{1,0:T(8,128)S(1)}, u32[]{:S(2)}, u32[]{:S(2)}) collective-permute-start(f32[16,3456]{1,0:T(8,128)S(1)} %get-tuple-element.60), channel_id=1, source_target_pairs={{0,3},{1,0},{2,1},{3,2},{4,7},{5,4},{6,5},{7,6},{8,11},{9,8},{10,9... | collective-permute-start | bytes 663560 | tf_op jit(solution)/shard_map/ppermute | solution.py:717
  109.0 1.3 collective-permute-start.11
  110.3 9.6 %collective-permute-start.14 = (f32[64,64]{1,0:T(8,128)S(1)}, f32[64,64]{1,0:T(8,128)S(1)}, u32[]{:S(2)}, u32[]{:S(2)}) collective-permute-start(f32[64,64]{1,0:T(8,128)S(1)} %add.30), channel_id=1, source_target_pairs={{0,24},{4,28},{8,16},{12,20},{16,8},{20,12},{24,0},{28,4},{32,56},... | collective-permute-start | bytes 49160 | tf_op jit(solution)/shard_map/ppermute | solution.py:722
  118.0 5.4 %collective-permute-start.13 = (f32[64,64]{1,0:T(8,128)S(1)}, f32[64,64]{1,0:T(8,128)S(1)}, u32[]{:S(2)}, u32[]{:S(2)}) collective-permute-start(f32[64,64]{1,0:T(8,128)S(1)} %add.30), channel_id=1, source_target_pairs={{0,16},{4,20},{8,24},{12,28},{16,0},{20,4},{24,8},{28,12},{32,48},... | collective-permute-start | bytes 49160 | tf_op jit(solution)/shard_map/ppermute | solution.py:722
  118.0 5.4 %collective-permute-start.12 = (f32[64,64]{1,0:T(8,128)S(1)}, f32[64,64]{1,0:T(8,128)S(1)}, u32[]{:S(2)}, u32[]{:S(2)}) collective-permute-start(f32[64,64]{1,0:T(8,128)S(1)} %add.30), channel_id=1, source_target_pairs={{0,8},{4,12},{8,0},{12,4},{16,24},{20,28},{24,16},{28,20},{32,40},... | collective-permute-start | bytes 49160 | tf_op jit(solution)/shard_map/ppermute | solution.py:722
  123.4 5.2 %collective-permute-start.17 = (f32[64,64]{1,0:T(8,128)S(1)}, f32[64,64]{1,0:T(8,128)S(1)}, u32[]{:S(2)}, u32[]{:S(2)}) collective-permute-start(f32[64,64]{1,0:T(8,128)S(1)} %add_add_fusion.2), channel_id=1, source_target_pairs={{0,96},{4,100},{8,104},{12,108},{16,112},{20,116},{24,120},{28,124... | collective-permute-start | bytes 49160 | tf_op jit(solution)/shard_map/ppermute | solution.py:722
  125.9 5.4 %collective-permute-start.16 = (f32[64,64]{1,0:T(8,128)S(1)}, f32[64,64]{1,0:T(8,128)S(1)}, u32[]{:S(2)}, u32[]{:S(2)}) collective-permute-start(f32[64,64]{1,0:T(8,128)S(1)} %add_add_fusion.2), channel_id=1, source_target_pairs={{0,64},{4,68},{8,72},{12,76},{16,80},{20,84},{24,88},{28,92},{32,9... | collective-permute-start | bytes 49160 | tf_op jit(solution)/shard_map/ppermute | solution.py:722
  126.8 4.5 %collective-permute-start.15 = (f32[64,64]{1,0:T(8,128)S(1)}, f32[64,64]{1,0:T(8,128)S(1)}, u32[]{:S(2)}, u32[]{:S(2)}) collective-permute-start(f32[64,64]{1,0:T(8,128)S(1)} %add_add_fusion.2), channel_id=1, source_target_pairs={{0,32},{4,36},{8,40},{12,44},{16,48},{20,52},{24,56},{28,60},{32,0... | collective-permute-start | bytes 49160 | tf_op jit(solution)/shard_map/ppermute | solution.py:722
  131.3 5.2 %collective-permute-start.20 = (f32[64,64]{1,0:T(8,128)S(1)}, f32[64,64]{1,0:T(8,128)S(1)}, u32[]{:S(2)}, u32[]{:S(2)}) collective-permute-start(f32[64,64]{1,0:T(8,128)S(1)} %add_add_fusion.1), channel_id=1, source_target_pairs={{0,3},{1,2},{2,1},{3,0},{4,7},{5,6},{6,5},{7,4},{8,11},{9,10},{10,... | collective-permute-start | bytes 49160 | tf_op jit(solution)/shard_map/ppermute | solution.py:722
  133.5 5.4 %collective-permute-start.19 = (f32[64,64]{1,0:T(8,128)S(1)}, f32[64,64]{1,0:T(8,128)S(1)}, u32[]{:S(2)}, u32[]{:S(2)}) collective-permute-start(f32[64,64]{1,0:T(8,128)S(1)} %add_add_fusion.1), channel_id=1, source_target_pairs={{0,2},{1,3},{2,0},{3,1},{4,6},{5,7},{6,4},{7,5},{8,10},{9,11},{10,... | collective-permute-start | bytes 49160 | tf_op jit(solution)/shard_map/ppermute | solution.py:722
  134.9 4.0 %collective-permute-start.18 = (f32[64,64]{1,0:T(8,128)S(1)}, f32[64,64]{1,0:T(8,128)S(1)}, u32[]{:S(2)}, u32[]{:S(2)}) collective-permute-start(f32[64,64]{1,0:T(8,128)S(1)} %add_add_fusion.1), channel_id=1, source_target_pairs={{0,1},{1,0},{2,3},{3,2},{4,5},{5,4},{6,7},{7,6},{8,9},{9,8},{10,11... | collective-permute-start | bytes 49160 | tf_op jit(solution)/shard_map/ppermute | solution.py:722
  145.8 9.6 %collective-permute-start.21 = (f32[16,3456]{1,0:T(8,128)S(1)}, f32[16,3456]{1,0:T(8,128)S(1)}, u32[]{:S(2)}, u32[]{:S(2)}) collective-permute-start(f32[16,3456]{1,0:T(8,128)S(1)} %get-tuple-element.64), channel_id=1, source_target_pairs={{0,1},{1,2},{2,3},{3,0},{4,5},{5,6},{6,7},{7,4},{8,9},{9,10},{10,1... | collective-permute-start | bytes 663560 | tf_op jit(solution)/shard_map/ppermute | solution.py:717
  146.3 9.1 %collective-permute-start.22 = (f32[16,3456]{1,0:T(8,128)S(1)}, f32[16,3456]{1,0:T(8,128)S(1)}, u32[]{:S(2)}, u32[]{:S(2)}) collective-permute-start(f32[16,3456]{1,0:T(8,128)S(1)} %get-tuple-element.65), channel_id=1, source_target_pairs={{0,2},{1,3},{2,0},{3,1},{4,6},{5,7},{6,4},{7,5},{8,10},{9,11},{10,... | collective-permute-start | bytes 663560 | tf_op jit(solution)/shard_map/ppermute | solution.py:717
  148.9 7.4 %collective-permute-start.23 = (f32[16,3456]{1,0:T(8,128)S(1)}, f32[16,3456]{1,0:T(8,128)S(1)}, u32[]{:S(2)}, u32[]{:S(2)}) collective-permute-start(f32[16,3456]{1,0:T(8,128)S(1)} %get-tuple-element.66), channel_id=1, source_target_pairs={{0,3},{1,0},{2,1},{3,2},{4,7},{5,4},{6,5},{7,6},{8,11},{9,8},{10,9... | collective-permute-start | bytes 663560 | tf_op jit(solution)/shard_map/ppermute | solution.py:717
  (7 other events, 9.1 us)

commit v4 on v3

--- a/solution.py
+++ b/solution.py
@@ -24,6 +24,7 @@
 PACK = 72
 PW = 2 * NPAD + L
 GROUP = 16
+RING = 4 * GROUP
 SLOTS = 14 * GROUP
 HPAD = 896
 HB = HPAD // L
@@ -39,7 +40,7 @@
 F32 = jnp.float32
 BF16 = jnp.bfloat16
 I32 = jnp.int32
-VLIM = 40 * 1024 * 1024
+VLIM = 28 * 1024 * 1024
 SMALL = 20 * 1024 * 1024
 WHOLE = 64 * 1024 * 1024
 
@@ -492,7 +493,7 @@
 def step_kernel(number, *refs):
     (u_ref, gl_ref, gr_ref, prev_ref, tab_ref, pot_ref, kh_ref, kl_ref,
      oh_ref, pe_ref, w_ref, src_ref, posr_ref, hq_ref, base_ref, start_ref, me_ref) = refs[:17]
-    outs = refs[17 : 17 + (4 if number == 3 else 3)]
+    outs = refs[17 : 17 + (8 if number == 3 else 3)]
     ext_ref, acc0_ref, acc1_ref, x_ref, p_ref, z_ref, g_ref, lhs_ref = refs[17 + len(outs) :]
     accs = (acc0_ref, acc1_ref)
     ext_ref[:, 0:RIM] = jnp.where(me_ref[1] > 0, gl_ref[...], 0.0)
@@ -513,7 +514,7 @@
                 acc = lanes(ext_ref[r, at(b)], lo)
                 for t in range(1, width):
                     acc = jnp.where(hi == t, lanes(ext_ref[r, at(b + t)], lo), acc)
-                x_ref[pl.ds(pl.multiple_of(slot * S + 8 * s, 8), 8), j * L : (j + 1) * L] = acc
+                x_ref[pl.ds(pl.multiple_of((slot & (RING - 1)) * S + 8 * s, 8), 8), j * L : (j + 1) * L] = acc
 
     def store(slot, parity, width):
         acc_ref = accs[parity]
@@ -529,7 +530,7 @@
             pot = jnp.broadcast_to(pot_ref[slot, j : j + 1, :], (8, L))
             vals = []
             for s in range(2):
-                r = pl.ds(pl.multiple_of(slot * S + 8 * s, 8), 8)
+                r = pl.ds(pl.multiple_of((slot & (RING - 1)) * S + 8 * s, 8), 8)
                 vals.append(scale * p_ref[r, col] + pot * x_ref[r, col])
             adds = []
             for t in range(width):
@@ -542,7 +543,7 @@
                     acc_ref[8 * s : 8 * s + 8, at(b + t)] = olds[t][s] + adds[t][s]
 
     def rows_of(i):
-        return pl.ds(pl.multiple_of(i * (GROUP * S), GROUP * S), GROUP * S)
+        return pl.ds(pl.multiple_of((i & 3) * (GROUP * S), GROUP * S), GROUP * S)
 
     def product(i):
         xh, xl = split(x_ref[rows_of(i), :])
@@ -615,11 +616,14 @@
         q = LOC // 4
         for k in range(4):
             outs[k][...] = new_ref[:, pl.ds(pl.multiple_of(((me + k) & 3) * q, L), q)]
+            for r in range(1, 4):
+                part = new_ref[:, pl.ds(pl.multiple_of(((me + k + r) & 3) * q, L), q)]
+                outs[4 + k][:, (r - 1) * q : r * q] = part
 
 
 def apply_step(number, u, gl, gr, prev, cell, base, hang, start, me):
     if number == 3:
-        shapes = (sds((S, LOC // 4)),) * 4
+        shapes = (sds((S, LOC // 4)),) * 4 + (sds((S, 3 * LOC // 4)),) * 4
     else:
         shapes = (sds((S, LOC)), sds((S, RIM)), sds((S, RIM)))
     return pl.pallas_call(
@@ -631,8 +635,8 @@
             pltpu.VMEM((S, EXT), F32),
             pltpu.VMEM((S, EXT), F32),
             pltpu.VMEM((S, EXT), F32),
-            pltpu.VMEM((SLOTS * S, NPAD), F32),
-            pltpu.VMEM((SLOTS * S, NPAD), F32),
+            pltpu.VMEM((RING * S, NPAD), F32),
+            pltpu.VMEM((RING * S, NPAD), F32),
             *HANG_SCRATCH,
         ],
         compiler_params=pltpu.CompilerParams(vmem_limit_bytes=VLIM),
@@ -660,56 +664,65 @@
     )(*qs, me)
 
 
-def basis_kernel(total, gram_ref, all_ref, me_ref, o0_ref, o1_ref, o2_ref, o3_ref, m_ref, r_ref):
+def factor_kernel(total, gram_ref, inv_ref):
     n = 4 * S
     eye = (iota((n, n), 0) == iota((n, n), 1)).astype(F32)
-    m_ref[...] = jnp.concatenate([gram_ref[...], eye], 1)
-    row_id = iota((n, 2 * n), 0)
-
-    m = m_ref[...]
-    diag = jnp.zeros((n, 1), F32)
-    for j in range(n):
-        pivot = m[j : j + 1, :]
-        d = pivot[:, j : j + 1]
-        f = m[:, j : j + 1] / d
-        m = m - jnp.where(row_id > j, f, 0.0) * pivot
-    dg = jnp.sum(jnp.where(row_id == iota((n, 2 * n), 1), m, 0.0), axis=1, keepdims=True)
-    inv = m[:, n:] * lax.rsqrt(dg) * jnp.sqrt(jnp.float32(total))
-    r_ref[...] = jnp.dot(inv, all_ref[...], preferred_element_type=F32, precision=lax.Precision.HIGHEST)
+    m = jnp.concatenate([gram_ref[...], eye], 1)
+    row = iota((n, 2 * n), 0)
+    for j in range(0, n, 2):
+        p1, p2 = m[j : j + 1, :], m[j + 1 : j + 2, :]
+        c1, c2 = m[:, j : j + 1], m[:, j + 1 : j + 2]
+        ra = 1.0 / p1[:, j : j + 1]
+        l = p2[:, j : j + 1] * ra
+        p2 = p2 - l * p1
+        rc = 1.0 / (m[j + 1 : j + 2, j + 1 : j + 2] - l * p1[:, j + 1 : j + 2])
+        update = c1 * (p1 * ra) + (c2 - c1 * (p1[:, j + 1 : j + 2] * ra)) * (p2 * rc)
+        m = jnp.where(row > j + 1, m - update, jnp.where(row == j + 1, p2, m))
+    dg = jnp.sum(jnp.where(row == iota((n, 2 * n), 1), m, 0.0), axis=1, keepdims=True)
+    inv_ref[...] = m[:, n:] * lax.rsqrt(dg) * jnp.sqrt(jnp.float32(total))
+
+
+def factor_of(gram, total):
+    return pl.pallas_call(
+        functools.partial(factor_kernel, total),
+        out_shape=sds((4 * S, 4 * S)),
+        in_specs=[VM],
+        out_specs=VM,
+        compiler_params=pltpu.CompilerParams(vmem_limit_bytes=SMALL),
+        name="factor",
+    )(gram)
+
+
+def basis_kernel(inv_ref, rows_ref, r0_ref, r1_ref, r2_ref, r3_ref, me_ref, out_ref, all_ref):
     me = me_ref[0]
-    for k, ref in enumerate((o0_ref, o1_ref, o2_ref, o3_ref)):
-        ref[...] = r_ref[pl.ds(pl.multiple_of(((me + k) & 3) * S, S), S), :]
-
-
-def basis_of(gram, rows, me, total):
-    n = rows.shape[1]
+    n = rows_ref.shape[1]
+    ih, il = split(inv_ref[pl.ds(pl.multiple_of(me * S, S), S), :])
+    lhs = jnp.concatenate([jnp.concatenate([ih, ih], 1), jnp.concatenate([il, jnp.zeros_like(il)], 1)], 0)
+    for k, ref in enumerate((r0_ref, r1_ref, r2_ref, r3_ref)):
+        all_ref[pl.ds(pl.multiple_of(((me - k) & 3) * S, S), S), :] = ref[...]
+
+    def times(x):
+        r = nn(lhs, jnp.concatenate(split(x), 0))
+        return r[:S] + r[S:]
+
+    for r in range(4):
+        for i in range(3):
+            w = n // 3
+            col = slice(i * w, (i + 1) * w)
+            x = rows_ref[:, col] if r == 0 else all_ref[:, (r - 1) * n + i * w : (r - 1) * n + (i + 1) * w]
+            out_ref[:, pl.ds(pl.multiple_of(((me + r) & 3) * n + i * w, L), w)] = times(x)
+
+
+def basis_of(inv, rows, rest, me):
     return pl.pallas_call(
-        functools.partial(basis_kernel, total),
-        out_shape=(sds((S, n)),) * 4,
-        in_specs=[VM, VM, SM],
-        out_specs=(VM,) * 4,
-        scratch_shapes=[pltpu.VMEM((4 * S, 8 * S), F32), pltpu.VMEM((4 * S, n), F32)],
-        compiler_params=pltpu.CompilerParams(vmem_limit_bytes=VLIM),
+        basis_kernel,
+        out_shape=sds((S, LOC)),
+        in_specs=[VM] * 6 + [SM],
+        out_specs=VM,
+        scratch_shapes=[pltpu.VMEM((4 * S, 3 * LOC // 4), F32)],
+        compiler_params=pltpu.CompilerParams(vmem_limit_bytes=SMALL),
         name="basis",
-    )(gram, rows, me)
-
-
-def join_kernel(q0_ref, q1_ref, q2_ref, q3_ref, me_ref, out_ref):
-    me = me_ref[0]
-    n = q0_ref.shape[1]
-    for k, ref in enumerate((q0_ref, q1_ref, q2_ref, q3_ref)):
-        out_ref[:, pl.ds(pl.multiple_of(((me - k) & 3) * n, L), n)] = ref[...]
-
-
-def join(qs, me):
-    return pl.pallas_call(
-        join_kernel,
-        out_shape=sds((S, LOC)),
-        in_specs=[VM] * 4 + [SM],
-        out_specs=VM,
-        compiler_params=pltpu.CompilerParams(vmem_limit_bytes=VLIM),
-        name="join",
-    )(*qs, me)
+    )(inv, rows, *rest, me)
 
 
 def shift(x, axis, by):
@@ -722,12 +735,9 @@
     return lax.ppermute(x, axis, [(i, i ^ bits) for i in range(size)])
 
 
-def summed(g):
-    g = g + swap(g, "dom", 1)
-    for axis, unit in (("dom", 2), ("dom", 8), ("band", 1)):
-        others = [swap(g, axis, unit * k) for k in (1, 2, 3)]
-        g = (g + others[0]) + (others[1] + others[2])
-    return g
+def four(g, axis, unit):
+    others = [swap(g, axis, unit * k) for k in (1, 2, 3)]
+    return (g + others[0]) + (others[1] + others[2])
 
 
 def body(
@@ -759,13 +769,16 @@
     gl, gr = ghosts(first, last)
     u2, first, last = apply_step(2, u1, gl, gr, u0, *args)
     gl, gr = ghosts(first, last)
-    qs = apply_step(3, u2, gl, gr, u1, *args)
+    *qs, r0, r1, r2, r3 = apply_step(3, u2, gl, gr, u1, *args)
     qs = [qs[0]] + [shift(qs[k], "band", k) for k in (1, 2, 3)]
     gram, rows = gram_of(qs, me)
-    gram = summed(gram)
-    outs = basis_of(gram, rows, me, LOC * lax.axis_size("dom"))
-    outs = [outs[0]] + [shift(outs[k], "band", k) for k in (1, 2, 3)]
-    return join(outs, me)
+    gram = four(gram, "band", 1)
+    gram, r1, r2, r3 = lax.optimization_barrier((gram, r1, r2, r3))
+    rest = [r0] + [shift(r, "band", k) for k, r in ((1, r1), (2, r2), (3, r3))]
+    gram = gram + swap(gram, "dom", 1)
+    gram = four(four(gram, "dom", 2), "dom", 8)
+    inv = factor_of(gram, LOC * lax.axis_size("dom"))
+    return basis_of(inv, rows, rest, me)
 
 
 def solution(mesh):

time: 156 us -> 164 us (1.051); the launches traced: 158 us -> 164 us
  Pallas kernels: 66.8 us -> 80.2 us
  starting transfers between devices: 51.3 us -> 38.8 us
  waiting for transfers between devices: 29.1 us -> 34.2 us
    ppermute x10, starting transfers between devices: 17.1 us -> 4.53 us  [swap(): return lax.ppermute(x, axis, [(i, i ^ bits) for i in range(size)])]
    ppermute x10, waiting for transfers between devices: 12.9 us -> 23.5 us  [swap(): return lax.ppermute(x, axis, [(i, i ^ bits) for i in range(size)])]
    pallas_call x3, Pallas kernels: 38.3 us -> 46.6 us  [apply_step(): pl.pallas_call(functools.partial(step_kernel, number), out_shape=shapes,...]
    ppermute x14, waiting for transfers between devices: 16.2 us -> 10.7 us  [shift(): return lax.ppermute(x, axis, [(i, (i + by) % size) for i in range(size)])]
    pallas_call x2, Pallas kernels: 8.37 us -> 11.7 us  [the longest x1 9.12 us: factor_of(): pl.pallas_call(functools.partial(factor_kernel, total), out_shape=sds((4...]
    pallas_call x1, Pallas kernels: 7.28 us -> 8.95 us  [cell_tables(): pl.pallas_call(cells_kernel, out_shape=(sds((SLOTS, 16, L), I32), sds((SL...]
  transfers between devices with their start and end apart: 24 -> 24, of which waited for: 13 -> 13; matrix products, arithmetic and copies ran while one was open for 0% -> 0% of each run, Pallas kernels for 11% -> 17%
where the time goes in v4:
time: 164 us
  Pallas kernels  80.2 us (49%)
  starting transfers between devices  38.8 us (24%)
  waiting for transfers between devices  34.2 us (21%)
  local copies, waits for them, and re-layouts  9.73 us (6%)
    pallas_call x3, Pallas kernels, apply_step(): pl.pallas_call(functools.partial(step_kernel, number), out_shape=shapes,...  46.6 us
    ppermute x14, starting transfers between devices, shift(): return lax.ppermute(x, axis, [(i, (i + by) % size) for i in range(size)])  34.2 us
    ppermute x10, waiting for transfers between devices, swap(): return lax.ppermute(x, axis, [(i, i ^ bits) for i in range(size)])  23.5 us
    ppermute x14, waiting for transfers between devices, shift(): return lax.ppermute(x, axis, [(i, (i + by) % size) for i in range(size)])  10.7 us
    pallas_call x1, Pallas kernels, prepare(): pl.pallas_call(prepare_kernel, out_shape=(sds((QLO, E), BF16), sds((1, E)...  9.75 us
    pallas_call x1, Pallas kernels, factor_of(): pl.pallas_call(functools.partial(factor_kernel, total), out_shape=sds((4...  9.12 us
    unnamed x14, local copies, waits for them, and re-layouts  9.04 us
    pallas_call x1, Pallas kernels, cell_tables(): pl.pallas_call(cells_kernel, out_shape=(sds((SLOTS, 16, L), I32), sds((SL...  8.95 us
  transfers between devices with their start and end apart: 24, of which 13 were waited for; matrix products, arithmetic and copies ran while one was open for 0% of the time, Pallas kernels for 17%

profile of v4, /device:TPU:0, one launch (start us, length us, event | category | flops | bytes accessed | tf_op | source)
XLA Modules:
  0.0 163.8 jit_solution(1102320151875532547)
XLA Ops:
  2.3 4.8 %collective-permute-start.3 = (f32[72,896]{1,0:T(8,128)}, f32[72,896]{1,0:T(8,128)S(1)}, u32[]{:S(2)}, u32[]{:S(2)}) collective-permute-start(f32[72,896]{1,0:T(8,128)} %pack.1.own_ref), channel_id=1, source_target_pairs={{0,124},{4,0},{8,4},{12,8},{16,12},{20,16},{24,20},{28,24},{32,28}... | collective-permute-start | bytes 774152 | tf_op jit(solution)/shard_map/ppermute | solution.py:730
  10.4 9.7 %prepare.1 = (bf16[512,4608]{1,0:T(8,128)(2,1)S(1)}, s32[1,4608]{1,0:T(1,128)S(1)}, f32[1,3584]{1,0:T(1,128)S(1)}, s32[40,128]{1,0:T(8,128)S(1)}, s32[128,128]{1...) custom-call(s32[1,864]{1,0:T(1,128)S(1)} %broadcast_in_dim.6.rows_hb, ...), custom_call_target="tpu_custom_call" | custom-call | tf_op jit(solution)/shard_map/prepare/pallas_call | solution.py:286
  22.3 5.1 %collective-permute-start.1 = (f32[16,2048]{1,0:T(8,128)S(1)}, f32[16,2048]{1,0:T(8,128)S(1)}, u32[]{:S(2)}, u32[]{:S(2)}) collective-permute-start(f32[16,2048]{1,0:T(8,128)S(1)} %get-tuple-element.42), channel_id=1, source_target_pairs={{0,124},{4,0},{8,4},{12,8},{16,12},{20,16},{24,20},{28,24},{32,28}... | collective-permute-start | bytes 393224 | tf_op jit(solution)/shard_map/ppermute | solution.py:730
  29.5 8.9 %cell_tables.1 = (s32[224,16,128]{2,1,0:T(8,128)S(1)}, f32[224,8,128]{2,1,0:T(8,128)S(1)}, bf16[384,384]{1,0:T(8,128)(2,1)S(1)}, bf16[384,384]{1,0:T(8,128)(2,1)S(1)}, s32[1024]{0:T(1024)S(1)}) custom-call(f32[72,896]{1,0:T(8,128)S(1)} %copy-done.2, f32[72,896]{1,0:T(8,128)S(1)} %collective-permute-done.2.left_ref, ...), custom_call_target="tpu_custom_call" | custom-call | tf_op jit(solution)/shard_map/cell_tables/pallas_call | solution.py:466
  38.5 2.3 %copy-done.1 = bf16[512,4608]{1,0:T(8,128)(2,1)S(1)} copy-done((bf16[512,4608]{1,0:T(8,128)(2,1)S(1)}, bf16[512,4608]{1,0:T(8,128)(2,1)}, u32[]{:S(2)}) %copy-start.1) | copy-done | bytes 4718616
  40.8 15.5 %step1.1 = (f32[16,13824]{1,0:T(8,128)S(1)}, f32[16,2048]{1,0:T(8,128)S(1)}, f32[16,2048]{1,0:T(8,128)S(1)}) custom-call(f32[16,13824]{1,0:T(8,128)S(1)} %get-tuple-element.40.refs_0_.refs_3_, f32[16,2048]{1,0:T(8,128)S(1)} %collective-permute-done.refs_1_, f32[16,2048]{1,0:T(8,128)S(1)} %collective-permute-done.1.refs_2_, ...), custom_call_target="tpu_custom_call" | custom-call | tf_op jit(solution)/shard_map/step1/pallas_call | solution.py:629
  56.4 5.1 %collective-permute-start.5 = (f32[16,2048]{1,0:T(8,128)S(1)}, f32[16,2048]{1,0:T(8,128)S(1)}, u32[]{:S(2)}, u32[]{:S(2)}) collective-permute-start(f32[16,2048]{1,0:T(8,128)S(1)} %get-tuple-element.57), channel_id=1, source_target_pairs={{0,124},{4,0},{8,4},{12,8},{16,12},{20,16},{24,20},{28,24},{32,28}... | collective-permute-start | bytes 393224 | tf_op jit(solution)/shard_map/ppermute | solution.py:730
  61.4 2.6 %collective-permute-done.4.refs_1_ = f32[16,2048]{1,0:T(8,128)S(1)} collective-permute-done((f32[16,2048]{1,0:T(8,128)S(1)}, f32[16,2048]{1,0:T(8,128)S(1)}, u32[]{:S(2)}, u32[]{:S(2)}) %collective-permute-start.4) | collective-permute-done | bytes 131104 | tf_op jit(solution)/shard_map/ppermute | solution.py:730
  64.1 15.3 %step2.1 = (f32[16,13824]{1,0:T(8,128)S(1)}, f32[16,2048]{1,0:T(8,128)S(1)}, f32[16,2048]{1,0:T(8,128)S(1)}) custom-call(f32[16,13824]{1,0:T(8,128)S(1)} %get-tuple-element.55.refs_0_.refs_3_, f32[16,2048]{1,0:T(8,128)S(1)} %collective-permute-done.4.refs_1_, f32[16,2048]{1,0:T(8,128)S(1)} %collective-permute-done.5.refs_2_, ...), custom_call_target="tpu_custom_call" | custom-call | tf_op jit(solution)/shard_map/step2/pallas_call | solution.py:629
  79.5 5.1 %collective-permute-start.7 = (f32[16,2048]{1,0:T(8,128)S(1)}, f32[16,2048]{1,0:T(8,128)S(1)}, u32[]{:S(2)}, u32[]{:S(2)}) collective-permute-start(f32[16,2048]{1,0:T(8,128)S(1)} %get-tuple-element.60), channel_id=1, source_target_pairs={{0,124},{4,0},{8,4},{12,8},{16,12},{20,16},{24,20},{28,24},{32,28}... | collective-permute-start | bytes 393224 | tf_op jit(solution)/shard_map/ppermute | solution.py:730
  84.6 2.6 %collective-permute-done.6.refs_1_ = f32[16,2048]{1,0:T(8,128)S(1)} collective-permute-done((f32[16,2048]{1,0:T(8,128)S(1)}, f32[16,2048]{1,0:T(8,128)S(1)}, u32[]{:S(2)}, u32[]{:S(2)}) %collective-permute-start.6) | collective-permute-done | bytes 131104 | tf_op jit(solution)/shard_map/ppermute | solution.py:730
  87.2 15.8 %step3.1 = (f32[16,3456]{1,0:T(8,128)S(1)}, f32[16,3456]{1,0:T(8,128)S(1)}, f32[16,3456]{1,0:T(8,128)S(1)}, f32[16,3456]{1,0:T(8,128)S(1)}, f32[16,10368]{1,0:T(...) custom-call(f32[16,13824]{1,0:T(8,128)S(1)} %get-tuple-element.58.refs_0_, ...), custom_call_target="tpu_custom_call" | custom-call | tf_op jit(solution)/shard_map/step3/pallas_call | solution.py:629
  105.0 3.6 %collective-permute-start.9 = (f32[16,3456]{1,0:T(8,128)S(1)}, f32[16,3456]{1,0:T(8,128)S(1)}, u32[]{:S(2)}, u32[]{:S(2)}) collective-permute-start(f32[16,3456]{1,0:T(8,128)S(1)} %get-tuple-element.63), channel_id=1, source_target_pairs={{0,2},{1,3},{2,0},{3,1},{4,6},{5,7},{6,4},{7,5},{8,10},{9,11},{10,... | collective-permute-start | bytes 663560 | tf_op jit(solution)/shard_map/ppermute | solution.py:730
  111.0 3.9 %collective-permute-done.9.q2_ref = f32[16,3456]{1,0:T(8,128)S(1)} collective-permute-done((f32[16,3456]{1,0:T(8,128)S(1)}, f32[16,3456]{1,0:T(8,128)S(1)}, u32[]{:S(2)}, u32[]{:S(2)}) %collective-permute-start.9) | collective-permute-done | bytes 221216 | tf_op jit(solution)/shard_map/ppermute | solution.py:730
  116.4 2.8 %collective-permute-start.13 = (f32[64,64]{1,0:T(8,128)S(1)}, f32[64,64]{1,0:T(8,128)S(1)}, u32[]{:S(2)}, u32[]{:S(2)}) collective-permute-start(f32[64,64]{1,0:T(8,128)S(1)} %get-tuple-element.65), channel_id=1, source_target_pairs={{0,3},{1,2},{2,1},{3,0},{4,7},{5,6},{6,5},{7,4},{8,11},{9,10},{10,... | collective-permute-start | bytes 49160 | tf_op jit(solution)/shard_map/ppermute | solution.py:735
  120.6 3.5 %collective-permute-done.13 = f32[64,64]{1,0:T(8,128)S(1)} collective-permute-done((f32[64,64]{1,0:T(8,128)S(1)}, f32[64,64]{1,0:T(8,128)S(1)}, u32[]{:S(2)}, u32[]{:S(2)}) %collective-permute-start.13) | collective-permute-done | bytes 16416 | tf_op jit(solution)/shard_map/ppermute | solution.py:735
  125.1 4.8 %collective-permute-start.21 = (f32[16,10368]{1,0:T(8,128)S(1)}, f32[16,10368]{1,0:T(8,128)S(1)}, u32[]{:S(2)}, u32[]{:S(2)}) collective-permute-start(f32[16,10368]{1,0:T(8,128)S(1)} %get-tuple-element.72), channel_id=1, source_target_pairs={{0,1},{1,2},{2,3},{3,0},{4,5},{5,6},{6,7},{7,4},{8,9},{9,10},{10,1... | collective-permute-start | bytes 1990664 | tf_op jit(solution)/shard_map/ppermute | solution.py:730
  129.8 2.4 %collective-permute-start.22 = (f32[16,10368]{1,0:T(8,128)S(1)}, f32[16,10368]{1,0:T(8,128)S(1)}, u32[]{:S(2)}, u32[]{:S(2)}) collective-permute-start(f32[16,10368]{1,0:T(8,128)S(1)} %get-tuple-element.73), channel_id=1, source_target_pairs={{0,2},{1,3},{2,0},{3,1},{4,6},{5,7},{6,4},{7,5},{8,10},{9,11},{10,... | collective-permute-start | bytes 1990664 | tf_op jit(solution)/shard_map/ppermute | solution.py:730
  133.9 5.0 %collective-permute-done.17 = f32[64,64]{1,0:T(8,128)S(1)} collective-permute-done((f32[64,64]{1,0:T(8,128)S(1)}, f32[64,64]{1,0:T(8,128)S(1)}, u32[]{:S(2)}, u32[]{:S(2)}) %collective-permute-start.17) | collective-permute-done | bytes 16416 | tf_op jit(solution)/shard_map/ppermute | solution.py:735
  139.3 3.5 %collective-permute-done.15 = f32[64,64]{1,0:T(8,128)S(1)} collective-permute-done((f32[64,64]{1,0:T(8,128)S(1)}, f32[64,64]{1,0:T(8,128)S(1)}, u32[]{:S(2)}, u32[]{:S(2)}) %collective-permute-start.15) | collective-permute-done | bytes 16416 | tf_op jit(solution)/shard_map/ppermute | solution.py:735
  143.1 5.0 %collective-permute-done.20 = f32[64,64]{1,0:T(8,128)S(1)} collective-permute-done((f32[64,64]{1,0:T(8,128)S(1)}, f32[64,64]{1,0:T(8,128)S(1)}, u32[]{:S(2)}, u32[]{:S(2)}) %collective-permute-start.20) | collective-permute-done | bytes 16416 | tf_op jit(solution)/shard_map/ppermute | solution.py:735
  148.7 3.3 %collective-permute-done.18 = f32[64,64]{1,0:T(8,128)S(1)} collective-permute-done((f32[64,64]{1,0:T(8,128)S(1)}, f32[64,64]{1,0:T(8,128)S(1)}, u32[]{:S(2)}, u32[]{:S(2)}) %collective-permute-start.18) | collective-permute-done | bytes 16416 | tf_op jit(solution)/shard_map/ppermute | solution.py:735
  152.0 9.1 %factor.1.inv_ref = f32[64,64]{1,0:T(8,128)S(1)} custom-call(f32[64,64]{1,0:T(8,128)S(1)} %add_add_fusion.gram_ref), custom_call_target="tpu_custom_call" | custom-call | tf_op jit(solution)/shard_map/factor/pallas_call | solution.py:686
  161.2 2.6 %basis.1 = f32[16,13824]{1,0:T(8,128)} custom-call(f32[64,64]{1,0:T(8,128)S(1)} %factor.1.inv_ref, f32[64,3456]{1,0:T(8,128)S(1)} %get-tuple-element.70.rows_ref, f32[16,10368]{1,0:T(8,128)S(1)} %get-tuple-element.71.r0_ref, f32[16,10368]{1,0:T(8,128)S(1)} %collective-permute-done.21.r1_ref, f32[16,10368]{1,0:T(8,128)S(1)} %collective-permute-done.22.r2_ref, ...), custom_call_target="tpu_custom_call" | custom-call | tf_op jit(solution)/shard_map/basis/pallas_call | solution.py:717
  (53 shorter events, 20.4 us)
Async XLA Ops:
  2.3 25.1 %collective-permute-start.3 = (f32[72,896]{1,0:T(8,128)}, f32[72,896]{1,0:T(8,128)S(1)}, u32[]{:S(2)}, u32[]{:S(2)}) collective-permute-start(f32[72,896]{1,0:T(8,128)} %pack.1.own_ref), channel_id=1, source_target_pairs={{0,124},{4,0},{8,4},{12,8},{16,12},{20,16},{24,20},{28,24},{32,28}... | collective-permute-start | bytes 774152 | tf_op jit(solution)/shard_map/ppermute | solution.py:730
  7.1 20.3 %collective-permute-start.2 = (f32[72,896]{1,0:T(8,128)}, f32[72,896]{1,0:T(8,128)S(1)}, u32[]{:S(2)}, u32[]{:S(2)}) collective-permute-start(f32[72,896]{1,0:T(8,128)} %pack.1.own_ref), channel_id=1, source_target_pairs={{0,4},{4,8},{8,12},{12,16},{16,20},{20,24},{24,28},{28,32},{32,36}... | collective-permute-start | bytes 774152 | tf_op jit(solution)/shard_map/ppermute | solution.py:730
  22.3 16.1 %collective-permute-start = (f32[16,2048]{1,0:T(8,128)S(1)}, f32[16,2048]{1,0:T(8,128)S(1)}, u32[]{:S(2)}, u32[]{:S(2)}) collective-permute-start(f32[16,2048]{1,0:T(8,128)S(1)} %get-tuple-element.41), channel_id=1, source_target_pairs={{0,4},{4,8},{8,12},{12,16},{16,20},{20,24},{24,28},{28,32},{32,36}... | collective-permute-start | bytes 393224 | tf_op jit(solution)/shard_map/ppermute | solution.py:730
  22.3 16.1 %collective-permute-start.1 = (f32[16,2048]{1,0:T(8,128)S(1)}, f32[16,2048]{1,0:T(8,128)S(1)}, u32[]{:S(2)}, u32[]{:S(2)}) collective-permute-start(f32[16,2048]{1,0:T(8,128)S(1)} %get-tuple-element.42), channel_id=1, source_target_pairs={{0,124},{4,0},{8,4},{12,8},{16,12},{20,16},{24,20},{28,24},{32,28}... | collective-permute-start | bytes 393224 | tf_op jit(solution)/shard_map/ppermute | solution.py:730
  56.3 7.8 %collective-permute-start.4 = (f32[16,2048]{1,0:T(8,128)S(1)}, f32[16,2048]{1,0:T(8,128)S(1)}, u32[]{:S(2)}, u32[]{:S(2)}) collective-permute-start(f32[16,2048]{1,0:T(8,128)S(1)} %get-tuple-element.56), channel_id=1, source_target_pairs={{0,4},{4,8},{8,12},{12,16},{16,20},{20,24},{24,28},{28,32},{32,36}... | collective-permute-start | bytes 393224 | tf_op jit(solution)/shard_map/ppermute | solution.py:730
  56.4 7.7 %collective-permute-start.5 = (f32[16,2048]{1,0:T(8,128)S(1)}, f32[16,2048]{1,0:T(8,128)S(1)}, u32[]{:S(2)}, u32[]{:S(2)}) collective-permute-start(f32[16,2048]{1,0:T(8,128)S(1)} %get-tuple-element.57), channel_id=1, source_target_pairs={{0,124},{4,0},{8,4},{12,8},{16,12},{20,16},{24,20},{28,24},{32,28}... | collective-permute-start | bytes 393224 | tf_op jit(solution)/shard_map/ppermute | solution.py:730
  79.4 7.8 %collective-permute-start.6 = (f32[16,2048]{1,0:T(8,128)S(1)}, f32[16,2048]{1,0:T(8,128)S(1)}, u32[]{:S(2)}, u32[]{:S(2)}) collective-permute-start(f32[16,2048]{1,0:T(8,128)S(1)} %get-tuple-element.59), channel_id=1, source_target_pairs={{0,4},{4,8},{8,12},{12,16},{16,20},{20,24},{24,28},{28,32},{32,36}... | collective-permute-start | bytes 393224 | tf_op jit(solution)/shard_map/ppermute | solution.py:730
  79.5 7.7 %collective-permute-start.7 = (f32[16,2048]{1,0:T(8,128)S(1)}, f32[16,2048]{1,0:T(8,128)S(1)}, u32[]{:S(2)}, u32[]{:S(2)}) collective-permute-start(f32[16,2048]{1,0:T(8,128)S(1)} %get-tuple-element.60), channel_id=1, source_target_pairs={{0,124},{4,0},{8,4},{12,8},{16,12},{20,16},{24,20},{28,24},{32,28}... | collective-permute-start | bytes 393224 | tf_op jit(solution)/shard_map/ppermute | solution.py:730
  103.0 8.0 %collective-permute-start.8 = (f32[16,3456]{1,0:T(8,128)S(1)}, f32[16,3456]{1,0:T(8,128)S(1)}, u32[]{:S(2)}, u32[]{:S(2)}) collective-permute-start(f32[16,3456]{1,0:T(8,128)S(1)} %get-tuple-element.62), channel_id=1, source_target_pairs={{0,1},{1,2},{2,3},{3,0},{4,5},{5,6},{6,7},{7,4},{8,9},{9,10},{10,1... | collective-permute-start | bytes 663560 | tf_op jit(solution)/shard_map/ppermute | solution.py:730
  105.0 10.0 %collective-permute-start.9 = (f32[16,3456]{1,0:T(8,128)S(1)}, f32[16,3456]{1,0:T(8,128)S(1)}, u32[]{:S(2)}, u32[]{:S(2)}) collective-permute-start(f32[16,3456]{1,0:T(8,128)S(1)} %get-tuple-element.63), channel_id=1, source_target_pairs={{0,2},{1,3},{2,0},{3,1},{4,6},{5,7},{6,4},{7,5},{8,10},{9,11},{10,... | collective-permute-start | bytes 663560 | tf_op jit(solution)/shard_map/ppermute | solution.py:730
  108.5 6.4 %collective-permute-start.10 = (f32[16,3456]{1,0:T(8,128)S(1)}, f32[16,3456]{1,0:T(8,128)S(1)}, u32[]{:S(2)}, u32[]{:S(2)}) collective-permute-start(f32[16,3456]{1,0:T(8,128)S(1)} %get-tuple-element.64), channel_id=1, source_target_pairs={{0,3},{1,0},{2,1},{3,2},{4,7},{5,4},{6,5},{7,6},{8,11},{9,8},{10,9... | collective-permute-start | bytes 663560 | tf_op jit(solution)/shard_map/ppermute | solution.py:730
  116.4 7.7 %collective-permute-start.13 = (f32[64,64]{1,0:T(8,128)S(1)}, f32[64,64]{1,0:T(8,128)S(1)}, u32[]{:S(2)}, u32[]{:S(2)}) collective-permute-start(f32[64,64]{1,0:T(8,128)S(1)} %get-tuple-element.65), channel_id=1, source_target_pairs={{0,3},{1,2},{2,1},{3,0},{4,7},{5,6},{6,5},{7,4},{8,11},{9,10},{10,... | collective-permute-start | bytes 49160 | tf_op jit(solution)/shard_map/ppermute | solution.py:735
  119.2 5.8 %collective-permute-start.12 = (f32[64,64]{1,0:T(8,128)S(1)}, f32[64,64]{1,0:T(8,128)S(1)}, u32[]{:S(2)}, u32[]{:S(2)}) collective-permute-start(f32[64,64]{1,0:T(8,128)S(1)} %get-tuple-element.65), channel_id=1, source_target_pairs={{0,2},{1,3},{2,0},{3,1},{4,6},{5,7},{6,4},{7,5},{8,10},{9,11},{10,... | collective-permute-start | bytes 49160 | tf_op jit(solution)/shard_map/ppermute | solution.py:735
  120.6 4.4 %collective-permute-start.11 = (f32[64,64]{1,0:T(8,128)S(1)}, f32[64,64]{1,0:T(8,128)S(1)}, u32[]{:S(2)}, u32[]{:S(2)}) collective-permute-start(f32[64,64]{1,0:T(8,128)S(1)} %get-tuple-element.65), channel_id=1, source_target_pairs={{0,1},{1,0},{2,3},{3,2},{4,5},{5,4},{6,7},{7,6},{8,9},{9,8},{10,11... | collective-permute-start | bytes 49160 | tf_op jit(solution)/shard_map/ppermute | solution.py:735
  125.1 36.1 %collective-permute-start.21 = (f32[16,10368]{1,0:T(8,128)S(1)}, f32[16,10368]{1,0:T(8,128)S(1)}, u32[]{:S(2)}, u32[]{:S(2)}) collective-permute-start(f32[16,10368]{1,0:T(8,128)S(1)} %get-tuple-element.72), channel_id=1, source_target_pairs={{0,1},{1,2},{2,3},{3,0},{4,5},{5,6},{6,7},{7,4},{8,9},{9,10},{10,1... | collective-permute-start | bytes 1990664 | tf_op jit(solution)/shard_map/ppermute | solution.py:730
  129.8 31.3 %collective-permute-start.22 = (f32[16,10368]{1,0:T(8,128)S(1)}, f32[16,10368]{1,0:T(8,128)S(1)}, u32[]{:S(2)}, u32[]{:S(2)}) collective-permute-start(f32[16,10368]{1,0:T(8,128)S(1)} %get-tuple-element.73), channel_id=1, source_target_pairs={{0,2},{1,3},{2,0},{3,1},{4,6},{5,7},{6,4},{7,5},{8,10},{9,11},{10,... | collective-permute-start | bytes 1990664 | tf_op jit(solution)/shard_map/ppermute | solution.py:730
  132.2 28.9 %collective-permute-start.23 = (f32[16,10368]{1,0:T(8,128)S(1)}, f32[16,10368]{1,0:T(8,128)S(1)}, u32[]{:S(2)}, u32[]{:S(2)}) collective-permute-start(f32[16,10368]{1,0:T(8,128)S(1)} %get-tuple-element.74), channel_id=1, source_target_pairs={{0,3},{1,0},{2,1},{3,2},{4,7},{5,4},{6,5},{7,6},{8,11},{9,8},{10,9... | collective-permute-start | bytes 1990664 | tf_op jit(solution)/shard_map/ppermute | solution.py:730
  132.6 1.2 collective-permute-start.14
  133.8 5.1 %collective-permute-start.17 = (f32[64,64]{1,0:T(8,128)S(1)}, f32[64,64]{1,0:T(8,128)S(1)}, u32[]{:S(2)}, u32[]{:S(2)}) collective-permute-start(f32[64,64]{1,0:T(8,128)S(1)} %add.33), channel_id=1, source_target_pairs={{0,24},{4,28},{8,16},{12,20},{16,8},{20,12},{24,0},{28,4},{32,56},... | collective-permute-start | bytes 49160 | tf_op jit(solution)/shard_map/ppermute | solution.py:735
  133.8 5.5 %collective-permute-start.16 = (f32[64,64]{1,0:T(8,128)S(1)}, f32[64,64]{1,0:T(8,128)S(1)}, u32[]{:S(2)}, u32[]{:S(2)}) collective-permute-start(f32[64,64]{1,0:T(8,128)S(1)} %add.33), channel_id=1, source_target_pairs={{0,16},{4,20},{8,24},{12,28},{16,0},{20,4},{24,8},{28,12},{32,48},... | collective-permute-start | bytes 49160 | tf_op jit(solution)/shard_map/ppermute | solution.py:735
  138.9 3.9 %collective-permute-start.15 = (f32[64,64]{1,0:T(8,128)S(1)}, f32[64,64]{1,0:T(8,128)S(1)}, u32[]{:S(2)}, u32[]{:S(2)}) collective-permute-start(f32[64,64]{1,0:T(8,128)S(1)} %add.33), channel_id=1, source_target_pairs={{0,8},{4,12},{8,0},{12,4},{16,24},{20,28},{24,16},{28,20},{32,40},... | collective-permute-start | bytes 49160 | tf_op jit(solution)/shard_map/ppermute | solution.py:735
  142.9 5.2 %collective-permute-start.20 = (f32[64,64]{1,0:T(8,128)S(1)}, f32[64,64]{1,0:T(8,128)S(1)}, u32[]{:S(2)}, u32[]{:S(2)}) collective-permute-start(f32[64,64]{1,0:T(8,128)S(1)} %add_add_fusion.1), channel_id=1, source_target_pairs={{0,96},{4,100},{8,104},{12,108},{16,112},{20,116},{24,120},{28,124... | collective-permute-start | bytes 49160 | tf_op jit(solution)/shard_map/ppermute | solution.py:735
  143.0 5.7 %collective-permute-start.19 = (f32[64,64]{1,0:T(8,128)S(1)}, f32[64,64]{1,0:T(8,128)S(1)}, u32[]{:S(2)}, u32[]{:S(2)}) collective-permute-start(f32[64,64]{1,0:T(8,128)S(1)} %add_add_fusion.1), channel_id=1, source_target_pairs={{0,64},{4,68},{8,72},{12,76},{16,80},{20,84},{24,88},{28,92},{32,9... | collective-permute-start | bytes 49160 | tf_op jit(solution)/shard_map/ppermute | solution.py:735
  148.1 3.9 %collective-permute-start.18 = (f32[64,64]{1,0:T(8,128)S(1)}, f32[64,64]{1,0:T(8,128)S(1)}, u32[]{:S(2)}, u32[]{:S(2)}) collective-permute-start(f32[64,64]{1,0:T(8,128)S(1)} %add_add_fusion.1), channel_id=1, source_target_pairs={{0,32},{4,36},{8,40},{12,44},{16,48},{20,52},{24,56},{28,60},{32,0... | collective-permute-start | bytes 49160 | tf_op jit(solution)/shard_map/ppermute | solution.py:735
  (7 other events, 9.1 us)
